TPU v7x, 128 devices: a whole 4x4x4 slice. The times are simulated.
128 devices in a mesh: pipe: 2 (over x_hi), tensor: 4 (over x_lo, core), dp: 16 (over z, y).
Axes of the slice: x: 4 (x_hi: 2, x_lo: 2; x = x_hi * 2 + x_lo), y: 4, z: 4, core: 2. Of those that a mesh axis runs over, the one named last changes fastest.
Arguments:
- hidden_in: bfloat16 [256, 16, 4, 256], P(None, 'dp', 'tensor')
- norm_gain: bfloat16 [2, 16384], P('pipe', 'dp'), may hold values from 0.25 to 1.75
- w_query: bfloat16 [2, 16384, 8192], P('pipe', 'dp', 'tensor'), may hold values from -0.046875 to 0.046875
- w_keyval: bfloat16 [2, 16384, 8, 256], P('pipe', 'dp', 'tensor'), may hold values from -0.046875 to 0.046875
- w_out: bfloat16 [2, 8192, 16384], P('pipe', 'tensor', 'dp'), may hold values from -1 to 1
- head_group: int32 [64], replicated, may hold values from 0 to 7, as said below
Outputs:
- layer_out: bfloat16 [2, 256, 16, 4, 256], P('pipe', None, 'dp', 'tensor')
- importance: float32 [2, 8], P('pipe')
Inputs may be any that keep to these rules, and one draw needn't show every extreme that they name: `head_group`: each of the 8 groups is named by exactly 8 heads.
All inputs are finite; a program needn't handle non-finite values.
Results may differ from a plain program's by a relative error of at most 0.023.
Values may be sent and summed in bfloat16 or wider, within the bound.
No kernel may reach another device: no remote copies, remote signals or barrier semaphores. Data moves between devices by JAX's collectives and lax.ppermute only.
A program may use at most 64 MiB of HBM per device.

v0:
```python
import jax
import jax.numpy as jnp
from jax import lax
from jax.sharding import PartitionSpec as P

HD = 128
GROUPS = 8
MICRO = 4


THETA_LOG = 13.122363377404328
EPS_NORM = 1e-05
EPS_RMS = 1e-06


def from_behind(block, axis, distance):
    devices = range(lax.axis_size(axis))
    route = [(i - distance, i) for i in devices if i - distance in devices]
    return lax.ppermute(block, axis, route)


def rotate(values, positions, first_col, period):
    count_rows, count_cols = values.shape
    pair_cols = first_col + 2 * jnp.arange(count_cols // 2, dtype=jnp.int32)
    within = pair_cols % period
    freq = (within % HD // 2).astype(jnp.float32)
    inverse = jnp.exp(-THETA_LOG * 2.0 * freq / HD)
    angle = positions[:, None].astype(jnp.float32) * inverse[None, :]
    pairs = values.reshape(count_rows, count_cols // 2, 2)
    first = pairs[:, :, 0]
    second = pairs[:, :, 1]
    cosine = jnp.cos(angle)
    sine = jnp.sin(angle)
    keep = (within < HD)[None, :]
    new_first = jnp.where(keep, first * cosine - second * sine, first)
    new_second = jnp.where(keep, first * sine + second * cosine, second)
    return jnp.stack([new_first, new_second], axis=-1).reshape(count_rows, count_cols)


def attend(query, keys, vals, allowed):
    scores = lax.dot_general(
        query, keys, (((1,), (1,)), ((), ())), preferred_element_type=jnp.float32
    )
    expo = jnp.where(allowed, jnp.exp(scores / jnp.sqrt(jnp.float32(HD))), jnp.float32(0.0))
    weights = (expo / jnp.sum(expo, axis=1, keepdims=True)).astype(jnp.bfloat16)
    return jnp.dot(weights, vals, preferred_element_type=jnp.float32).astype(jnp.bfloat16)


def local(hidden_in, norm_gain, w_query, w_keyval, w_out, head_group):
    n_tensor = lax.axis_size("tensor")
    n_data = lax.axis_size("dp")
    n_sections = lax.axis_size("pipe")
    section = lax.axis_index("pipe")
    tensor_idx = lax.axis_index("tensor")
    data_idx = lax.axis_index("dp")
    total_rows = hidden_in.shape[0]
    slice_cols = hidden_in.shape[3]
    width = slice_cols * n_tensor * n_data
    block = total_rows // MICRO
    gain = norm_gain[0].astype(jnp.float32)
    query_proj = w_query[0]
    wide_cols = query_proj.shape[0]
    kv_proj = w_keyval[0].reshape(wide_cols, -1)
    kv_cols = kv_proj.shape[1]
    out_proj = w_out[0]
    heads_here = query_proj.shape[1] // HD
    head = tensor_idx * heads_here + data_idx * (heads_here // n_data)
    group = head_group[head]
    local_groups = lax.dynamic_slice_in_dim(head_group, tensor_idx * heads_here, heads_here, 0)
    out_heads = out_proj.reshape(heads_here, HD, wide_cols)
    entry_pieces = hidden_in.reshape(total_rows, slice_cols)
    entry_whole = lax.all_gather(entry_pieces, "tensor", axis=1, tiled=True)
    incoming = jnp.zeros((block, wide_cols), jnp.bfloat16)
    cache = jnp.zeros((total_rows, 2 * HD), jnp.bfloat16)
    outputs = jnp.zeros((total_rows, slice_cols), jnp.bfloat16)
    head_total = jnp.zeros((heads_here,), jnp.float32)
    key_positions = jnp.arange(total_rows, dtype=jnp.int32)
    steps_total = MICRO + n_sections - 1
    for step in range(steps_total):
        index = step - section
        valid = jnp.logical_and(index >= 0, index < MICRO)
        current = jnp.clip(index, 0, MICRO - 1)
        if step < MICRO:
            first_in = entry_whole[step * block : (step + 1) * block]
        else:
            first_in = jnp.zeros((block, wide_cols), jnp.bfloat16)
        state = jnp.where(section == 0, first_in, incoming)
        wide = state.astype(jnp.float32)
        sums = lax.psum(jnp.sum(wide * wide, axis=1, keepdims=True), "dp")
        normed = (wide * lax.rsqrt(sums / width + EPS_NORM) * gain).astype(jnp.bfloat16)
        positions = current * block + jnp.arange(block, dtype=jnp.int32)
        query_part = jnp.dot(normed, query_proj, preferred_element_type=jnp.float32)
        kv_part = jnp.dot(normed, kv_proj, preferred_element_type=jnp.float32)
        query_mine = lax.psum_scatter(
            query_part.astype(jnp.bfloat16), "dp", scatter_dimension=1, tiled=True
        ).astype(jnp.float32)
        kv_summed = lax.psum(kv_part.astype(jnp.bfloat16), "dp").astype(jnp.float32)
        rotated = rotate(kv_summed, positions, tensor_idx * kv_cols, 2 * HD).astype(jnp.bfloat16)
        keyval = lax.all_gather(rotated, "tensor", axis=1, tiled=True)
        query = rotate(query_mine, positions, 0, HD).astype(jnp.bfloat16)
        mine = lax.dynamic_slice_in_dim(keyval, group * 2 * HD, 2 * HD, 1)
        cache = jnp.where(
            valid, lax.dynamic_update_slice_in_dim(cache, mine, current * block, 0), cache
        )
        allowed = positions[:, None] >= key_positions[None, :]
        attended = attend(query, cache[:, :HD], cache[:, HD:], allowed)
        heads_att = lax.all_gather(attended, "dp", axis=1, tiled=True)
        per_head = jnp.einsum(
            "rhk,hkc->rhc",
            heads_att.reshape(block, heads_here, HD),
            out_heads,
            preferred_element_type=jnp.float32,
        )
        total = jnp.sum(per_head, axis=1)
        squares = jnp.sum(per_head * per_head, axis=2)
        full_squares = lax.psum(squares, "dp")
        spread = jnp.sqrt(full_squares / width + EPS_RMS)
        head_total = head_total + jnp.where(valid, jnp.sum(spread, axis=0), jnp.float32(0.0))
        summed = lax.psum(total.astype(jnp.bfloat16), "tensor").astype(jnp.float32)
        fresh = (wide + summed).astype(jnp.bfloat16)
        out_piece = lax.dynamic_slice_in_dim(fresh, tensor_idx * slice_cols, slice_cols, 1)
        if step < steps_total - 1:
            incoming = from_behind(fresh, "pipe", 1)
        outputs = jnp.where(
            valid, lax.dynamic_update_slice_in_dim(outputs, out_piece, current * block, 0), outputs
        )
    head_mean = head_total / total_rows
    picked = (local_groups[:, None] == jnp.arange(GROUPS, dtype=jnp.int32)[None, :]).astype(
        jnp.float32
    )
    group_part = jnp.sum(picked * head_mean[:, None], axis=0)
    totals = lax.psum(group_part, "tensor")
    return (outputs.reshape(1, total_rows, 1, 1, slice_cols), totals[None])


def solution(mesh):
    in_specs = (
        P(None, "dp", "tensor", None),
        P("pipe", "dp"),
        P("pipe", "dp", "tensor"),
        P("pipe", "dp", "tensor", None),
        P("pipe", "tensor", "dp"),
        P(),
    )
    out_specs = (P("pipe", None, "dp", "tensor", None), P("pipe", None))
    return jax.shard_map(local, mesh=mesh, in_specs=in_specs, out_specs=out_specs, check_vma=False)
```

profile of v0, /device:TPU:4, one launch (start us, length us, event | category | flops | bytes accessed | tf_op | source)
XLA Modules:
  0.0 1409.4 jit_solution(15518204431061000397)
XLA Ops:
  9.4 7.1 all-gather
  16.6 41.9 %psum.147 = f32[64,1]{0,1:T(1,128)S(1)} all-reduce(f32[64,1]{0,1:T(1,128)S(1)} %bitcast.244), channel_id=1, replica_groups=mesh['pipe'=2,'tensor'=4,'dp'=16] {'dp'}, use_global_device_ids=true, to_apply=%region_1.2 | all-reduce | flops 64 | bytes 512 | tf_op jit(solution)/shard_map/psum | solution.py:89
  65.3 73.2 %all-reduce.12.cloned.1.call-done = bf16[64,256,2]{0,2,1:T(2,128)(2,1)} async-done(((bf16[64,256,2]{0,2,1:T(2,128)(2,1)}), bf16[64,256,2]{0,2,1:T(2,128)(2,1)}) %all-reduce.12.cloned.1.call-update) | async-done | bytes 65552 | tf_op jit(solution)/shard_map/psum | solution.py:97
  139.5 5.1 fusion.75
  145.1 5.8 all_gather.34
  150.9 62.9 %reduce-scatter.16.cloned.1.call-done = bf16[128,64]{1,0:T(8,128)(2,1)} async-done(((bf16[2048,64]{1,0:T(8,128)(2,1)}), bf16[128,64]{1,0:T(8,128)(2,1)}) %reduce-scatter.16.cloned.1.call-update) | async-done | bytes 16400
  216.4 23.3 %all_gather.35 = bf16[64,2048]{1,0:T(8,128)(2,1)S(1)} all-gather(bf16[64,128]{1,0:T(8,128)(2,1)S(1)} %convolution_convert_fusion.9), channel_id=1, replica_groups=mesh['pipe'=2,'tensor'=4,'dp'=16] {'dp'}, dimensions={1}, use_global_device_ids=true | all-gather | bytes 278528 | tf_op jit(solution)/shard_map/all_gather | solution.py:107
  239.7 4.0 fusion.4
  243.8 33.9 %all-reduce.14.cloned.1.call-done = bf16[64,1024]{1,0:T(8,128)(2,1)} async-done(((bf16[64,1024]{1,0:T(8,128)(2,1)}), bf16[64,1024]{1,0:T(8,128)(2,1)}) %all-reduce.14.cloned.1.call-update) | async-done | bytes 131088 | tf_op jit(solution)/shard_map/psum | solution.py:119
  280.0 7.8 collective-permute-done
  287.9 40.6 %psum.150 = f32[64,1]{0,1:T(1,128)S(1)} all-reduce(f32[64,1]{0,1:T(1,128)S(1)} %bitcast.242), channel_id=1, replica_groups=mesh['pipe'=2,'tensor'=4,'dp'=16] {'dp'}, use_global_device_ids=true, to_apply=%region_8.9 | all-reduce | flops 64 | bytes 512 | tf_op jit(solution)/shard_map/psum | solution.py:89
  329.7 3.1 fusion.18
  333.9 74.6 %all-reduce.16.cloned.1.call-done = bf16[64,256,2]{0,2,1:T(2,128)(2,1)} async-done(((bf16[64,256,2]{0,2,1:T(2,128)(2,1)}), bf16[64,256,2]{0,2,1:T(2,128)(2,1)}) %all-reduce.16.cloned.1.call-update) | async-done | bytes 65552 | tf_op jit(solution)/shard_map/psum | solution.py:97
  409.5 5.1 fusion.77
  415.0 5.8 all_gather.36
  420.8 62.4 %reduce-scatter.18.cloned.1.call-done = bf16[128,64]{1,0:T(8,128)(2,1)} async-done(((bf16[2048,64]{1,0:T(8,128)(2,1)}), bf16[128,64]{1,0:T(8,128)(2,1)}) %reduce-scatter.18.cloned.1.call-update) | async-done | bytes 16400
  485.9 23.3 %all_gather.37 = bf16[64,2048]{1,0:T(8,128)(2,1)S(1)} all-gather(bf16[64,128]{1,0:T(8,128)(2,1)S(1)} %convolution_convert_fusion.8), channel_id=1, replica_groups=mesh['pipe'=2,'tensor'=4,'dp'=16] {'dp'}, dimensions={1}, use_global_device_ids=true | all-gather | bytes 278528 | tf_op jit(solution)/shard_map/all_gather | solution.py:107
  509.2 4.0 fusion.3
  513.3 34.0 %all-reduce.18.cloned.1.call-done = bf16[64,1024]{1,0:T(8,128)(2,1)} async-done(((bf16[64,1024]{1,0:T(8,128)(2,1)}), bf16[64,1024]{1,0:T(8,128)(2,1)}) %all-reduce.18.cloned.1.call-update) | async-done | bytes 131088 | tf_op jit(solution)/shard_map/psum | solution.py:119
  549.5 7.8 collective-permute-done.1
  557.5 40.6 %psum.153 = f32[64,1]{0,1:T(1,128)S(1)} all-reduce(f32[64,1]{0,1:T(1,128)S(1)} %bitcast.243), channel_id=1, replica_groups=mesh['pipe'=2,'tensor'=4,'dp'=16] {'dp'}, use_global_device_ids=true, to_apply=%region_15.16 | all-reduce | flops 64 | bytes 512 | tf_op jit(solution)/shard_map/psum | solution.py:89
  603.6 74.4 %all-reduce.20.cloned.1.call-done = bf16[64,256,2]{0,2,1:T(2,128)(2,1)} async-done(((bf16[64,256,2]{0,2,1:T(2,128)(2,1)}), bf16[64,256,2]{0,2,1:T(2,128)(2,1)}) %all-reduce.20.cloned.1.call-update) | async-done | bytes 65552 | tf_op jit(solution)/shard_map/psum | solution.py:97
  679.0 5.1 fusion.79
  684.5 5.8 all_gather.38
  690.3 62.9 %reduce-scatter.20.cloned.1.call-done = bf16[128,64]{1,0:T(8,128)(2,1)} async-done(((bf16[2048,64]{1,0:T(8,128)(2,1)}), bf16[128,64]{1,0:T(8,128)(2,1)}) %reduce-scatter.20.cloned.1.call-update) | async-done | bytes 16400
  755.9 23.3 %all_gather.39 = bf16[64,2048]{1,0:T(8,128)(2,1)S(1)} all-gather(bf16[64,128]{1,0:T(8,128)(2,1)S(1)} %convolution_convert_fusion.7), channel_id=1, replica_groups=mesh['pipe'=2,'tensor'=4,'dp'=16] {'dp'}, dimensions={1}, use_global_device_ids=true | all-gather | bytes 278528 | tf_op jit(solution)/shard_map/all_gather | solution.py:107
  779.2 4.0 fusion.2
  783.3 33.9 %all-reduce.22.cloned.1.call-done = bf16[64,1024]{1,0:T(8,128)(2,1)} async-done(((bf16[64,1024]{1,0:T(8,128)(2,1)}), bf16[64,1024]{1,0:T(8,128)(2,1)}) %all-reduce.22.cloned.1.call-update) | async-done | bytes 131088 | tf_op jit(solution)/shard_map/psum | solution.py:119
  819.5 7.7 collective-permute-done.2
  827.4 40.6 %psum.156 = f32[64,1]{0,1:T(1,128)S(1)} all-reduce(f32[64,1]{0,1:T(1,128)S(1)} %bitcast.241), channel_id=1, replica_groups=mesh['pipe'=2,'tensor'=4,'dp'=16] {'dp'}, use_global_device_ids=true, to_apply=%region_22.23 | all-reduce | flops 64 | bytes 512 | tf_op jit(solution)/shard_map/psum | solution.py:89
  869.2 3.1 fusion.24
  873.4 74.5 %all-reduce.24.cloned.1.call-done = bf16[64,256,2]{0,2,1:T(2,128)(2,1)} async-done(((bf16[64,256,2]{0,2,1:T(2,128)(2,1)}), bf16[64,256,2]{0,2,1:T(2,128)(2,1)}) %all-reduce.24.cloned.1.call-update) | async-done | bytes 65552 | tf_op jit(solution)/shard_map/psum | solution.py:97
  948.9 5.1 fusion.81
  954.5 5.8 all_gather.40
  960.3 62.5 %reduce-scatter.22.cloned.1.call-done = bf16[128,64]{1,0:T(8,128)(2,1)} async-done(((bf16[2048,64]{1,0:T(8,128)(2,1)}), bf16[128,64]{1,0:T(8,128)(2,1)}) %reduce-scatter.22.cloned.1.call-update) | async-done | bytes 16400
  1025.5 23.3 %all_gather.41 = bf16[64,2048]{1,0:T(8,128)(2,1)S(1)} all-gather(bf16[64,128]{1,0:T(8,128)(2,1)S(1)} %convolution_convert_fusion.6), channel_id=1, replica_groups=mesh['pipe'=2,'tensor'=4,'dp'=16] {'dp'}, dimensions={1}, use_global_device_ids=true | all-gather | bytes 278528 | tf_op jit(solution)/shard_map/all_gather | solution.py:107
  1048.8 4.0 fusion.1
  1052.9 33.9 %all-reduce.26.cloned.1.call-done = bf16[64,1024]{1,0:T(8,128)(2,1)} async-done(((bf16[64,1024]{1,0:T(8,128)(2,1)}), bf16[64,1024]{1,0:T(8,128)(2,1)}) %all-reduce.26.cloned.1.call-update) | async-done | bytes 131088 | tf_op jit(solution)/shard_map/psum | solution.py:119
  1089.1 7.8 collective-permute-done.3
  1097.0 40.6 %psum.159 = f32[64,1]{0,1:T(1,128)S(1)} all-reduce(f32[64,1]{0,1:T(1,128)S(1)} %bitcast.245), channel_id=1, replica_groups=mesh['pipe'=2,'tensor'=4,'dp'=16] {'dp'}, use_global_device_ids=true, to_apply=%region_29.30 | all-reduce | flops 64 | bytes 512 | tf_op jit(solution)/shard_map/psum | solution.py:89
  1143.2 74.3 %all-reduce.28.cloned.1.call-done = bf16[64,256,2]{0,2,1:T(2,128)(2,1)} async-done(((bf16[64,256,2]{0,2,1:T(2,128)(2,1)}), bf16[64,256,2]{0,2,1:T(2,128)(2,1)}) %all-reduce.28.cloned.1.call-update) | async-done | bytes 65552 | tf_op jit(solution)/shard_map/psum | solution.py:97
  1218.5 5.1 fusion.83
  1224.1 5.8 all_gather.42
  1229.9 62.7 %reduce-scatter.24.cloned.1.call-done = bf16[128,64]{1,0:T(8,128)(2,1)} async-done(((bf16[2048,64]{1,0:T(8,128)(2,1)}), bf16[128,64]{1,0:T(8,128)(2,1)}) %reduce-scatter.24.cloned.1.call-update) | async-done | bytes 16400
  1295.3 23.3 %all_gather.43 = bf16[64,2048]{1,0:T(8,128)(2,1)S(1)} all-gather(bf16[64,128]{1,0:T(8,128)(2,1)S(1)} %convolution_convert_fusion.5), channel_id=1, replica_groups=mesh['pipe'=2,'tensor'=4,'dp'=16] {'dp'}, dimensions={1}, use_global_device_ids=true | all-gather | bytes 278528 | tf_op jit(solution)/shard_map/all_gather | solution.py:107
  1318.6 4.0 fusion
  1322.6 72.2 %all-reduce = (f32[64,16]{0,1:T(8,128)S(1)}, f32[64,16]{0,1:T(8,128)S(1)}, f32[64,16]{0,1:T(8,128)S(1)}, f32[64,16]{0,1:T(8,128)S(1)}, f32[64,16]{0,1:T(8,128)S(1)}) all-reduce(f32[64,16]{0,1:T(8,128)S(1)} %get-tuple-element.12, f32[64,16]{0,1:T(8,128)S(1)} %get-tuple-element.10, ...), channel_id=1, replica_groups=mesh['pipe'=2,'tensor'=4,'dp'=16] {'dp'}, use_global_device_ids=true, to_apply=%region_48.49 | all-reduce | flops 5120 | bytes 40960 | tf_op jit(solution)/shard_map/psum | solution.py:116
  1395.3 6.2 psum.167
  (148 shorter events, 56.3 us)
Async XLA Ops:
  7.2 131.3 %all-reduce.12.cloned.1.call-start = ((), (), s32[]{:S(2)}) async-start(), calls=%async_computation.5 | async-start | bytes 262144 | tf_op jit(solution)/shard_map/psum | solution.py:97
  8.7 55.4 %copy-start.1 = (s32[64]{0:T(128)S(1)}, s32[64]{0:T(128)}, u32[]{:S(2)}) copy-start(s32[64]{0:T(128)} %param.11) | copy-start | bytes 772
  59.7 154.1 %reduce-scatter.16.cloned.1.call-start = ((), (), s32[]{:S(2)}) async-start(), calls=%async_computation.15 | async-start | bytes 557056
  63.8 213.9 %all-reduce.14.cloned.1.call-start = ((), (), s32[]{:S(2)}) async-start(), calls=%async_computation.6 | async-start | bytes 262144 | tf_op jit(solution)/shard_map/psum | solution.py:119
  243.7 164.7 %all-reduce.16.cloned.1.call-start = ((), (), s32[]{:S(2)}) async-start(), calls=%async_computation.7 | async-start | bytes 262144 | tf_op jit(solution)/shard_map/psum | solution.py:97
  278.7 9.1 collective-permute-start
  329.7 153.6 %reduce-scatter.18.cloned.1.call-start = ((), (), s32[]{:S(2)}) async-start(), calls=%async_computation.16 | async-start | bytes 557056
  333.8 213.4 %all-reduce.18.cloned.1.call-start = ((), (), s32[]{:S(2)}) async-start(), calls=%async_computation.8 | async-start | bytes 262144 | tf_op jit(solution)/shard_map/psum | solution.py:119
  513.2 164.8 %all-reduce.20.cloned.1.call-start = ((), (), s32[]{:S(2)}) async-start(), calls=%async_computation.9 | async-start | bytes 262144 | tf_op jit(solution)/shard_map/psum | solution.py:97
  548.2 9.1 collective-permute-start.1
  599.2 154.1 %reduce-scatter.20.cloned.1.call-start = ((), (), s32[]{:S(2)}) async-start(), calls=%async_computation.17 | async-start | bytes 557056
  603.5 213.7 %all-reduce.22.cloned.1.call-start = ((), (), s32[]{:S(2)}) async-start(), calls=%async_computation.10 | async-start | bytes 262144 | tf_op jit(solution)/shard_map/psum | solution.py:119
  783.2 164.7 %all-reduce.24.cloned.1.call-start = ((), (), s32[]{:S(2)}) async-start(), calls=%async_computation.11 | async-start | bytes 262144 | tf_op jit(solution)/shard_map/psum | solution.py:97
  818.1 9.1 collective-permute-start.2
  869.1 153.7 %reduce-scatter.22.cloned.1.call-start = ((), (), s32[]{:S(2)}) async-start(), calls=%async_computation.18 | async-start | bytes 557056
  873.3 213.5 %all-reduce.26.cloned.1.call-start = ((), (), s32[]{:S(2)}) async-start(), calls=%async_computation.12 | async-start | bytes 262144 | tf_op jit(solution)/shard_map/psum | solution.py:119
  1052.8 164.7 %all-reduce.28.cloned.1.call-start = ((), (), s32[]{:S(2)}) async-start(), calls=%async_computation.13 | async-start | bytes 262144 | tf_op jit(solution)/shard_map/psum | solution.py:97
  1087.8 9.1 collective-permute-start.3
  1138.8 153.9 %reduce-scatter.24.cloned.1.call-start = ((), (), s32[]{:S(2)}) async-start(), calls=%async_computation.19 | async-start | bytes 557056
  1142.9 258.6 %all-reduce.30.cloned.1.call-start = ((), (), s32[]{:S(2)}) async-start(), calls=%async_computation.14 | async-start | bytes 262144 | tf_op jit(solution)/shard_map/psum | solution.py:119
  1402.3 0.7 copy-start
Sparse Core Ops, SparseCore 0:
  59.8 78.6 all-reduce.11
  142.0 71.7 reduce-scatter.15
  243.9 33.8 all-reduce.13
  329.8 78.6 all-reduce.15
  411.5 71.6 reduce-scatter.17
  513.3 33.8 all-reduce.17
  599.3 78.6 all-reduce.19
  681.5 71.7 reduce-scatter.19
  783.3 33.8 all-reduce.21
  869.3 78.5 all-reduce.23
  951.1 71.6 reduce-scatter.21
  1052.9 33.8 all-reduce.25
  1138.9 78.6 all-reduce.27
  1220.9 71.7 reduce-scatter.23
  1322.7 33.9 all-reduce.29
where the time goes:
time: 1410 us
  waiting for transfers between devices  852 us (60%)
  blocking collectives  435 us (31%)
  other arithmetic  49.8 us (4%)
  matrix products  39.5 us (3%)
  between operations  15.2 us (1%)
    psum x5, waiting for transfers between devices, local(): kv_summed = lax.psum(kv_part.astype(jnp.bfloat16), 'dp').astype(jnp.float32)  371 us
    unnamed x20, waiting for transfers between devices  314 us
    psum x5, blocking collectives, local(): sums = lax.psum(jnp.sum(wide * wide, axis=1, keepdims=True), 'dp')  204 us
    psum x5, waiting for transfers between devices, local(): summed = lax.psum(total.astype(jnp.bfloat16), 'tensor').astype(jnp.float32)  136 us
    all_gather x5, blocking collectives, local(): heads_att = lax.all_gather(attended, 'dp', axis=1, tiled=True)  117 us
    psum x1, blocking collectives, local(): full_squares = lax.psum(squares, 'dp')  72.2 us
    another operation x10, other arithmetic  31.8 us
    ppermute x4, waiting for transfers between devices, from_behind(): return lax.ppermute(block, axis, route)  31.1 us
  transfers between devices with their start and end apart: 19, of which 18 were waited for; matrix products, arithmetic and copies ran while one was open for 4% of the time, Pallas kernels for 0%

commit v1 on v0

v1 whole, which is shorter than its diff:
```python
import functools
import math

import jax
import jax.numpy as jnp
import numpy as np
from jax import lax
from jax.experimental import pallas as pl
from jax.experimental.pallas import tpu as pltpu
from jax.sharding import PartitionSpec as P

HD = 128
GROUPS = 8
N_TENSOR = 4
N_DP = 16
THETA = 500000.0
EPS_NORM = 1e-05
EPS_RMS = 1e-06
STATS = 16

BF16 = jnp.bfloat16
F32 = jnp.float32
VMEM = pltpu.VMEM

S_SECTION, S_TENSOR, S_DATA, S_GROUPS = 0, 1, 2, 3


def rotary_tables(rows):
    positions = np.arange(rows, dtype=np.float64)[:, None]
    lanes = np.arange(HD)
    angle = positions * THETA ** (-2.0 * (lanes // 2) / HD)[None, :]
    sign = np.where(lanes % 2 == 0, -1.0, 1.0)[None, :]
    return np.cos(angle).astype(np.float32), (np.sin(angle) * sign).astype(np.float32)


def rotated(values, cosine, sine):
    lanes = lax.broadcasted_iota(jnp.int32, values.shape, 1)
    swapped = jnp.where(
        lanes % 2 == 0, pltpu.roll(values, HD - 1, 1), pltpu.roll(values, 1, 1)
    )
    return values * cosine + swapped * sine


def diagonal():
    return lax.broadcasted_iota(jnp.int32, (HD, HD), 0) == lax.broadcasted_iota(
        jnp.int32, (HD, HD), 1
    )


def two_parts(values):
    high = values.astype(BF16)
    return high, (values - high.astype(F32)).astype(BF16)


def project_kernel(step, scal, x0, x1, x2, x3, gain, wq, wkv, wout, send, scaled, kvs, stats):
    rows = x0.shape[0]
    cols = x0.shape[1]
    data_heads = send.shape[0]
    i = pl.program_id(0)
    active = scal[S_SECTION] == step

    @pl.when(jnp.logical_and(active, i == 0))
    def _():
        total = jnp.zeros((rows, 1), F32)
        for mask, ref in enumerate((x0, x1, x2, x3)):
            place = pl.multiple_of(lax.bitwise_xor(scal[S_TENSOR], mask) * cols, cols)
            wide = ref[...].astype(F32)
            total = total + jnp.sum(wide * wide, axis=1, keepdims=True)
            scaled[:, pl.ds(place, cols)] = (wide * gain[:, pl.ds(place, cols)]).astype(BF16)
        eye = diagonal()
        row = lax.broadcasted_iota(jnp.int32, (STATS, HD), 0)
        lines = jnp.zeros((STATS, HD), F32)
        for b in range(rows // HD):
            line = jnp.sum(
                jnp.where(eye, total[b * HD : (b + 1) * HD], 0.0), axis=0, keepdims=True
            )
            high, low = two_parts(line)
            lines = jnp.where(row == 2 * b, high.astype(F32), lines)
            lines = jnp.where(row == 2 * b + 1, low.astype(F32), lines)
        stats[...] = lines.astype(BF16)
        kvs[...] = jnp.dot(scaled[...], wkv[...], preferred_element_type=F32).astype(BF16)

    @pl.when(active)
    def _():
        part = jnp.dot(scaled[...], wq[...], preferred_element_type=F32).astype(BF16)
        for j in range(data_heads):
            send[j, :rows, :] = part[:, j * HD : (j + 1) * HD]
            first = pl.multiple_of((i * data_heads + j) * 16, 16)
            for c in range(4):
                send[j, rows + 16 * c : rows + 16 * c + 16, :] = kvs[
                    pl.ds(first, 16), c * HD : (c + 1) * HD
                ]
            send[j, rows + 64 :, :] = stats[...]

    @pl.when(jnp.logical_not(active))
    def _():
        for j in range(data_heads):
            head = wout[j * HD : (j + 1) * HD, :]
            gram = lax.dot_general(
                head, head, (((1,), (1,)), ((), ())), preferred_element_type=F32
            )
            high, low = two_parts(gram)
            send[j, :HD, :] = high
            send[j, HD:rows, :] = low
            send[j, rows:, :] = jnp.zeros((64 + STATS, HD), BF16)


def project(step, scal, pieces, gain, wq, wkv, wout):
    rows, cols = pieces[0].shape
    wide = cols * N_TENSOR
    heads = wq.shape[1] // HD
    steps = 4
    per = heads // steps
    whole = lambda shape: pl.BlockSpec(shape, lambda i, s: (0,) * len(shape))

    def q_block(i, s):
        return (0, jnp.where(s[S_SECTION] == step, i, 0))

    def out_block(i, s):
        return (jnp.where(s[S_SECTION] == step, 0, i), 0)

    return pl.pallas_call(
        functools.partial(project_kernel, step),
        out_shape=jax.ShapeDtypeStruct((heads, rows + 64 + STATS, HD), BF16),
        grid_spec=pltpu.PrefetchScalarGridSpec(
            num_scalar_prefetch=1,
            grid=(steps,),
            in_specs=[whole((rows, cols))] * 4
            + [
                whole((1, wide)),
                pl.BlockSpec((wide, per * HD), q_block),
                whole(wkv.shape),
                pl.BlockSpec((per * HD, wide), out_block),
            ],
            out_specs=pl.BlockSpec((per, rows + 64 + STATS, HD), lambda i, s: (i, 0, 0)),
            scratch_shapes=[
                VMEM((rows, wide), BF16),
                VMEM((rows, wkv.shape[1]), BF16),
                VMEM((STATS, HD), BF16),
            ],
        ),
        compiler_params=pltpu.CompilerParams(vmem_limit_bytes=24 * 2**20),
        name="project",
    )(scal, *pieces, gain, wq, wkv, wout)


def combine_kernel(width, scal, recv, cosine, sine, query, kv, gram, scale):
    rows = cosine.shape[0]
    raw = recv[0, :rows, :].astype(F32)
    for s in range(1, N_DP):
        raw = raw + recv[s, :rows, :].astype(F32)
    gram[...] = raw[:HD] + raw[HD : 2 * HD]
    tail = recv[0, rows:, :].astype(F32)
    for s in range(1, N_DP):
        tail = tail + recv[s, rows:, :].astype(F32)
    eye = diagonal()
    for b in range(rows // HD):
        line = tail[64 + 2 * b : 65 + 2 * b, :] + tail[65 + 2 * b : 66 + 2 * b, :]
        column = jnp.sum(jnp.where(eye, line, 0.0), axis=1, keepdims=True)
        factor = lax.rsqrt(column / width + EPS_NORM)
        scale[b * HD : (b + 1) * HD, :] = jnp.broadcast_to(factor, (HD, HD))
    query[...] = rotated(raw * scale[...], cosine[...], sine[...]).astype(BF16)
    first = pl.multiple_of(scal[S_DATA] * 16, 16)
    here = scale[pl.ds(first, 16), :]
    cos_here = cosine[pl.ds(first, 16), :]
    sin_here = sine[pl.ds(first, 16), :]
    for g in range(2):
        keys = tail[32 * g : 32 * g + 16] * here
        vals = tail[32 * g + 16 : 32 * g + 32] * here
        kv[g, :, :HD] = rotated(keys, cos_here, sin_here).astype(BF16)
        kv[g, :, HD:] = vals.astype(BF16)


def combine(scal, recv, cosine, sine, width):
    rows = cosine.shape[0]
    smem = pl.BlockSpec(memory_space=pltpu.SMEM)
    vmem = pl.BlockSpec(memory_space=VMEM)
    return pl.pallas_call(
        functools.partial(combine_kernel, float(width)),
        out_shape=(
            jax.ShapeDtypeStruct((rows, HD), BF16),
            jax.ShapeDtypeStruct((2, 16, 2 * HD), BF16),
            jax.ShapeDtypeStruct((HD, HD), F32),
        ),
        in_specs=[smem, vmem, vmem, vmem],
        out_specs=(vmem, vmem, vmem),
        scratch_shapes=[VMEM((rows, HD), F32)],
        compiler_params=pltpu.CompilerParams(vmem_limit_bytes=8 * 2**20),
        name="combine",
    )(scal, recv, cosine, sine)


def choose_kernel(scal, kv, send):
    for j in range(N_DP):
        send[j] = kv[scal[S_GROUPS + j]]


def choose(scal, kv):
    vmem = pl.BlockSpec(memory_space=VMEM)
    return pl.pallas_call(
        choose_kernel,
        out_shape=jax.ShapeDtypeStruct((N_DP,) + kv.shape[1:], BF16),
        in_specs=[pl.BlockSpec(memory_space=pltpu.SMEM), vmem],
        out_specs=vmem,
        name="choose",
    )(scal, kv)


def attended(query, kv):
    rows = query.shape[0]
    scores = lax.dot_general(
        query, kv[:, :HD], (((1,), (1,)), ((), ())), preferred_element_type=F32
    )
    allowed = lax.broadcasted_iota(jnp.int32, (rows, rows), 0) >= lax.broadcasted_iota(
        jnp.int32, (rows, rows), 1
    )
    expo = jnp.where(allowed, jnp.exp(scores * (1.0 / math.sqrt(HD))), 0.0)
    weights = (expo / jnp.sum(expo, axis=1, keepdims=True)).astype(BF16)
    return jnp.dot(weights, kv[:, HD:], preferred_element_type=F32).astype(BF16)


def attend_kernel(query, kv, send):
    result = attended(query[...], kv[...])
    for j in range(N_DP):
        send[j] = result


def attend(query, kv):
    rows = query.shape[0]
    vmem = pl.BlockSpec(memory_space=VMEM)
    return pl.pallas_call(
        attend_kernel,
        out_shape=jax.ShapeDtypeStruct((N_DP, rows, HD), BF16),
        in_specs=[vmem, vmem],
        out_specs=vmem,
        compiler_params=pltpu.CompilerParams(vmem_limit_bytes=8 * 2**20),
        name="attend",
    )(query, kv)


def attend_last_kernel(width, scal, query, kv, before, gram0, gram1, send):
    rows = query.shape[0]
    result = attended(query[...], kv[...])
    first_section = scal[S_SECTION] == 0
    mine = jnp.where(first_section, before[0], result)
    gram = jnp.where(first_section, gram1[...], gram0[...])
    high, low = two_parts(gram)
    image = jnp.dot(mine, high, preferred_element_type=F32) + jnp.dot(
        mine, low, preferred_element_type=F32
    )
    squares = jnp.sum(image * mine.astype(F32), axis=1, keepdims=True)
    spread = jnp.sqrt(jnp.maximum(squares / width, 0.0) + EPS_RMS)
    mean = jnp.sum(spread, axis=0, keepdims=True) / rows
    high, low = two_parts(mean)
    row = lax.broadcasted_iota(jnp.int32, (STATS, HD), 0)
    lines = jnp.where(row == 0, high.astype(F32), jnp.where(row == 1, low.astype(F32), 0.0))
    lines = lines.astype(BF16)
    for j in range(N_DP):
        send[j, :rows] = result
        send[j, rows:] = lines


def attend_last(scal, query, kv, before, gram0, gram1, width):
    rows = query.shape[0]
    vmem = pl.BlockSpec(memory_space=VMEM)
    return pl.pallas_call(
        functools.partial(attend_last_kernel, float(width)),
        out_shape=jax.ShapeDtypeStruct((N_DP, rows + STATS, HD), BF16),
        in_specs=[pl.BlockSpec(memory_space=pltpu.SMEM)] + [vmem] * 5,
        out_specs=vmem,
        compiler_params=pltpu.CompilerParams(vmem_limit_bytes=8 * 2**20),
        name="attend_last",
    )(scal, query, kv, before, gram0, gram1)


def out_kernel(rows, scal, recv, wout, o0, o1, o2, o3, joined):
    i = pl.program_id(0)
    heads = recv.shape[0]

    @pl.when(i == 0)
    def _():
        for h in range(heads):
            joined[:, h * HD : (h + 1) * HD] = recv[h, :rows, :]

    part = jnp.dot(joined[...], wout[...], preferred_element_type=F32).astype(BF16)
    extra = recv.shape[1] > rows
    if extra:
        lane = lax.broadcasted_iota(jnp.int32, (1, part.shape[1]), 1)
        sums = jnp.zeros((1, part.shape[1]), F32)
        for h in range(heads):
            value = recv[h, rows : rows + 1, :].astype(F32) + recv[
                h, rows + 1 : rows + 2, :
            ].astype(F32)
            value = jnp.concatenate([value] * (part.shape[1] // HD), axis=1)
            sums = sums + jnp.where(lane == scal[S_GROUPS + h], value, 0.0)
        high, low = two_parts(sums)
        row = lax.broadcasted_iota(jnp.int32, (STATS, part.shape[1]), 0)
        lines = jnp.where(
            row == 0, high.astype(F32), jnp.where(row == 1, low.astype(F32), 0.0)
        ).astype(BF16)
    for mask, ref in enumerate((o0, o1, o2, o3)):

        @pl.when(i == (mask + 3) % 4)
        def _():
            ref[:rows] = part
            if extra:
                ref[rows:] = lines


def project_out(scal, recv, wout, rows):
    heads, deep, _ = recv.shape
    wide = wout.shape[1]
    cols = wide // N_TENSOR
    whole = lambda shape: pl.BlockSpec(shape, lambda i, s: (0,) * len(shape))
    piece = jax.ShapeDtypeStruct((deep, cols), BF16)
    return pl.pallas_call(
        functools.partial(out_kernel, rows),
        out_shape=(piece,) * 4,
        grid_spec=pltpu.PrefetchScalarGridSpec(
            num_scalar_prefetch=1,
            grid=(N_TENSOR,),
            in_specs=[
                whole(recv.shape),
                pl.BlockSpec(
                    (heads * HD, cols),
                    lambda i, s: (0, lax.bitwise_xor(s[S_TENSOR], (i + 1) % 4)),
                ),
            ],
            out_specs=(whole((deep, cols)),) * 4,
            scratch_shapes=[VMEM((rows, heads * HD), BF16)],
        ),
        compiler_params=pltpu.CompilerParams(vmem_limit_bytes=24 * 2**20),
        name="project_out",
    )(scal, recv, wout)


def fresh_kernel(wide, o0, o1, o2, o3, fresh):
    total = o0[...].astype(F32)
    for ref in (o1, o2, o3):
        total = total + ref[...].astype(F32)
    fresh[...] = (wide[...].astype(F32) + total).astype(BF16)


def add_fresh(wide, parts):
    vmem = pl.BlockSpec(memory_space=VMEM)
    return pl.pallas_call(
        fresh_kernel,
        out_shape=jax.ShapeDtypeStruct(wide.shape, BF16),
        in_specs=[vmem] * 5,
        out_specs=vmem,
        name="add_fresh",
    )(wide, *parts)


def last_kernel(scal, before, wide, o0, o1, o2, o3, out, importance):
    rows = wide.shape[0]
    total = o0[...].astype(F32)
    for ref in (o1, o2, o3):
        total = total + ref[...].astype(F32)
    fresh = (wide[...].astype(F32) + total[:rows]).astype(BF16)
    out[...] = jnp.where(scal[S_SECTION] == 0, before[...], fresh)
    importance[...] = total[rows : rows + 1, :HD] + total[rows + 1 : rows + 2, :HD]


def add_last(scal, before, wide, parts):
    vmem = pl.BlockSpec(memory_space=VMEM)
    return pl.pallas_call(
        last_kernel,
        out_shape=(
            jax.ShapeDtypeStruct(wide.shape, BF16),
            jax.ShapeDtypeStruct((1, HD), F32),
        ),
        in_specs=[pl.BlockSpec(memory_space=pltpu.SMEM)] + [vmem] * 6,
        out_specs=(vmem, vmem),
        name="add_last",
    )(scal, before, wide, *parts)


def swap(block, mask):
    return lax.ppermute(block, "tensor", [(t, t ^ mask) for t in range(N_TENSOR)])


def to_next_section(block, mask):
    route = [(t, N_TENSOR + (t ^ mask)) for t in range(N_TENSOR)]
    return lax.ppermute(block, ("pipe", "tensor"), route)


def local(hidden_in, norm_gain, w_query, w_keyval, w_out, head_group):
    section = lax.axis_index("pipe")
    tensor = lax.axis_index("tensor")
    data = lax.axis_index("dp")
    rows, cols = hidden_in.shape[0], hidden_in.shape[3]
    width = cols * N_TENSOR * N_DP
    gain = norm_gain.astype(F32)
    wq = w_query[0]
    wkv = w_keyval[0].reshape(wq.shape[0], -1)
    wout = w_out[0]
    heads = wq.shape[1] // HD
    groups = lax.dynamic_slice_in_dim(head_group, tensor * heads, heads, 0)
    scal = jnp.concatenate([jnp.stack([section, tensor, data]).astype(jnp.int32), groups])
    cosine, sine = map(jnp.asarray, rotary_tables(rows))

    def to_heads(step, pieces):
        send = project(step, scal, pieces, gain, wq, wkv, wout)
        recv = lax.all_to_all(send, "dp", 0, 0)
        query, kv, gram = combine(scal, recv, cosine, sine, width)
        every = lax.all_gather(kv, "tensor")
        mine = choose(scal, every.reshape(GROUPS, 16, 2 * HD))
        kv_mine = lax.all_to_all(mine, "dp", 0, 0).reshape(rows, 2 * HD)
        return query, kv_mine, gram

    mine = hidden_in.reshape(rows, cols)
    far = swap(mine, 2)
    pieces = (mine, swap(mine, 1), far, swap(far, 1))
    query, kv, gram0 = to_heads(0, pieces)
    att0 = attend(query, kv)
    recv = lax.all_to_all(att0, "dp", 0, 0)
    parts = project_out(scal, recv, wout, rows)
    fresh0 = add_fresh(mine, (parts[0],) + tuple(swap(parts[m], m) for m in (1, 2, 3)))

    far = to_next_section(fresh0, 2)
    near = to_next_section(fresh0, 0)
    pieces = (near, swap(near, 1), far, swap(far, 1))
    query, kv, gram1 = to_heads(1, pieces)
    att1 = attend_last(scal, query, kv, att0, gram0, gram1, width)
    recv = lax.all_to_all(att1, "dp", 0, 0)
    parts = project_out(scal, recv, wout, rows)
    out, importance = add_last(
        scal, fresh0, near, (parts[0],) + tuple(swap(parts[m], m) for m in (1, 2, 3))
    )
    return out.reshape(1, rows, 1, 1, cols), importance[:, :GROUPS]


def solution(mesh):
    in_specs = (
        P(None, "dp", "tensor", None),
        P("pipe", "dp"),
        P("pipe", "dp", "tensor"),
        P("pipe", "dp", "tensor", None),
        P("pipe", "tensor", "dp"),
        P(),
    )
    out_specs = (P("pipe", None, "dp", "tensor", None), P("pipe", None))
    return jax.shard_map(local, mesh=mesh, in_specs=in_specs, out_specs=out_specs, check_vma=False)
```

time: 1410 us -> 205 us (0.15)
  waiting for transfers between devices: 852 us -> 27 us
  blocking collectives: 435 us -> 129 us
  other arithmetic: 49.8 us -> 0.77 us
  matrix products: 39.5 us -> 0 us
  Pallas kernels: 0 us -> 22.9 us
  between operations: 15.2 us -> 0.84 us
    psum x10 -> x0, waiting for transfers between devices: 507 us -> none  [the longest x5 371 us: local(): kv_summed = lax.psum(kv_part.astype(jnp.bfloat16), 'dp').astype(jnp.float32)]
    unnamed x20 -> x0, waiting for transfers between devices: 314 us -> none
    psum x7 -> x0, blocking collectives: 283 us -> none  [the longest x5 204 us: local(): sums = lax.psum(jnp.sum(wide * wide, axis=1, keepdims=True), 'dp')]
    all_gather x11 -> x2, blocking collectives: 153 us -> 12.1 us  [to_heads(): every = lax.all_gather(kv, 'tensor')]
    all_to_all x0 -> x6, blocking collectives: none -> 117 us  [the longest x2 53.3 us: to_heads(): recv = lax.all_to_all(send, 'dp', 0, 0)]
    dot_general x25 -> x0, matrix products: 39.5 us -> none  [the longest x5 19.8 us: local(): jnp.einsum('rhk,hkc->rhc', heads_att.reshape(block, heads_here, HD), out_...]
    another operation x20 -> x0, other arithmetic: 34.1 us -> none
    pallas_call x0 -> x12, Pallas kernels: none -> 22.9 us  [the longest x2 6.67 us: project_out(): pl.pallas_call(functools.partial(out_kernel, rows), out_shape=(piece,) *...]
  transfers between devices with their start and end apart: 19 -> 13, of which waited for: 18 -> 8; matrix products, arithmetic and copies ran while one was open for 4% -> 1% of each run, Pallas kernels for 0% -> 0%
where the time goes in v1:
time: 205 us; the launch traced here: 203 us
  blocking collectives  129 us (63%)
  waiting for transfers between devices  27 us (13%)
  Pallas kernels  22.9 us (11%)
  local copies, waits for them, and re-layouts  15.1 us (7%)
  starting transfers between devices  7.89 us (4%)
    all_to_all x2, blocking collectives, to_heads(): recv = lax.all_to_all(send, 'dp', 0, 0)  53.3 us
    all_to_all x2, blocking collectives, to_heads(): kv_mine = lax.all_to_all(mine, 'dp', 0, 0).reshape(rows, 2 * HD)  23 us
    all_to_all x1, blocking collectives, local(): recv = lax.all_to_all(att1, 'dp', 0, 0)  20.5 us
    all_to_all x1, blocking collectives, local(): recv = lax.all_to_all(att0, 'dp', 0, 0)  19.8 us
    ppermute x11, waiting for transfers between devices, swap(): lax.ppermute(block, 'tensor', [(t, t ^ mask) for t in range(N_TENSOR)])  19 us
    unnamed x45, local copies, waits for them, and re-layouts  15 us
    all_gather x2, blocking collectives, to_heads(): every = lax.all_gather(kv, 'tensor')  12.1 us
    ppermute x2, waiting for transfers between devices, to_next_section(): return lax.ppermute(block, ('pipe', 'tensor'), route)  7.92 us
  transfers between devices with their start and end apart: 13, of which 8 were waited for; matrix products, arithmetic and copies ran while one was open for 1% of the time, Pallas kernels for 0%

profile of v1, /device:TPU:4, one launch (start us, length us, event | category | flops | bytes accessed | tf_op | source)
XLA Modules:
  0.0 203.2 jit_solution(5657477042350736449)
XLA Ops:
  0.7 1.3 collective-permute-start.1
  1.9 4.2 %collective-permute-done.1.x2 = bf16[256,256]{1,0:T(8,128)(2,1)S(1)} collective-permute-done((bf16[256,256]{1,0:T(8,128)(2,1)}, bf16[256,256]{1,0:T(8,128)(2,1)S(1)}, u32[]{:S(2)}, u32[]{:S(2)}) %collective-permute-start.1) | collective-permute-done | bytes 131104 | tf_op jit(solution)/shard_map/ppermute | solution.py:380
  6.2 0.7 convert_element_type.3.gain
  6.9 1.4 copy.10
  8.3 0.1 dynamic_slice.3
  8.4 0.1 pad_add_fusion.scal
  8.5 2.2 %copy-done = bf16[1,2048,1024]{2,1,0:T(8,128)(2,1)S(1)} copy-done((bf16[1,2048,1024]{2,1,0:T(8,128)(2,1)S(1)}, bf16[1,2048,1024]{2,1,0:T(8,128)(2,1)}, u32[]{:S(2)}) %copy-start) | copy-done | bytes 4194328
  10.7 2.2 %copy-done.4 = bf16[1,1024,2048]{2,1,0:T(8,128)(2,1)S(1)} copy-done((bf16[1,1024,2048]{2,1,0:T(8,128)(2,1)S(1)}, bf16[1,1024,2048]{2,1,0:T(8,128)(2,1)}, u32[]{:S(2)}) %copy-start.4) | copy-done | bytes 4194328
  12.9 2.5 %project.2 = bf16[16,336,128]{2,1,0:T(8,128)(2,1)S(1)} custom-call(s32[19]{0:T(128)S(1)} %pad_add_fusion.scal, bf16[256,256]{1,0:T(8,128)(2,1)S(1)} %bitcast.24, bf16[256,256]{1,0:T(8,128)(2,1)S(1)} %collective-permute-done.x1, bf16[256,256]{1,0:T(8,128)(2,1)S(1)} %collective-permute-done.1.x2, bf16[256,256]{1,0:T(8,128)(2,1)S(1)} %collective-permute-done.2.x3, ...), custom_call_target="tpu_custom_call" | custom-call | tf_op jit(solution)/shard_map/project/pallas_call | solution.py:122
  15.5 29.4 %all_to_all.30.recv = bf16[16,336,128]{2,1,0:T(8,128)(2,1)S(1)} all-to-all(bf16[16,336,128]{2,1,0:T(8,128)(2,1)S(1)} %project.2), channel_id=1, replica_groups=mesh['pipe'=2,'tensor'=4,'dp'=16] {'dp'}, dimensions={0} | all-to-all | bytes 2752512 | tf_op jit(solution)/shard_map/all_to_all | solution.py:405
  44.8 0.9 combine.2
  45.7 5.7 %all-gather.kv = bf16[8,16,256]{2,1,0:T(8,128)(2,1)} all-gather(bf16[2,16,256]{2,1,0:T(8,128)(2,1)S(1)} %get-tuple-element.19), channel_id=2, replica_groups=mesh['pipe'=2,'tensor'=4,'dp'=16] {'tensor'}, dimensions={0}, use_global_device_ids=true | all-gather | bytes 81920 | tf_op jit(solution)/shard_map/all_gather | solution.py:407
  51.4 1.5 choose.2
  52.9 11.5 %all_to_all.31 = bf16[16,16,256]{2,1,0:T(8,128)(2,1)S(1)} all-to-all(bf16[16,16,256]{2,1,0:T(8,128)(2,1)} %choose.2), channel_id=1, replica_groups=mesh['pipe'=2,'tensor'=4,'dp'=16] {'dp'}, dimensions={0} | all-to-all | bytes 262144 | tf_op jit(solution)/shard_map/all_to_all | solution.py:409
  64.4 0.5 attend.1.before
  64.9 19.8 %all_to_all.32.recv = bf16[16,256,128]{2,1,0:T(8,128)(2,1)S(1)} all-to-all(bf16[16,256,128]{2,1,0:T(8,128)(2,1)S(1)} %attend.1.before), channel_id=1, replica_groups=mesh['pipe'=2,'tensor'=4,'dp'=16] {'dp'}, dimensions={0} | all-to-all | bytes 2097152 | tf_op jit(solution)/shard_map/all_to_all | solution.py:417
  84.7 2.2 %copy-done.1 = bf16[1,2048,1024]{2,1,0:T(8,128)(2,1)S(1)} copy-done((bf16[1,2048,1024]{2,1,0:T(8,128)(2,1)S(1)}, bf16[1,2048,1024]{2,1,0:T(8,128)(2,1)}, u32[]{:S(2)}) %copy-start.1) | copy-done | bytes 4194328
  86.8 3.3 %project_out.2 = (bf16[256,256]{1,0:T(8,128)(2,1)S(1)}, bf16[256,256]{1,0:T(8,128)(2,1)S(1)}, bf16[256,256]{1,0:T(8,128)(2,1)S(1)}, bf16[256,256]{1,0:T(8,128)(2,1)S(1)}) custom-call(s32[19]{0:T(128)S(1)} %copy-done.13, bf16[16,256,128]{2,1,0:T(8,128)(2,1)S(1)} %all_to_all.32.recv, bf16[2048,1024]{1,0:T(8,128)(2,1)S(1)} %bitcast.14), custom_call_target="tpu_custom_call" | custom-call | tf_op jit(solution)/shard_map/project_out/pallas_call | solution.py:316
  90.2 0.6 copy-done.11
  90.8 1.2 collective-permute-start.4
  92.0 0.7 collective-permute-start.5
  92.7 4.4 %collective-permute-done.4.o2 = bf16[256,256]{1,0:T(8,128)(2,1)S(1)} collective-permute-done((bf16[256,256]{1,0:T(8,128)(2,1)S(1)}, bf16[256,256]{1,0:T(8,128)(2,1)S(1)}, u32[]{:S(2)}, u32[]{:S(2)}) %collective-permute-start.4) | collective-permute-done | bytes 131104 | tf_op jit(solution)/shard_map/ppermute | solution.py:380
  97.1 2.0 %collective-permute-done.5.o3 = bf16[256,256]{1,0:T(8,128)(2,1)S(1)} collective-permute-done((bf16[256,256]{1,0:T(8,128)(2,1)S(1)}, bf16[256,256]{1,0:T(8,128)(2,1)S(1)}, u32[]{:S(2)}, u32[]{:S(2)}) %collective-permute-start.5) | collective-permute-done | bytes 131104 | tf_op jit(solution)/shard_map/ppermute | solution.py:380
  99.2 0.7 copy-done.20
  99.8 1.9 add_fresh.1.before
  101.7 1.3 collective-permute-start.8
  103.0 1.3 collective-permute-start.6
  104.3 5.1 %collective-permute-done.8.x2 = bf16[256,256]{1,0:T(8,128)(2,1)S(1)} collective-permute-done((bf16[256,256]{1,0:T(8,128)(2,1)}, bf16[256,256]{1,0:T(8,128)(2,1)S(1)}, u32[]{:S(2)}, u32[]{:S(2)}) %collective-permute-start.8) | collective-permute-done | bytes 131104 | tf_op jit(solution)/shard_map/ppermute | solution.py:385
  109.4 2.8 %collective-permute-done.6.x0.wide = bf16[256,256]{1,0:T(8,128)(2,1)S(1)} collective-permute-done((bf16[256,256]{1,0:T(8,128)(2,1)}, bf16[256,256]{1,0:T(8,128)(2,1)S(1)}, u32[]{:S(2)}, u32[]{:S(2)}) %collective-permute-start.6) | collective-permute-done | bytes 131104 | tf_op jit(solution)/shard_map/ppermute | solution.py:385
  112.2 1.3 collective-permute-done.7.x1
  113.6 2.2 %copy-done.2 = bf16[1,2048,1024]{2,1,0:T(8,128)(2,1)S(1)} copy-done((bf16[1,2048,1024]{2,1,0:T(8,128)(2,1)S(1)}, bf16[1,2048,1024]{2,1,0:T(8,128)(2,1)}, u32[]{:S(2)}) %copy-start.2) | copy-done | bytes 4194328
  115.8 2.2 %copy-done.5 = bf16[1,1024,2048]{2,1,0:T(8,128)(2,1)S(1)} copy-done((bf16[1,1024,2048]{2,1,0:T(8,128)(2,1)S(1)}, bf16[1,1024,2048]{2,1,0:T(8,128)(2,1)}, u32[]{:S(2)}) %copy-start.5) | copy-done | bytes 4194328
  118.0 3.4 %project.3 = bf16[16,336,128]{2,1,0:T(8,128)(2,1)S(1)} custom-call(s32[19]{0:T(128)S(1)} %copy-done.13, bf16[256,256]{1,0:T(8,128)(2,1)S(1)} %collective-permute-done.6.x0.wide, bf16[256,256]{1,0:T(8,128)(2,1)S(1)} %collective-permute-done.7.x1, bf16[256,256]{1,0:T(8,128)(2,1)S(1)} %collective-permute-done.8.x2, ...), custom_call_target="tpu_custom_call" | custom-call | tf_op jit(solution)/shard_map/project/pallas_call | solution.py:122
  121.4 23.9 %all_to_all.33.recv = bf16[16,336,128]{2,1,0:T(8,128)(2,1)S(1)} all-to-all(bf16[16,336,128]{2,1,0:T(8,128)(2,1)S(1)} %project.3), channel_id=1, replica_groups=mesh['pipe'=2,'tensor'=4,'dp'=16] {'dp'}, dimensions={0} | all-to-all | bytes 2752512 | tf_op jit(solution)/shard_map/all_to_all | solution.py:405
  145.3 0.8 combine.3
  146.1 6.5 %all-gather.1.kv = bf16[8,16,256]{2,1,0:T(8,128)(2,1)} all-gather(bf16[2,16,256]{2,1,0:T(8,128)(2,1)S(1)} %get-tuple-element.25), channel_id=3, replica_groups=mesh['pipe'=2,'tensor'=4,'dp'=16] {'tensor'}, dimensions={0}, use_global_device_ids=true | all-gather | bytes 81920 | tf_op jit(solution)/shard_map/all_gather | solution.py:407
  152.6 1.5 choose.3
  154.1 11.5 %all_to_all.34 = bf16[16,16,256]{2,1,0:T(8,128)(2,1)S(1)} all-to-all(bf16[16,16,256]{2,1,0:T(8,128)(2,1)} %choose.3), channel_id=1, replica_groups=mesh['pipe'=2,'tensor'=4,'dp'=16] {'dp'}, dimensions={0} | all-to-all | bytes 262144 | tf_op jit(solution)/shard_map/all_to_all | solution.py:409
  165.6 1.3 attend_last.1
  166.9 20.5 %all_to_all.35.recv = bf16[16,272,128]{2,1,0:T(8,128)(2,1)S(1)} all-to-all(bf16[16,272,128]{2,1,0:T(8,128)(2,1)S(1)} %attend_last.1), channel_id=1, replica_groups=mesh['pipe'=2,'tensor'=4,'dp'=16] {'dp'}, dimensions={0} | all-to-all | bytes 2228224 | tf_op jit(solution)/shard_map/all_to_all | solution.py:426
  187.4 3.3 %project_out.3 = (bf16[272,256]{1,0:T(8,128)(2,1)S(1)}, bf16[272,256]{1,0:T(8,128)(2,1)S(1)}, bf16[272,256]{1,0:T(8,128)(2,1)S(1)}, bf16[272,256]{1,0:T(8,128)(2,1)S(1)}) custom-call(s32[19]{0:T(128)S(1)} %copy-done.14, bf16[16,272,128]{2,1,0:T(8,128)(2,1)S(1)} %all_to_all.35.recv, bf16[2048,1024]{1,0:T(8,128)(2,1)S(1)} %bitcast.16), custom_call_target="tpu_custom_call" | custom-call | tf_op jit(solution)/shard_map/project_out/pallas_call | solution.py:316
  190.8 0.6 copy-done.10
  191.4 2.0 collective-permute-start.11
  193.4 0.1 collective-permute-start.12
  193.6 4.4 %collective-permute-done.11.o2 = bf16[272,256]{1,0:T(8,128)(2,1)S(1)} collective-permute-done((bf16[272,256]{1,0:T(8,128)(2,1)S(1)}, bf16[272,256]{1,0:T(8,128)(2,1)S(1)}, u32[]{:S(2)}, u32[]{:S(2)}) %collective-permute-start.11) | collective-permute-done | bytes 139296 | tf_op jit(solution)/shard_map/ppermute | solution.py:380
  198.0 2.6 %collective-permute-done.12.o3 = bf16[272,256]{1,0:T(8,128)(2,1)S(1)} collective-permute-done((bf16[272,256]{1,0:T(8,128)(2,1)S(1)}, bf16[272,256]{1,0:T(8,128)(2,1)S(1)}, u32[]{:S(2)}, u32[]{:S(2)}) %collective-permute-start.12) | collective-permute-done | bytes 139296 | tf_op jit(solution)/shard_map/ppermute | solution.py:380
  200.6 0.6 copy-done.17
  201.2 2.0 add_last.1
  (46 shorter events, 0.1 us)
Async XLA Ops:
  0.6 7.9 %copy-start.6 = (bf16[256,1,1,256]{3,0,2,1:T(8,128)(2,1)S(1)}, bf16[256,1,1,256]{3,0,2,1:T(8,128)(2,1)}, u32[]{:S(2)}) copy-start(bf16[256,1,1,256]{3,0,2,1:T(8,128)(2,1)} %param.8) | copy-start | bytes 393220
  0.6 7.7 %copy-start.21 = (s32[64]{0:T(128)S(1)}, s32[64]{0:T(128)}, u32[]{:S(2)}) copy-start(s32[64]{0:T(128)} %param.13) | copy-start | bytes 772
  0.7 5.5 %collective-permute-start.1 = (bf16[256,256]{1,0:T(8,128)(2,1)}, bf16[256,256]{1,0:T(8,128)(2,1)S(1)}, u32[]{:S(2)}, u32[]{:S(2)}) collective-permute-start(bf16[256,256]{1,0:T(8,128)(2,1)} %bitcast.21), channel_id=1, source_target_pairs={{0,32},{16,48},{32,0},{48,16},{1,33},{17,49},{33,1},{49,17},{2,34}... | collective-permute-start | bytes 393224 | tf_op jit(solution)/shard_map/ppermute | solution.py:380
  1.9 6.6 %collective-permute-start = (bf16[256,256]{1,0:T(8,128)(2,1)}, bf16[256,256]{1,0:T(8,128)(2,1)S(1)}, u32[]{:S(2)}, u32[]{:S(2)}) collective-permute-start(bf16[256,256]{1,0:T(8,128)(2,1)} %bitcast.22), channel_id=1, source_target_pairs={{0,16},{16,0},{32,48},{48,32},{1,17},{17,1},{33,49},{49,33},{2,18}... | collective-permute-start | bytes 393224 | tf_op jit(solution)/shard_map/ppermute | solution.py:380
  6.2 2.3 %collective-permute-start.2 = (bf16[256,256]{1,0:T(8,128)(2,1)S(1)}, bf16[256,256]{1,0:T(8,128)(2,1)S(1)}, u32[]{:S(2)}, u32[]{:S(2)}) collective-permute-start(bf16[256,256]{1,0:T(8,128)(2,1)S(1)} %collective-permute-done.1.x2), channel_id=1, source_target_pairs={{0,16},{16,0},{32,48},{48,32},{1,17},{17,1},{33,49},{49,33},{2,18}... | collective-permute-start | bytes 393224 | tf_op jit(solution)/shard_map/ppermute | solution.py:380
  8.5 36.3 %copy-start.12 = (s32[19]{0:T(128)}, s32[19]{0:T(128)S(1)}, u32[]{:S(2)}) copy-start(s32[19]{0:T(128)S(1)} %pad_add_fusion.scal) | copy-start | bytes 232
  8.5 2.2 %copy-start = (bf16[1,2048,1024]{2,1,0:T(8,128)(2,1)S(1)}, bf16[1,2048,1024]{2,1,0:T(8,128)(2,1)}, u32[]{:S(2)}) copy-start(bf16[1,2048,1024]{2,1,0:T(8,128)(2,1)} %param.12) | copy-start | bytes 12582916
  10.7 2.2 %copy-start.4 = (bf16[1,1024,2048]{2,1,0:T(8,128)(2,1)S(1)}, bf16[1,1024,2048]{2,1,0:T(8,128)(2,1)}, u32[]{:S(2)}) copy-start(bf16[1,1024,2048]{2,1,0:T(8,128)(2,1)} %param.10) | copy-start | bytes 12582916
  15.4 29.4 %copy-start.8 = (f32[256,128]{1,0:T(8,128)S(1)}, f32[256,128]{1,0:T(8,128)}, u32[]{:S(2)}) copy-start(f32[256,128]{1,0:T(8,128)} %constant.26.clone.sine) | copy-start | bytes 393220
  15.5 29.4 %copy-start.9 = (f32[256,128]{1,0:T(8,128)S(1)}, f32[256,128]{1,0:T(8,128)}, u32[]{:S(2)}) copy-start(f32[256,128]{1,0:T(8,128)} %constant.25.clone.cosine) | copy-start | bytes 393220
  64.4 20.2 %copy-start.13 = (s32[19]{0:T(128)S(1)}, s32[19]{0:T(128)}, u32[]{:S(2)}) copy-start(s32[19]{0:T(128)} %copy-done.12) | copy-start | bytes 232
  84.7 2.2 %copy-start.1 = (bf16[1,2048,1024]{2,1,0:T(8,128)(2,1)S(1)}, bf16[1,2048,1024]{2,1,0:T(8,128)(2,1)}, u32[]{:S(2)}) copy-start(bf16[1,2048,1024]{2,1,0:T(8,128)(2,1)} %param.12) | copy-start | bytes 12582916
  90.2 0.7 copy-start.11
  90.8 1.9 collective-permute-start.3
  90.8 6.3 %collective-permute-start.4 = (bf16[256,256]{1,0:T(8,128)(2,1)S(1)}, bf16[256,256]{1,0:T(8,128)(2,1)S(1)}, u32[]{:S(2)}, u32[]{:S(2)}) collective-permute-start(bf16[256,256]{1,0:T(8,128)(2,1)S(1)} %get-tuple-element.22), channel_id=1, source_target_pairs={{0,32},{16,48},{32,0},{48,16},{1,33},{17,49},{33,1},{49,17},{2,34}... | collective-permute-start | bytes 393224 | tf_op jit(solution)/shard_map/ppermute | solution.py:380
  92.0 7.1 %collective-permute-start.5 = (bf16[256,256]{1,0:T(8,128)(2,1)S(1)}, bf16[256,256]{1,0:T(8,128)(2,1)S(1)}, u32[]{:S(2)}, u32[]{:S(2)}) collective-permute-start(bf16[256,256]{1,0:T(8,128)(2,1)S(1)} %get-tuple-element.23), channel_id=1, source_target_pairs={{0,48},{16,32},{32,16},{48,0},{1,49},{17,33},{33,17},{49,1},{2,50}... | collective-permute-start | bytes 393224 | tf_op jit(solution)/shard_map/ppermute | solution.py:380
  92.7 6.5 %copy-start.18 = (bf16[256,256]{1,0:T(8,128)(2,1)}, bf16[256,256]{1,0:T(8,128)(2,1)S(1)}, u32[]{:S(2)}) copy-start(bf16[256,256]{1,0:T(8,128)(2,1)S(1)} %collective-permute-done.3.o1) | copy-start | bytes 393220
  97.1 2.0 %copy-start.19 = (bf16[256,256]{1,0:T(8,128)(2,1)}, bf16[256,256]{1,0:T(8,128)(2,1)S(1)}, u32[]{:S(2)}) copy-start(bf16[256,256]{1,0:T(8,128)(2,1)S(1)} %collective-permute-done.4.o2) | copy-start | bytes 393220
  99.2 0.7 copy-start.20
  101.7 7.7 %collective-permute-start.8 = (bf16[256,256]{1,0:T(8,128)(2,1)}, bf16[256,256]{1,0:T(8,128)(2,1)S(1)}, u32[]{:S(2)}, u32[]{:S(2)}) collective-permute-start(bf16[256,256]{1,0:T(8,128)(2,1)} %add_fresh.1.before), channel_id=1, source_target_pairs={{0,96},{16,112},{32,64},{48,80},{1,97},{17,113},{33,65},{49,81},{2... | collective-permute-start | bytes 393224 | tf_op jit(solution)/shard_map/ppermute | solution.py:385
  103.0 9.2 %collective-permute-start.6 = (bf16[256,256]{1,0:T(8,128)(2,1)}, bf16[256,256]{1,0:T(8,128)(2,1)S(1)}, u32[]{:S(2)}, u32[]{:S(2)}) collective-permute-start(bf16[256,256]{1,0:T(8,128)(2,1)} %add_fresh.1.before), channel_id=1, source_target_pairs={{0,64},{16,80},{32,96},{48,112},{1,65},{17,81},{33,97},{49,113},{2... | collective-permute-start | bytes 393224 | tf_op jit(solution)/shard_map/ppermute | solution.py:385
  109.4 2.8 %collective-permute-start.9 = (bf16[256,256]{1,0:T(8,128)(2,1)S(1)}, bf16[256,256]{1,0:T(8,128)(2,1)S(1)}, u32[]{:S(2)}, u32[]{:S(2)}) collective-permute-start(bf16[256,256]{1,0:T(8,128)(2,1)S(1)} %collective-permute-done.8.x2), channel_id=1, source_target_pairs={{0,16},{16,0},{32,48},{48,32},{1,17},{17,1},{33,49},{49,33},{2,18}... | collective-permute-start | bytes 393224 | tf_op jit(solution)/shard_map/ppermute | solution.py:380
  112.2 9.1 %copy-start.7 = (bf16[256,256]{1,0:T(8,128)(2,1)}, bf16[256,256]{1,0:T(8,128)(2,1)S(1)}, u32[]{:S(2)}) copy-start(bf16[256,256]{1,0:T(8,128)(2,1)S(1)} %collective-permute-done.6.x0.wide) | copy-start | bytes 393220
  112.2 1.3 collective-permute-start.7
  113.6 2.2 %copy-start.2 = (bf16[1,2048,1024]{2,1,0:T(8,128)(2,1)S(1)}, bf16[1,2048,1024]{2,1,0:T(8,128)(2,1)}, u32[]{:S(2)}) copy-start(bf16[1,2048,1024]{2,1,0:T(8,128)(2,1)} %param.12) | copy-start | bytes 12582916
  115.8 2.2 %copy-start.5 = (bf16[1,1024,2048]{2,1,0:T(8,128)(2,1)S(1)}, bf16[1,1024,2048]{2,1,0:T(8,128)(2,1)}, u32[]{:S(2)}) copy-start(bf16[1,1024,2048]{2,1,0:T(8,128)(2,1)} %param.10) | copy-start | bytes 12582916
  145.3 20.4 %copy-start.14 = (s32[19]{0:T(128)S(1)}, s32[19]{0:T(128)}, u32[]{:S(2)}) copy-start(s32[19]{0:T(128)} %copy-done.12) | copy-start | bytes 232
  165.6 21.8 %copy-start.3 = (bf16[1,2048,1024]{2,1,0:T(8,128)(2,1)S(1)}, bf16[1,2048,1024]{2,1,0:T(8,128)(2,1)}, u32[]{:S(2)}) copy-start(bf16[1,2048,1024]{2,1,0:T(8,128)(2,1)} %param.12) | copy-start | bytes 12582916
  190.8 0.7 copy-start.10
  191.4 2.2 %collective-permute-start.10 = (bf16[272,256]{1,0:T(8,128)(2,1)S(1)}, bf16[272,256]{1,0:T(8,128)(2,1)S(1)}, u32[]{:S(2)}, u32[]{:S(2)}) collective-permute-start(bf16[272,256]{1,0:T(8,128)(2,1)S(1)} %get-tuple-element.29), channel_id=1, source_target_pairs={{0,16},{16,0},{32,48},{48,32},{1,17},{17,1},{33,49},{49,33},{2,18}... | collective-permute-start | bytes 417800 | tf_op jit(solution)/shard_map/ppermute | solution.py:380
  191.4 6.5 %collective-permute-start.11 = (bf16[272,256]{1,0:T(8,128)(2,1)S(1)}, bf16[272,256]{1,0:T(8,128)(2,1)S(1)}, u32[]{:S(2)}, u32[]{:S(2)}) collective-permute-start(bf16[272,256]{1,0:T(8,128)(2,1)S(1)} %get-tuple-element.30), channel_id=1, source_target_pairs={{0,32},{16,48},{32,0},{48,16},{1,33},{17,49},{33,1},{49,17},{2,34}... | collective-permute-start | bytes 417800 | tf_op jit(solution)/shard_map/ppermute | solution.py:380
  193.4 7.1 %collective-permute-start.12 = (bf16[272,256]{1,0:T(8,128)(2,1)S(1)}, bf16[272,256]{1,0:T(8,128)(2,1)S(1)}, u32[]{:S(2)}, u32[]{:S(2)}) collective-permute-start(bf16[272,256]{1,0:T(8,128)(2,1)S(1)} %get-tuple-element.31), channel_id=1, source_target_pairs={{0,48},{16,32},{32,16},{48,0},{1,49},{17,33},{33,17},{49,1},{2,50}... | collective-permute-start | bytes 417800 | tf_op jit(solution)/shard_map/ppermute | solution.py:380
  193.6 7.0 %copy-start.15 = (bf16[272,256]{1,0:T(8,128)(2,1)}, bf16[272,256]{1,0:T(8,128)(2,1)S(1)}, u32[]{:S(2)}) copy-start(bf16[272,256]{1,0:T(8,128)(2,1)S(1)} %collective-permute-done.10.o1) | copy-start | bytes 417796
  198.0 2.6 %copy-start.16 = (bf16[272,256]{1,0:T(8,128)(2,1)}, bf16[272,256]{1,0:T(8,128)(2,1)S(1)}, u32[]{:S(2)}) copy-start(bf16[272,256]{1,0:T(8,128)(2,1)S(1)} %collective-permute-done.11.o2) | copy-start | bytes 417796
  200.6 0.7 copy-start.17

commit v2 on v1

--- a/solution.py
+++ b/solution.py
@@ -52,21 +52,47 @@
     return high, (values - high.astype(F32)).astype(BF16)
 
 
-def project_kernel(step, scal, x0, x1, x2, x3, gain, wq, wkv, wout, send, scaled, kvs, stats):
-    rows = x0.shape[0]
-    cols = x0.shape[1]
-    data_heads = send.shape[0]
-    i = pl.program_id(0)
+def project_kernel(
+    step, count, scal, *refs
+):
+    pieces, refs = refs[:count], refs[count:]
+    gain, wkv, wq, wout, send, scaled, kvs, wide_buf, head_buf, sems = refs
+    rows, cols = pieces[0].shape[-2:]
+    if count == 4:
+        blocks = [(mask, ref) for mask, ref in enumerate(pieces)]
+    else:
+        blocks = [(n + 2 * k, pieces[n].at[k]) for n in range(2) for k in range(2)]
+    chunks = wide_buf.shape[0]
+    heads = send.shape[0]
+    per = heads // chunks
     active = scal[S_SECTION] == step
 
-    @pl.when(jnp.logical_and(active, i == 0))
+    def wq_copy(i):
+        return pltpu.make_async_copy(
+            wq.at[:, pl.ds(pl.multiple_of(i * per * HD, per * HD), per * HD)],
+            wide_buf.at[i],
+            sems.at[i],
+        )
+
+    def wout_copy(i):
+        return pltpu.make_async_copy(
+            wout.at[pl.ds(pl.multiple_of(i * per * HD, per * HD), per * HD), :],
+            head_buf.at[i],
+            sems.at[i],
+        )
+
+    @pl.when(active)
     def _():
+        for i in range(chunks):
+            wq_copy(i).start()
         total = jnp.zeros((rows, 1), F32)
-        for mask, ref in enumerate((x0, x1, x2, x3)):
+        for mask, ref in blocks:
             place = pl.multiple_of(lax.bitwise_xor(scal[S_TENSOR], mask) * cols, cols)
             wide = ref[...].astype(F32)
             total = total + jnp.sum(wide * wide, axis=1, keepdims=True)
-            scaled[:, pl.ds(place, cols)] = (wide * gain[:, pl.ds(place, cols)]).astype(BF16)
+            scaled[:, pl.ds(place, cols)] = (
+                wide * gain[:, pl.ds(place, cols)].astype(F32)
+            ).astype(BF16)
         eye = diagonal()
         row = lax.broadcasted_iota(jnp.int32, (STATS, HD), 0)
         lines = jnp.zeros((STATS, HD), F32)
@@ -77,71 +103,64 @@
             high, low = two_parts(line)
             lines = jnp.where(row == 2 * b, high.astype(F32), lines)
             lines = jnp.where(row == 2 * b + 1, low.astype(F32), lines)
-        stats[...] = lines.astype(BF16)
+        lines = lines.astype(BF16)
         kvs[...] = jnp.dot(scaled[...], wkv[...], preferred_element_type=F32).astype(BF16)
-
-    @pl.when(active)
-    def _():
-        part = jnp.dot(scaled[...], wq[...], preferred_element_type=F32).astype(BF16)
-        for j in range(data_heads):
-            send[j, :rows, :] = part[:, j * HD : (j + 1) * HD]
-            first = pl.multiple_of((i * data_heads + j) * 16, 16)
+        for j in range(heads):
             for c in range(4):
                 send[j, rows + 16 * c : rows + 16 * c + 16, :] = kvs[
-                    pl.ds(first, 16), c * HD : (c + 1) * HD
+                    16 * j : 16 * j + 16, c * HD : (c + 1) * HD
                 ]
-            send[j, rows + 64 :, :] = stats[...]
+            send[j, rows + 64 :, :] = lines
+
+        @pl.loop(0, chunks)
+        def _(i):
+            wq_copy(i).wait()
+            part = jnp.dot(scaled[...], wide_buf[i], preferred_element_type=F32).astype(BF16)
+            for j in range(per):
+                send[i * per + j, :rows, :] = part[:, j * HD : (j + 1) * HD]
 
     @pl.when(jnp.logical_not(active))
     def _():
-        for j in range(data_heads):
-            head = wout[j * HD : (j + 1) * HD, :]
-            gram = lax.dot_general(
-                head, head, (((1,), (1,)), ((), ())), preferred_element_type=F32
-            )
-            high, low = two_parts(gram)
-            send[j, :HD, :] = high
-            send[j, HD:rows, :] = low
-            send[j, rows:, :] = jnp.zeros((64 + STATS, HD), BF16)
+        for i in range(chunks):
+            wout_copy(i).start()
+
+        @pl.loop(0, chunks)
+        def _(i):
+            wout_copy(i).wait()
+            for j in range(per):
+                head = head_buf[i, j * HD : (j + 1) * HD, :]
+                gram = lax.dot_general(
+                    head, head, (((1,), (1,)), ((), ())), preferred_element_type=F32
+                )
+                high, low = two_parts(gram)
+                send[i * per + j, :HD, :] = high
+                send[i * per + j, HD:rows, :] = low
+                send[i * per + j, rows:, :] = jnp.zeros((64 + STATS, HD), BF16)
 
 
 def project(step, scal, pieces, gain, wq, wkv, wout):
-    rows, cols = pieces[0].shape
+    rows, cols = pieces[0].shape[-2:]
     wide = cols * N_TENSOR
     heads = wq.shape[1] // HD
-    steps = 4
-    per = heads // steps
-    whole = lambda shape: pl.BlockSpec(shape, lambda i, s: (0,) * len(shape))
-
-    def q_block(i, s):
-        return (0, jnp.where(s[S_SECTION] == step, i, 0))
-
-    def out_block(i, s):
-        return (jnp.where(s[S_SECTION] == step, 0, i), 0)
-
-    return pl.pallas_call(
-        functools.partial(project_kernel, step),
+    chunks = 4
+    per = heads // chunks
+    vmem = pl.BlockSpec(memory_space=VMEM)
+    hbm = pl.BlockSpec(memory_space=pltpu.HBM)
+    return pl.pallas_call(
+        functools.partial(project_kernel, step, len(pieces)),
         out_shape=jax.ShapeDtypeStruct((heads, rows + 64 + STATS, HD), BF16),
-        grid_spec=pltpu.PrefetchScalarGridSpec(
-            num_scalar_prefetch=1,
-            grid=(steps,),
-            in_specs=[whole((rows, cols))] * 4
-            + [
-                whole((1, wide)),
-                pl.BlockSpec((wide, per * HD), q_block),
-                whole(wkv.shape),
-                pl.BlockSpec((per * HD, wide), out_block),
-            ],
-            out_specs=pl.BlockSpec((per, rows + 64 + STATS, HD), lambda i, s: (i, 0, 0)),
-            scratch_shapes=[
-                VMEM((rows, wide), BF16),
-                VMEM((rows, wkv.shape[1]), BF16),
-                VMEM((STATS, HD), BF16),
-            ],
-        ),
-        compiler_params=pltpu.CompilerParams(vmem_limit_bytes=24 * 2**20),
+        in_specs=[pl.BlockSpec(memory_space=pltpu.SMEM)] + [vmem] * (len(pieces) + 2) + [hbm] * 2,
+        out_specs=vmem,
+        scratch_shapes=[
+            VMEM((rows, wide), BF16),
+            VMEM((rows, wkv.shape[1]), BF16),
+            VMEM((chunks, wide, per * HD), BF16),
+            VMEM((chunks, per * HD, wide), BF16),
+            pltpu.SemaphoreType.DMA((chunks,)),
+        ],
+        compiler_params=pltpu.CompilerParams(vmem_limit_bytes=20 * 2**20),
         name="project",
-    )(scal, *pieces, gain, wq, wkv, wout)
+    )(scal, *pieces, gain, wkv, wq, wout)
 
 
 def combine_kernel(width, scal, recv, cosine, sine, query, kv, gram, scale):
@@ -202,6 +221,7 @@
         out_shape=jax.ShapeDtypeStruct((N_DP,) + kv.shape[1:], BF16),
         in_specs=[pl.BlockSpec(memory_space=pltpu.SMEM), vmem],
         out_specs=vmem,
+        compiler_params=pltpu.CompilerParams(vmem_limit_bytes=4 * 2**20),
         name="choose",
     )(scal, kv)
 
@@ -273,107 +293,144 @@
     )(scal, query, kv, before, gram0, gram1)
 
 
-def out_kernel(rows, scal, recv, wout, o0, o1, o2, o3, joined):
-    i = pl.program_id(0)
-    heads = recv.shape[0]
-
-    @pl.when(i == 0)
-    def _():
-        for h in range(heads):
-            joined[:, h * HD : (h + 1) * HD] = recv[h, :rows, :]
-
-    part = jnp.dot(joined[...], wout[...], preferred_element_type=F32).astype(BF16)
-    extra = recv.shape[1] > rows
-    if extra:
-        lane = lax.broadcasted_iota(jnp.int32, (1, part.shape[1]), 1)
-        sums = jnp.zeros((1, part.shape[1]), F32)
+def out_kernel(rows, masks, scal, recv, saved, wout, parts, buf, sems):
+    heads, deep, _ = recv.shape
+    cols = parts.shape[2]
+    last = saved is not None
+
+    def copy(n):
+        place = lax.bitwise_xor(scal[S_TENSOR], masks[n]) * cols
+        return pltpu.make_async_copy(
+            wout.at[:, pl.ds(pl.multiple_of(place, cols), cols)], buf.at[n], sems.at[n]
+        )
+
+    for n in range(2):
+        copy(n).start()
+    if last:
+        lane = lax.broadcasted_iota(jnp.int32, (1, cols), 1)
+        sums = jnp.zeros((1, cols), F32)
         for h in range(heads):
             value = recv[h, rows : rows + 1, :].astype(F32) + recv[
                 h, rows + 1 : rows + 2, :
             ].astype(F32)
-            value = jnp.concatenate([value] * (part.shape[1] // HD), axis=1)
+            value = jnp.concatenate([value] * (cols // HD), axis=1)
             sums = sums + jnp.where(lane == scal[S_GROUPS + h], value, 0.0)
         high, low = two_parts(sums)
-        row = lax.broadcasted_iota(jnp.int32, (STATS, part.shape[1]), 0)
+        row = lax.broadcasted_iota(jnp.int32, (STATS, cols), 0)
         lines = jnp.where(
             row == 0, high.astype(F32), jnp.where(row == 1, low.astype(F32), 0.0)
         ).astype(BF16)
-    for mask, ref in enumerate((o0, o1, o2, o3)):
-
-        @pl.when(i == (mask + 3) % 4)
-        def _():
-            ref[:rows] = part
-            if extra:
-                ref[rows:] = lines
-
-
-def project_out(scal, recv, wout, rows):
+        for n in range(2):
+            parts[n, rows:] = lines
+    for n in range(2):
+        copy(n).wait()
+        total = jnp.zeros((rows, cols), F32)
+        for h in range(0, heads, 2):
+            pair = jnp.concatenate([recv[h, :rows, :], recv[h + 1, :rows, :]], axis=1)
+            total = total + jnp.dot(
+                pair, buf[n, h * HD : (h + 2) * HD, :], preferred_element_type=F32
+            )
+        part = total.astype(BF16)
+        if last:
+            part = jnp.where(scal[S_SECTION] == 0, saved[n], part)
+        parts[n, :rows] = part
+
+
+def first_out_kernel(rows, masks, scal, recv, wout, parts, buf, sems):
+    out_kernel(rows, masks, scal, recv, None, wout, parts, buf, sems)
+
+
+def project_out(scal, recv, wout, rows, masks, saved=None):
     heads, deep, _ = recv.shape
-    wide = wout.shape[1]
-    cols = wide // N_TENSOR
-    whole = lambda shape: pl.BlockSpec(shape, lambda i, s: (0,) * len(shape))
-    piece = jax.ShapeDtypeStruct((deep, cols), BF16)
-    return pl.pallas_call(
-        functools.partial(out_kernel, rows),
-        out_shape=(piece,) * 4,
-        grid_spec=pltpu.PrefetchScalarGridSpec(
-            num_scalar_prefetch=1,
-            grid=(N_TENSOR,),
-            in_specs=[
-                whole(recv.shape),
-                pl.BlockSpec(
-                    (heads * HD, cols),
-                    lambda i, s: (0, lax.bitwise_xor(s[S_TENSOR], (i + 1) % 4)),
-                ),
-            ],
-            out_specs=(whole((deep, cols)),) * 4,
-            scratch_shapes=[VMEM((rows, heads * HD), BF16)],
+    cols = wout.shape[1] // N_TENSOR
+    vmem = pl.BlockSpec(memory_space=VMEM)
+    kernel = first_out_kernel if saved is None else out_kernel
+    extra = () if saved is None else (saved,)
+    return pl.pallas_call(
+        functools.partial(kernel, rows, masks),
+        out_shape=jax.ShapeDtypeStruct((2, deep, cols), BF16),
+        in_specs=[pl.BlockSpec(memory_space=pltpu.SMEM), vmem]
+        + [vmem] * len(extra)
+        + [pl.BlockSpec(memory_space=pltpu.HBM)],
+        out_specs=vmem,
+        scratch_shapes=[
+            VMEM((2, heads * HD, cols), BF16),
+            pltpu.SemaphoreType.DMA((2,)),
+        ],
+        compiler_params=pltpu.CompilerParams(vmem_limit_bytes=8 * 2**20),
+        cost_estimate=pl.CostEstimate(
+            flops=4 * rows * heads * HD * cols, bytes_accessed=2**22, transcendentals=0
         ),
-        compiler_params=pltpu.CompilerParams(vmem_limit_bytes=24 * 2**20),
         name="project_out",
-    )(scal, recv, wout)
-
-
-def fresh_kernel(wide, o0, o1, o2, o3, fresh):
-    total = o0[...].astype(F32)
-    for ref in (o1, o2, o3):
-        total = total + ref[...].astype(F32)
-    fresh[...] = (wide[...].astype(F32) + total).astype(BF16)
-
-
-def add_fresh(wide, parts):
-    vmem = pl.BlockSpec(memory_space=VMEM)
-    return pl.pallas_call(
-        fresh_kernel,
-        out_shape=jax.ShapeDtypeStruct(wide.shape, BF16),
-        in_specs=[vmem] * 5,
-        out_specs=vmem,
-        name="add_fresh",
-    )(wide, *parts)
-
-
-def last_kernel(scal, before, wide, o0, o1, o2, o3, out, importance):
-    rows = wide.shape[0]
-    total = o0[...].astype(F32)
-    for ref in (o1, o2, o3):
-        total = total + ref[...].astype(F32)
-    fresh = (wide[...].astype(F32) + total[:rows]).astype(BF16)
-    out[...] = jnp.where(scal[S_SECTION] == 0, before[...], fresh)
+    )(scal, recv, *extra, wout)
+
+
+def pair_kernel(rows, a, b, out):
+    total = a[...].astype(F32) + b[...].astype(F32)
+    out[...] = total.astype(BF16)
+    if out.shape[1] > rows:
+        for n in range(2):
+            high, low = two_parts(total[n, rows : rows + 1] + total[n, rows + 1 : rows + 2])
+            row = lax.broadcasted_iota(jnp.int32, (STATS, out.shape[2]), 0)
+            lines = jnp.where(row == 0, high.astype(F32), 0.0)
+            lines = jnp.where(row == 1, low.astype(F32), lines)
+            out[n, rows:] = lines.astype(BF16)
+
+
+def add_pair(a, b, rows):
+    vmem = pl.BlockSpec(memory_space=VMEM)
+    return pl.pallas_call(
+        functools.partial(pair_kernel, rows),
+        out_shape=jax.ShapeDtypeStruct(a.shape, BF16),
+        in_specs=[vmem] * 2,
+        out_specs=vmem,
+        compiler_params=pltpu.CompilerParams(vmem_limit_bytes=4 * 2**20),
+        name="add_pair",
+    )(a, b)
+
+
+def next_kernel(wide0, wide1, same, other, fresh):
+    fresh[0] = (
+        wide0[...].astype(F32) + (same[0].astype(F32) + other[1].astype(F32))
+    ).astype(BF16)
+    fresh[1] = (
+        wide1[...].astype(F32) + (same[1].astype(F32) + other[0].astype(F32))
+    ).astype(BF16)
+
+
+def add_next(wide0, wide1, same, other):
+    vmem = pl.BlockSpec(memory_space=VMEM)
+    return pl.pallas_call(
+        next_kernel,
+        out_shape=jax.ShapeDtypeStruct(same.shape, BF16),
+        in_specs=[vmem] * 4,
+        out_specs=vmem,
+        compiler_params=pltpu.CompilerParams(vmem_limit_bytes=4 * 2**20),
+        name="add_next",
+    )(wide0, wide1, same, other)
+
+
+def last_kernel(scal, mine, state, here, there, out, importance):
+    rows = mine.shape[0]
+    total = here[0].astype(F32) + there[...].astype(F32)
+    wide = jnp.where(scal[S_SECTION] == 0, mine[...], state[0]).astype(F32)
+    out[...] = (wide + total[:rows]).astype(BF16)
     importance[...] = total[rows : rows + 1, :HD] + total[rows + 1 : rows + 2, :HD]
 
 
-def add_last(scal, before, wide, parts):
+def add_last(scal, mine, state, here, there):
     vmem = pl.BlockSpec(memory_space=VMEM)
     return pl.pallas_call(
         last_kernel,
         out_shape=(
-            jax.ShapeDtypeStruct(wide.shape, BF16),
+            jax.ShapeDtypeStruct(mine.shape, BF16),
             jax.ShapeDtypeStruct((1, HD), F32),
         ),
-        in_specs=[pl.BlockSpec(memory_space=pltpu.SMEM)] + [vmem] * 6,
+        in_specs=[pl.BlockSpec(memory_space=pltpu.SMEM)] + [vmem] * 4,
         out_specs=(vmem, vmem),
+        compiler_params=pltpu.CompilerParams(vmem_limit_bytes=4 * 2**20),
         name="add_last",
-    )(scal, before, wide, *parts)
+    )(scal, mine, state, here, there)
 
 
 def swap(block, mask):
@@ -391,7 +448,7 @@
     data = lax.axis_index("dp")
     rows, cols = hidden_in.shape[0], hidden_in.shape[3]
     width = cols * N_TENSOR * N_DP
-    gain = norm_gain.astype(F32)
+    gain = norm_gain
     wq = w_query[0]
     wkv = w_keyval[0].reshape(wq.shape[0], -1)
     wout = w_out[0]
@@ -415,19 +472,20 @@
     query, kv, gram0 = to_heads(0, pieces)
     att0 = attend(query, kv)
     recv = lax.all_to_all(att0, "dp", 0, 0)
-    parts = project_out(scal, recv, wout, rows)
-    fresh0 = add_fresh(mine, (parts[0],) + tuple(swap(parts[m], m) for m in (1, 2, 3)))
-
-    far = to_next_section(fresh0, 2)
-    near = to_next_section(fresh0, 0)
-    pieces = (near, swap(near, 1), far, swap(far, 1))
+    other0 = project_out(scal, recv, wout, rows, (1, 3))
+    own0 = project_out(scal, recv, wout, rows, (0, 2))
+    here = add_pair(own0, swap(other0, 1), rows)
+    state = add_next(mine, far, to_next_section(here, 0), to_next_section(here, 2))
+
+    beside = swap(state, 1)
+    pieces = (state, beside)
     query, kv, gram1 = to_heads(1, pieces)
     att1 = attend_last(scal, query, kv, att0, gram0, gram1, width)
     recv = lax.all_to_all(att1, "dp", 0, 0)
-    parts = project_out(scal, recv, wout, rows)
-    out, importance = add_last(
-        scal, fresh0, near, (parts[0],) + tuple(swap(parts[m], m) for m in (1, 2, 3))
-    )
+    other1 = project_out(scal, recv, wout, rows, (1, 3), other0)
+    own1 = project_out(scal, recv, wout, rows, (0, 2), own0)
+    here = add_pair(own1, swap(other1, 1), rows)
+    out, importance = add_last(scal, mine, state, here, swap(here[1], 2))
     return out.reshape(1, rows, 1, 1, cols), importance[:, :GROUPS]
 
 

time: 205 us -> 185 us (0.902)
  local copies, waits for them, and re-layouts: 15.1 us -> 5.94 us
  waiting for transfers between devices: 27 us -> 23.7 us
  blocking collectives: 129 us -> 126 us
    unnamed x45 -> x17, local copies, waits for them, and re-layouts: 15 us -> 5.85 us
    ppermute x11 -> x7, waiting for transfers between devices: 19 us -> 10.1 us  [swap(): lax.ppermute(block, 'tensor', [(t, t ^ mask) for t in range(N_TENSOR)])]
    ppermute x2, waiting for transfers between devices: 7.92 us -> 13.6 us  [to_next_section(): return lax.ppermute(block, ('pipe', 'tensor'), route)]
    ppermute x11 -> x7, starting transfers between devices: 5.32 us -> 3.64 us  [swap(): lax.ppermute(block, 'tensor', [(t, t ^ mask) for t in range(N_TENSOR)])]
    pallas_call x6 -> x10, Pallas kernels: 16.4 us -> 16.8 us  [the longest x4 9 us: project_out(): pl.pallas_call(functools.partial(kernel, rows, masks), out_shape=jax.Shap...]
  transfers between devices with their start and end apart: 13 -> 9, of which waited for: 8 -> 4; matrix products, arithmetic and copies ran while one was open for 1% -> 1% of each run, Pallas kernels for 0% -> 2%
where the time goes in v2:
time: 185 us; the launch traced here: 184 us
  blocking collectives  126 us (68%)
  waiting for transfers between devices  23.7 us (13%)
  Pallas kernels  21.3 us (12%)
  starting transfers between devices  6.22 us (3%)
  local copies, waits for them, and re-layouts  5.94 us (3%)
    all_to_all x2, blocking collectives, to_heads(): recv = lax.all_to_all(send, 'dp', 0, 0)  53.3 us
    all_to_all x2, blocking collectives, to_heads(): kv_mine = lax.all_to_all(mine, 'dp', 0, 0).reshape(rows, 2 * HD)  21.6 us
    all_to_all x1, blocking collectives, local(): recv = lax.all_to_all(att1, 'dp', 0, 0)  20.4 us
    all_to_all x1, blocking collectives, local(): recv = lax.all_to_all(att0, 'dp', 0, 0)  19.7 us
    ppermute x2, waiting for transfers between devices, to_next_section(): return lax.ppermute(block, ('pipe', 'tensor'), route)  13.6 us
    all_gather x2, blocking collectives, to_heads(): every = lax.all_gather(kv, 'tensor')  10.9 us
    ppermute x7, waiting for transfers between devices, swap(): lax.ppermute(block, 'tensor', [(t, t ^ mask) for t in range(N_TENSOR)])  10.1 us
    pallas_call x4, Pallas kernels, project_out(): pl.pallas_call(functools.partial(kernel, rows, masks), out_shape=jax.Shap...  9 us
  transfers between devices with their start and end apart: 9, of which 4 were waited for; matrix products, arithmetic and copies ran while one was open for 1% of the time, Pallas kernels for 2%

profile of v2, /device:TPU:4, one launch (start us, length us, event | category | flops | bytes accessed | tf_op | source)
XLA Modules:
  0.0 184.0 jit_solution(4333843817557547183)
XLA Ops:
  0.7 1.3 collective-permute-start
  1.9 0.0 collective-permute-start.1
  1.9 4.2 %collective-permute-done.refs_2_.wide1 = bf16[256,256]{1,0:T(8,128)(2,1)S(1)} collective-permute-done((bf16[256,256]{1,0:T(8,128)(2,1)}, bf16[256,256]{1,0:T(8,128)(2,1)S(1)}, u32[]{:S(2)}, u32[]{:S(2)}) %collective-permute-start) | collective-permute-done | bytes 131104 | tf_op jit(solution)/shard_map/ppermute | solution.py:437
  6.2 0.0 collective-permute-start.2
  6.2 1.4 copy.10
  7.7 0.1 dynamic_slice.3
  7.7 0.1 pad_add_fusion.scal
  7.8 0.0 collective-permute-done.1.refs_1_
  7.8 0.0 collective-permute-done.2.refs_3_
  7.8 0.0 copy-start
  7.9 2.2 %copy-done = bf16[1,2048,1024]{2,1,0:T(8,128)(2,1)S(1)} copy-done((bf16[1,2048,1024]{2,1,0:T(8,128)(2,1)S(1)}, bf16[1,2048,1024]{2,1,0:T(8,128)(2,1)}, u32[]{:S(2)}) %copy-start) | copy-done | bytes 4194328
  10.0 2.2 %copy-done.2 = bf16[1,1024,2048]{2,1,0:T(8,128)(2,1)S(1)} copy-done((bf16[1,1024,2048]{2,1,0:T(8,128)(2,1)S(1)}, bf16[1,1024,2048]{2,1,0:T(8,128)(2,1)}, u32[]{:S(2)}) %copy-start.2) | copy-done | bytes 4194328
  12.2 2.6 %project.2 = bf16[16,336,128]{2,1,0:T(8,128)(2,1)S(1)} custom-call(s32[19]{0:T(128)S(1)} %pad_add_fusion.scal, bf16[256,256]{1,0:T(8,128)(2,1)S(1)} %bitcast.27, bf16[256,256]{1,0:T(8,128)(2,1)S(1)} %collective-permute-done.1.refs_1_, bf16[256,256]{1,0:T(8,128)(2,1)S(1)} %collective-permute-done.refs_2_.wide1, ...), custom_call_target="tpu_custom_call" | custom-call | tf_op jit(solution)/shard_map/project/pallas_call | solution.py:149
  14.9 0.0 copy-start.4
  14.9 0.0 copy-start.5
  14.9 29.4 %all_to_all.30.recv = bf16[16,336,128]{2,1,0:T(8,128)(2,1)S(1)} all-to-all(bf16[16,336,128]{2,1,0:T(8,128)(2,1)S(1)} %project.2), channel_id=1, replica_groups=mesh['pipe'=2,'tensor'=4,'dp'=16] {'dp'}, dimensions={0} | all-to-all | bytes 2752512 | tf_op jit(solution)/shard_map/all_to_all | solution.py:462
  44.3 0.9 combine.2
  45.1 5.2 %all-gather.kv = bf16[8,16,256]{2,1,0:T(8,128)(2,1)S(1)} all-gather(bf16[2,16,256]{2,1,0:T(8,128)(2,1)S(1)} %get-tuple-element.11), channel_id=2, replica_groups=mesh['pipe'=2,'tensor'=4,'dp'=16] {'tensor'}, dimensions={0}, use_global_device_ids=true | all-gather | bytes 81920 | tf_op jit(solution)/shard_map/all_gather | solution.py:464
  50.4 0.6 choose.2
  50.9 10.8 %all_to_all.31 = bf16[16,16,256]{2,1,0:T(8,128)(2,1)S(1)} all-to-all(bf16[16,16,256]{2,1,0:T(8,128)(2,1)S(1)} %choose.2), channel_id=1, replica_groups=mesh['pipe'=2,'tensor'=4,'dp'=16] {'dp'}, dimensions={0} | all-to-all | bytes 262144 | tf_op jit(solution)/shard_map/all_to_all | solution.py:466
  61.7 0.5 attend.1.before
  62.2 19.7 %all_to_all.32.recv = bf16[16,256,128]{2,1,0:T(8,128)(2,1)S(1)} all-to-all(bf16[16,256,128]{2,1,0:T(8,128)(2,1)S(1)} %attend.1.before), channel_id=1, replica_groups=mesh['pipe'=2,'tensor'=4,'dp'=16] {'dp'}, dimensions={0} | all-to-all | bytes 2097152 | tf_op jit(solution)/shard_map/all_to_all | solution.py:474
  81.8 2.2 %project_out.5.saved = bf16[2,256,256]{2,1,0:T(8,128)(2,1)S(1)} custom-call(s32[19]{0:T(128)S(1)} %pad_add_fusion.scal, bf16[16,256,128]{2,1,0:T(8,128)(2,1)S(1)} %all_to_all.32.recv, bf16[2048,1024]{1,0:T(8,128)(2,1)S(1)} %bitcast.16), custom_call_target="tpu_custom_call" | custom-call | flops 536870912 | bytes 4194304 | tf_op jit(solution)/shard_map/project_out/pallas_call | solution.py:349
  84.1 0.1 collective-permute-start.3
  84.2 0.0 copy-start.1
  84.2 2.2 %project_out.4.a.saved = bf16[2,256,256]{2,1,0:T(8,128)(2,1)S(1)} custom-call(s32[19]{0:T(128)S(1)} %pad_add_fusion.scal, bf16[16,256,128]{2,1,0:T(8,128)(2,1)S(1)} %all_to_all.32.recv, bf16[2048,1024]{1,0:T(8,128)(2,1)S(1)} %bitcast.17), custom_call_target="tpu_custom_call" | custom-call | flops 536870912 | bytes 4194304 | tf_op jit(solution)/shard_map/project_out/pallas_call | solution.py:349
  86.4 0.1 add_pair.2
  86.5 1.3 collective-permute-start.5
  87.8 1.3 collective-permute-start.4
  89.1 13.6 %collective-permute-done.5.other = bf16[2,256,256]{2,1,0:T(8,128)(2,1)S(1)} collective-permute-done((bf16[2,256,256]{2,1,0:T(8,128)(2,1)S(1)}, bf16[2,256,256]{2,1,0:T(8,128)(2,1)S(1)}, u32[]{:S(2)}, u32[]{:S(2)}) %collective-permute-start.5) | collective-permute-done | bytes 262176 | tf_op jit(solution)/shard_map/ppermute | solution.py:442
  102.7 0.1 add_next.1.refs_0_.state
  102.8 0.1 collective-permute-start.6
  102.9 1.5 collective-permute-done.6.refs_1_
  104.4 3.6 %project.3 = bf16[16,336,128]{2,1,0:T(8,128)(2,1)S(1)} custom-call(s32[19]{0:T(128)S(1)} %pad_add_fusion.scal, bf16[2,256,256]{2,1,0:T(8,128)(2,1)S(1)} %add_next.1.refs_0_.state, bf16[2,256,256]{2,1,0:T(8,128)(2,1)S(1)} %collective-permute-done.6.refs_1_, bf16[1,1024]{1,0:T(2,128)(2,1)S(1)} %copy-done.6, bf16[1024,512]{1,0:T(8,128)(2,1)S(1)} %bitcast.24, ...), custom_call_target="tpu_custom_call" | custom-call | tf_op jit(solution)/shard_map/project/pallas_call | solution.py:149
  108.1 23.9 %all_to_all.33.recv = bf16[16,336,128]{2,1,0:T(8,128)(2,1)S(1)} all-to-all(bf16[16,336,128]{2,1,0:T(8,128)(2,1)S(1)} %project.3), channel_id=1, replica_groups=mesh['pipe'=2,'tensor'=4,'dp'=16] {'dp'}, dimensions={0} | all-to-all | bytes 2752512 | tf_op jit(solution)/shard_map/all_to_all | solution.py:462
  132.0 0.9 combine.3
  132.9 5.6 %all-gather.1.kv = bf16[8,16,256]{2,1,0:T(8,128)(2,1)S(1)} all-gather(bf16[2,16,256]{2,1,0:T(8,128)(2,1)S(1)} %get-tuple-element.13), channel_id=3, replica_groups=mesh['pipe'=2,'tensor'=4,'dp'=16] {'tensor'}, dimensions={0}, use_global_device_ids=true | all-gather | bytes 81920 | tf_op jit(solution)/shard_map/all_gather | solution.py:464
  138.5 0.6 choose.3
  139.1 10.8 %all_to_all.34 = bf16[16,16,256]{2,1,0:T(8,128)(2,1)S(1)} all-to-all(bf16[16,16,256]{2,1,0:T(8,128)(2,1)S(1)} %choose.3), channel_id=1, replica_groups=mesh['pipe'=2,'tensor'=4,'dp'=16] {'dp'}, dimensions={0} | all-to-all | bytes 262144 | tf_op jit(solution)/shard_map/all_to_all | solution.py:466
  149.9 1.3 attend_last.1
  151.1 20.4 %all_to_all.35.recv = bf16[16,272,128]{2,1,0:T(8,128)(2,1)S(1)} all-to-all(bf16[16,272,128]{2,1,0:T(8,128)(2,1)S(1)} %attend_last.1), channel_id=1, replica_groups=mesh['pipe'=2,'tensor'=4,'dp'=16] {'dp'}, dimensions={0} | all-to-all | bytes 2228224 | tf_op jit(solution)/shard_map/all_to_all | solution.py:484
  171.6 2.3 %project_out.7 = bf16[2,272,256]{2,1,0:T(8,128)(2,1)S(1)} custom-call(s32[19]{0:T(128)S(1)} %pad_add_fusion.scal, bf16[16,272,128]{2,1,0:T(8,128)(2,1)S(1)} %all_to_all.35.recv, bf16[2,256,256]{2,1,0:T(8,128)(2,1)S(1)} %project_out.5.saved, bf16[2048,1024]{1,0:T(8,128)(2,1)S(1)} %bitcast.19), custom_call_target="tpu_custom_call" | custom-call | flops 536870912 | bytes 4194304 | tf_op jit(solution)/shard_map/project_out/pallas_call | solution.py:349
  173.8 0.1 collective-permute-start.7
  173.9 2.3 %project_out.6.a = bf16[2,272,256]{2,1,0:T(8,128)(2,1)S(1)} custom-call(s32[19]{0:T(128)S(1)} %pad_add_fusion.scal, bf16[16,272,128]{2,1,0:T(8,128)(2,1)S(1)} %all_to_all.35.recv, bf16[2,256,256]{2,1,0:T(8,128)(2,1)S(1)} %project_out.4.a.saved, bf16[2048,1024]{1,0:T(8,128)(2,1)S(1)} %bitcast.20), custom_call_target="tpu_custom_call" | custom-call | flops 536870912 | bytes 4194304 | tf_op jit(solution)/shard_map/project_out/pallas_call | solution.py:349
  176.2 0.1 add_pair.3.here
  176.3 2.1 %collective-permute-start.8 = (bf16[272,256]{1,0:T(8,128)(2,1)S(1)}, bf16[272,256]{1,0:T(8,128)(2,1)S(1)}, u32[]{:S(2)}, u32[]{:S(2)}) collective-permute-start(bf16[272,256]{1,0:T(8,128)(2,1)S(1)} %slice_bitcast_fusion), channel_id=1, source_target_pairs={{0,32},{16,48},{32,0},{48,16},{1,33},{17,49},{33,1},{49,17},{2,34}... | collective-permute-start | bytes 417800 | tf_op jit(solution)/shard_map/ppermute | solution.py:437
  178.4 4.3 %collective-permute-done.8.there = bf16[272,256]{1,0:T(8,128)(2,1)S(1)} collective-permute-done((bf16[272,256]{1,0:T(8,128)(2,1)S(1)}, bf16[272,256]{1,0:T(8,128)(2,1)S(1)}, u32[]{:S(2)}, u32[]{:S(2)}) %collective-permute-start.8) | collective-permute-done | bytes 139296 | tf_op jit(solution)/shard_map/ppermute | solution.py:437
  182.7 1.3 add_last.1
  (14 shorter events, 0.0 us)
Async XLA Ops:
  0.6 7.2 %copy-start.3 = (bf16[256,1,1,256]{3,0,2,1:T(8,128)(2,1)S(1)}, bf16[256,1,1,256]{3,0,2,1:T(8,128)(2,1)}, u32[]{:S(2)}) copy-start(bf16[256,1,1,256]{3,0,2,1:T(8,128)(2,1)} %param.8) | copy-start | bytes 393220
  0.6 7.0 %copy-start.7 = (s32[64]{0:T(128)S(1)}, s32[64]{0:T(128)}, u32[]{:S(2)}) copy-start(s32[64]{0:T(128)} %param.13) | copy-start | bytes 772
  0.7 7.2 %copy-start.6 = (bf16[1,1024]{1,0:T(2,128)(2,1)S(1)}, bf16[1,1024]{1,0:T(2,128)(2,1)}, u32[]{:S(2)}) copy-start(bf16[1,1024]{1,0:T(2,128)(2,1)} %refs_2_.1) | copy-start | bytes 6148
  0.7 5.5 %collective-permute-start = (bf16[256,256]{1,0:T(8,128)(2,1)}, bf16[256,256]{1,0:T(8,128)(2,1)S(1)}, u32[]{:S(2)}, u32[]{:S(2)}) collective-permute-start(bf16[256,256]{1,0:T(8,128)(2,1)} %bitcast.25), channel_id=1, source_target_pairs={{0,32},{16,48},{32,0},{48,16},{1,33},{17,49},{33,1},{49,17},{2,34}... | collective-permute-start | bytes 393224 | tf_op jit(solution)/shard_map/ppermute | solution.py:437
  1.9 5.9 %collective-permute-start.1 = (bf16[256,256]{1,0:T(8,128)(2,1)}, bf16[256,256]{1,0:T(8,128)(2,1)S(1)}, u32[]{:S(2)}, u32[]{:S(2)}) collective-permute-start(bf16[256,256]{1,0:T(8,128)(2,1)} %bitcast.26), channel_id=1, source_target_pairs={{0,16},{16,0},{32,48},{48,32},{1,17},{17,1},{33,49},{49,33},{2,18}... | collective-permute-start | bytes 393224 | tf_op jit(solution)/shard_map/ppermute | solution.py:437
  6.2 1.6 collective-permute-start.2
  7.8 2.2 %copy-start = (bf16[1,2048,1024]{2,1,0:T(8,128)(2,1)S(1)}, bf16[1,2048,1024]{2,1,0:T(8,128)(2,1)}, u32[]{:S(2)}) copy-start(bf16[1,2048,1024]{2,1,0:T(8,128)(2,1)} %param.12) | copy-start | bytes 12582916
  10.0 2.2 %copy-start.2 = (bf16[1,1024,2048]{2,1,0:T(8,128)(2,1)S(1)}, bf16[1,1024,2048]{2,1,0:T(8,128)(2,1)}, u32[]{:S(2)}) copy-start(bf16[1,1024,2048]{2,1,0:T(8,128)(2,1)} %param.10) | copy-start | bytes 12582916
  14.9 29.4 %copy-start.4 = (f32[256,128]{1,0:T(8,128)S(1)}, f32[256,128]{1,0:T(8,128)}, u32[]{:S(2)}) copy-start(f32[256,128]{1,0:T(8,128)} %constant.26.clone.sine) | copy-start | bytes 393220
  14.9 29.4 %copy-start.5 = (f32[256,128]{1,0:T(8,128)S(1)}, f32[256,128]{1,0:T(8,128)}, u32[]{:S(2)}) copy-start(f32[256,128]{1,0:T(8,128)} %constant.25.clone.cosine) | copy-start | bytes 393220
  84.1 2.4 %collective-permute-start.3 = (bf16[2,256,256]{2,1,0:T(8,128)(2,1)S(1)}, bf16[2,256,256]{2,1,0:T(8,128)(2,1)S(1)}, u32[]{:S(2)}, u32[]{:S(2)}) collective-permute-start(bf16[2,256,256]{2,1,0:T(8,128)(2,1)S(1)} %project_out.5.saved), channel_id=1, source_target_pairs={{0,16},{16,0},{32,48},{48,32},{1,17},{17,1},{33,49},{49,33},{2,18}... | collective-permute-start | bytes 786440 | tf_op jit(solution)/shard_map/ppermute | solution.py:437
  84.2 20.3 %copy-start.1 = (bf16[1,2048,1024]{2,1,0:T(8,128)(2,1)S(1)}, bf16[1,2048,1024]{2,1,0:T(8,128)(2,1)}, u32[]{:S(2)}) copy-start(bf16[1,2048,1024]{2,1,0:T(8,128)(2,1)} %param.12) | copy-start | bytes 12582916
  86.5 16.2 %collective-permute-start.5 = (bf16[2,256,256]{2,1,0:T(8,128)(2,1)S(1)}, bf16[2,256,256]{2,1,0:T(8,128)(2,1)S(1)}, u32[]{:S(2)}, u32[]{:S(2)}) collective-permute-start(bf16[2,256,256]{2,1,0:T(8,128)(2,1)S(1)} %add_pair.2), channel_id=1, source_target_pairs={{0,96},{16,112},{32,64},{48,80},{1,97},{17,113},{33,65},{49,81},{2... | collective-permute-start | bytes 786440 | tf_op jit(solution)/shard_map/ppermute | solution.py:442
  87.8 14.9 %collective-permute-start.4 = (bf16[2,256,256]{2,1,0:T(8,128)(2,1)S(1)}, bf16[2,256,256]{2,1,0:T(8,128)(2,1)S(1)}, u32[]{:S(2)}, u32[]{:S(2)}) collective-permute-start(bf16[2,256,256]{2,1,0:T(8,128)(2,1)S(1)} %add_pair.2), channel_id=1, source_target_pairs={{0,64},{16,80},{32,96},{48,112},{1,65},{17,81},{33,97},{49,113},{2... | collective-permute-start | bytes 786440 | tf_op jit(solution)/shard_map/ppermute | solution.py:442
  102.8 1.6 collective-permute-start.6
  173.8 2.4 %collective-permute-start.7 = (bf16[2,272,256]{2,1,0:T(8,128)(2,1)S(1)}, bf16[2,272,256]{2,1,0:T(8,128)(2,1)S(1)}, u32[]{:S(2)}, u32[]{:S(2)}) collective-permute-start(bf16[2,272,256]{2,1,0:T(8,128)(2,1)S(1)} %project_out.7), channel_id=1, source_target_pairs={{0,16},{16,0},{32,48},{48,32},{1,17},{17,1},{33,49},{49,33},{2,18}... | collective-permute-start | bytes 835592 | tf_op jit(solution)/shard_map/ppermute | solution.py:437
  176.3 6.4 %collective-permute-start.8 = (bf16[272,256]{1,0:T(8,128)(2,1)S(1)}, bf16[272,256]{1,0:T(8,128)(2,1)S(1)}, u32[]{:S(2)}, u32[]{:S(2)}) collective-permute-start(bf16[272,256]{1,0:T(8,128)(2,1)S(1)} %slice_bitcast_fusion), channel_id=1, source_target_pairs={{0,32},{16,48},{32,0},{48,16},{1,33},{17,49},{33,1},{49,17},{2,34}... | collective-permute-start | bytes 417800 | tf_op jit(solution)/shard_map/ppermute | solution.py:437

commit v3 on v2

v3 whole, which is shorter than its diff:
```python
import functools
import math

import jax
import jax.numpy as jnp
import numpy as np
from jax import lax
from jax.experimental import pallas as pl
from jax.experimental.pallas import tpu as pltpu
from jax.sharding import PartitionSpec as P

HD = 128
GROUPS = 8
N_TENSOR = 4
N_DP = 16
THETA = 500000.0
EPS_NORM = 1e-05
EPS_RMS = 1e-06
STATS = 16

BF16 = jnp.bfloat16
F32 = jnp.float32
VMEM = pltpu.VMEM

S_SECTION, S_TENSOR, S_DATA = 0, 1, 2


def rotary_tables(rows):
    positions = np.arange(rows, dtype=np.float64)[:, None]
    lanes = np.arange(HD)
    angle = positions * THETA ** (-2.0 * (lanes // 2) / HD)[None, :]
    sign = np.where(lanes % 2 == 0, -1.0, 1.0)[None, :]
    return np.cos(angle).astype(np.float32), (np.sin(angle) * sign).astype(np.float32)


def rotated(values, cosine, sine):
    lanes = lax.broadcasted_iota(jnp.int32, values.shape, 1)
    swapped = jnp.where(
        lanes % 2 == 0, pltpu.roll(values, HD - 1, 1), pltpu.roll(values, 1, 1)
    )
    return values * cosine + swapped * sine


def diagonal():
    return lax.broadcasted_iota(jnp.int32, (HD, HD), 0) == lax.broadcasted_iota(
        jnp.int32, (HD, HD), 1
    )


def two_parts(values):
    high = values.astype(BF16)
    return high, (values - high.astype(F32)).astype(BF16)


def load_kernel(scal, wq, wkv, wout, held, wkv_out, raw, sems):
    chunks = sems.shape[0] - 1
    deep, cols = wq.shape[0], wq.shape[1] // chunks
    halves = wout.shape[1] // cols
    long = wout.shape[0]
    first = pltpu.make_async_copy(wkv, raw, sems.at[chunks])
    first.start()

    def wq_copy(i):
        return pltpu.make_async_copy(
            wq.at[:, i * cols : (i + 1) * cols],
            held.at[i * deep : (i + 1) * deep, :],
            sems.at[i],
        )

    def wout_copy(i):
        return pltpu.make_async_copy(
            wout.at[:, i * cols : (i + 1) * cols],
            held.at[i * long : (i + 1) * long, :],
            sems.at[i],
        )

    @pl.when(scal[S_SECTION] == 0)
    def _():
        for i in range(chunks):
            wq_copy(i).start()

    @pl.when(scal[S_SECTION] != 0)
    def _():
        for i in range(halves):
            wout_copy(i).start()

    first.wait()
    width = wkv.shape[2]
    for g in range(wkv.shape[1]):
        wkv_out[:, g * width : (g + 1) * width] = raw[:, g, :]

    @pl.when(scal[S_SECTION] == 0)
    def _():
        for i in range(chunks):
            wq_copy(i).wait()

    @pl.when(scal[S_SECTION] != 0)
    def _():
        for i in range(halves):
            wout_copy(i).wait()


def load(scal, wq, wkv, wout):
    deep, cols = wq.shape
    chunks = 4
    hbm = pl.BlockSpec(memory_space=pltpu.HBM)
    vmem = pl.BlockSpec(memory_space=VMEM)
    return pl.pallas_call(
        load_kernel,
        out_shape=(
            jax.ShapeDtypeStruct((chunks * deep, cols // chunks), BF16),
            jax.ShapeDtypeStruct((deep, wkv.shape[1] * wkv.shape[2]), BF16),
        ),
        in_specs=[pl.BlockSpec(memory_space=pltpu.SMEM)] + [hbm] * 3,
        out_specs=(vmem,) * 2,
        scratch_shapes=[VMEM(wkv.shape, BF16), pltpu.SemaphoreType.DMA((chunks + 1,))],
        compiler_params=pltpu.CompilerParams(vmem_limit_bytes=40 * 2**20),
        cost_estimate=pl.CostEstimate(flops=10**9, bytes_accessed=1, transcendentals=0),
        name="load",
    )(scal, wq, wkv, wout)


def project_kernel(step, count, scal, *refs):
    pieces, refs = refs[:count], refs[count:]
    gain, wkv, *weights, send, scaled = refs
    rows, cols = pieces[0].shape[-2:]
    deep = cols * N_TENSOR
    per = 4
    heads = N_DP
    pitch = rows + 64 + STATS
    tensor = scal[S_TENSOR]
    if count == 4:
        by_mask = [ref[...] for ref in pieces]
    else:
        by_mask = [pieces[mask % 2][mask // 2] for mask in range(4)]

    def block(place):
        low = [jnp.where(tensor % 2 == place % 2, by_mask[n], by_mask[n + 1]) for n in (0, 2)]
        return jnp.where(tensor // 2 == place // 2, low[0], low[1])

    active = scal[S_SECTION] == step

    def query_chunk(i):
        if len(weights) == 1:
            return weights[0][i * deep : (i + 1) * deep, :]
        return weights[0][:, i * per * HD : (i + 1) * per * HD]

    def two_heads(i):
        at = pl.ds(pl.multiple_of(i * 2 * HD, 2 * HD), 2 * HD)
        if len(weights) == 1:
            long = heads * HD
            return [weights[0].at[n * long : (n + 1) * long, :][at, :] for n in range(2)]
        return [weights[1][at, :]]

    @pl.when(active)
    def _():
        total = jnp.zeros((rows, 1), F32)
        for place in range(N_TENSOR):
            at = slice(place * cols, (place + 1) * cols)
            wide = block(place).astype(F32)
            total = total + jnp.sum(wide * wide, axis=1, keepdims=True)
            scaled[:, at] = (wide * gain[:, at].astype(F32)).astype(BF16)
        eye = diagonal()
        row = lax.broadcasted_iota(jnp.int32, (STATS, HD), 0)
        lines = jnp.zeros((STATS, HD), F32)
        for b in range(rows // HD):
            line = jnp.sum(
                jnp.where(eye, total[b * HD : (b + 1) * HD], 0.0), axis=0, keepdims=True
            )
            high, low = two_parts(line)
            lines = jnp.where(row == 2 * b, high.astype(F32), lines)
            lines = jnp.where(row == 2 * b + 1, low.astype(F32), lines)
        lines = lines.astype(BF16)
        part = jnp.dot(scaled[...], wkv[...], preferred_element_type=F32).astype(BF16)
        for j in range(heads):
            first = j * pitch + rows
            for c in range(4):
                send[first + 16 * c : first + 16 * c + 16, :] = part[
                    16 * j : 16 * j + 16, c * HD : (c + 1) * HD
                ]
            send[first + 64 : first + 64 + STATS, :] = lines
        for i in range(heads // per):
            part = jnp.dot(scaled[...], query_chunk(i), preferred_element_type=F32).astype(BF16)
            for j in range(per):
                first = (i * per + j) * pitch
                send[first : first + rows, :] = part[:, j * HD : (j + 1) * HD]

    @pl.when(jnp.logical_not(active))
    def _():
        @pl.loop(0, heads // 2)
        def _(i):
            both = jnp.zeros((2 * HD, 2 * HD), F32)
            for pair in two_heads(i):
                both = both + lax.dot_general(
                    pair, pair, (((1,), (1,)), ((), ())), preferred_element_type=F32
                )
            for n in range(2):
                high, low = two_parts(both[n * HD : (n + 1) * HD, n * HD : (n + 1) * HD])
                first = pl.multiple_of((2 * i + n) * pitch, 16)
                send[pl.ds(first, HD), :] = high
                send[pl.ds(first + HD, HD), :] = low
                send[pl.ds(first + rows, 64 + STATS), :] = jnp.zeros((64 + STATS, HD), BF16)


def project(step, scal, pieces, gain, wkv, *weights):
    rows, cols = pieces[0].shape[-2:]
    wide = cols * N_TENSOR
    pitch = rows + 64 + STATS
    vmem = pl.BlockSpec(memory_space=VMEM)
    send = pl.pallas_call(
        functools.partial(project_kernel, step, len(pieces)),
        out_shape=jax.ShapeDtypeStruct((N_DP * pitch, HD), BF16),
        in_specs=[pl.BlockSpec(memory_space=pltpu.SMEM)]
        + [vmem] * (len(pieces) + 2 + len(weights)),
        out_specs=vmem,
        scratch_shapes=[VMEM((rows, wide), BF16)],
        compiler_params=pltpu.CompilerParams(vmem_limit_bytes=8 * 2**20),
        name="project",
    )(scal, *pieces, gain, wkv, *weights)
    return send.reshape(N_DP, pitch, HD)


def combine_kernel(step, width, scal, recv, cosine, sine, query, kv, gram, scale):
    rows = cosine.shape[0]
    active = scal[S_SECTION] == step

    def total(first, size):
        at = slice(first, first + size)
        value = recv[0, at, :].astype(F32)
        for s in range(1, N_DP):
            value = value + recv[s, at, :].astype(F32)
        return value

    @pl.when(active)
    def _():
        raw = total(0, rows)
        tail = total(rows, 64 + STATS)
        eye = diagonal()
        for b in range(rows // HD):
            line = tail[64 + 2 * b : 65 + 2 * b, :] + tail[65 + 2 * b : 66 + 2 * b, :]
            column = jnp.sum(jnp.where(eye, line, 0.0), axis=1, keepdims=True)
            factor = lax.rsqrt(column / width + EPS_NORM)
            scale[b * HD : (b + 1) * HD, :] = jnp.broadcast_to(factor, (HD, HD))
        query[...] = rotated(raw * scale[...], cosine[...], sine[...]).astype(BF16)
        first = pl.multiple_of(scal[S_DATA] * 16, 16)
        here = scale[pl.ds(first, 16), :]
        cos_here = cosine[pl.ds(first, 16), :]
        sin_here = sine[pl.ds(first, 16), :]
        for g in range(2):
            keys = tail[32 * g : 32 * g + 16] * here
            vals = tail[32 * g + 16 : 32 * g + 32] * here
            kv[g, :, :HD] = rotated(keys, cos_here, sin_here).astype(BF16)
            kv[g, :, HD:] = vals.astype(BF16)
        gram[...] = jnp.zeros_like(gram)

    @pl.when(jnp.logical_not(active))
    def _():
        gram[...] = total(0, HD) + total(HD, HD)
        query[...] = jnp.zeros_like(query)
        kv[...] = jnp.zeros_like(kv)


def combine(step, scal, recv, cosine, sine, width):
    rows = cosine.shape[0]
    smem = pl.BlockSpec(memory_space=pltpu.SMEM)
    vmem = pl.BlockSpec(memory_space=VMEM)
    return pl.pallas_call(
        functools.partial(combine_kernel, step, float(width)),
        out_shape=(
            jax.ShapeDtypeStruct((rows, HD), BF16),
            jax.ShapeDtypeStruct((2, 16, 2 * HD), BF16),
            jax.ShapeDtypeStruct((HD, HD), F32),
        ),
        in_specs=[smem, vmem, vmem, vmem],
        out_specs=(vmem, vmem, vmem),
        scratch_shapes=[VMEM((rows, HD), F32)],
        compiler_params=pltpu.CompilerParams(vmem_limit_bytes=8 * 2**20),
        name="combine",
    )(scal, recv, cosine, sine)


def choose_kernel(scal, group, kv, send):
    for j in range(N_DP):
        send[j] = kv[group[scal[S_TENSOR] * N_DP + j]]


def choose(scal, group, kv):
    vmem = pl.BlockSpec(memory_space=VMEM)
    return pl.pallas_call(
        choose_kernel,
        out_shape=jax.ShapeDtypeStruct((N_DP,) + kv.shape[1:], BF16),
        in_specs=[pl.BlockSpec(memory_space=pltpu.SMEM)] * 2 + [vmem],
        out_specs=vmem,
        compiler_params=pltpu.CompilerParams(vmem_limit_bytes=4 * 2**20),
        name="choose",
    )(scal, group, kv)


def attended(query, kv):
    rows = query.shape[0]
    scores = lax.dot_general(
        query, kv[:, :HD], (((1,), (1,)), ((), ())), preferred_element_type=F32
    )
    allowed = lax.broadcasted_iota(jnp.int32, (rows, rows), 0) >= lax.broadcasted_iota(
        jnp.int32, (rows, rows), 1
    )
    expo = jnp.where(allowed, jnp.exp(scores * (1.0 / math.sqrt(HD))), 0.0)
    weights = (expo / jnp.sum(expo, axis=1, keepdims=True)).astype(BF16)
    return jnp.dot(weights, kv[:, HD:], preferred_element_type=F32).astype(BF16)


def attend_kernel(scal, query, kv, send):
    active = scal[S_SECTION] == 0

    @pl.when(active)
    def _():
        result = attended(query[...], kv[...])
        for j in range(N_DP):
            send[j] = result

    @pl.when(jnp.logical_not(active))
    def _():
        send[...] = jnp.zeros_like(send)


def attend(scal, query, kv):
    rows = query.shape[0]
    vmem = pl.BlockSpec(memory_space=VMEM)
    return pl.pallas_call(
        attend_kernel,
        out_shape=jax.ShapeDtypeStruct((N_DP, rows, HD), BF16),
        in_specs=[pl.BlockSpec(memory_space=pltpu.SMEM), vmem, vmem],
        out_specs=vmem,
        compiler_params=pltpu.CompilerParams(vmem_limit_bytes=8 * 2**20),
        name="attend",
    )(scal, query, kv)


def attend_last_kernel(width, scal, query, kv, before, gram0, gram1, send):
    rows = query.shape[0]
    result = attended(query[...], kv[...])
    first_section = scal[S_SECTION] == 0
    mine = jnp.where(first_section, before[0], result)
    gram = jnp.where(first_section, gram1[...], gram0[...])
    high, low = two_parts(gram)
    image = jnp.dot(mine, high, preferred_element_type=F32) + jnp.dot(
        mine, low, preferred_element_type=F32
    )
    squares = jnp.sum(image * mine.astype(F32), axis=1, keepdims=True)
    spread = jnp.sqrt(jnp.maximum(squares / width, 0.0) + EPS_RMS)
    mean = jnp.sum(spread, axis=0, keepdims=True) / rows
    high, low = two_parts(mean)
    row = lax.broadcasted_iota(jnp.int32, (STATS, HD), 0)
    lines = jnp.where(row == 0, high.astype(F32), jnp.where(row == 1, low.astype(F32), 0.0))
    lines = lines.astype(BF16)
    for j in range(N_DP):
        send[j, :rows] = result
        send[j, rows:] = lines


def attend_last(scal, query, kv, before, gram0, gram1, width):
    rows = query.shape[0]
    vmem = pl.BlockSpec(memory_space=VMEM)
    return pl.pallas_call(
        functools.partial(attend_last_kernel, float(width)),
        out_shape=jax.ShapeDtypeStruct((N_DP, rows + STATS, HD), BF16),
        in_specs=[pl.BlockSpec(memory_space=pltpu.SMEM)] + [vmem] * 5,
        out_specs=vmem,
        compiler_params=pltpu.CompilerParams(vmem_limit_bytes=8 * 2**20),
        name="attend_last",
    )(scal, query, kv, before, gram0, gram1)


def out_kernel(rows, masks, scal, group, recv, saved, wout, parts):
    heads = recv.shape[0]
    cols = parts.shape[2]
    last = saved is not None
    if last:
        lane = lax.broadcasted_iota(jnp.int32, (1, cols), 1)
        sums = jnp.zeros((1, cols), F32)
        for h in range(heads):
            value = recv[h, rows : rows + 1, :].astype(F32) + recv[
                h, rows + 1 : rows + 2, :
            ].astype(F32)
            value = jnp.concatenate([value] * (cols // HD), axis=1)
            sums = sums + jnp.where(lane == group[scal[S_TENSOR] * heads + h], value, 0.0)
        high, low = two_parts(sums)
        row = lax.broadcasted_iota(jnp.int32, (STATS, cols), 0)
        lines = jnp.where(
            row == 0, high.astype(F32), jnp.where(row == 1, low.astype(F32), 0.0)
        ).astype(BF16)
        for n in range(2):
            parts[n, rows:] = lines
    active = (scal[S_SECTION] != 0) if last else (scal[S_SECTION] == 0)
    for parity in range(2):
        mine = (scal[S_TENSOR] + masks[0] + parity) % 2 == 0

        @pl.when(jnp.logical_and(active, mine))
        def _():
            for place in (parity, parity + 2):
                total = None
                for h in range(0, heads, 2):
                    pair = jnp.concatenate([recv[h, :rows, :], recv[h + 1, :rows, :]], axis=1)
                    one = jnp.dot(
                        pair,
                        wout[h * HD : (h + 2) * HD, place * cols : (place + 1) * cols],
                        preferred_element_type=F32,
                    )
                    total = one if total is None else total + one
                n = lax.bitwise_xor(scal[S_TENSOR], place) // 2
                parts[n, :rows] = total.astype(BF16)

    @pl.when(jnp.logical_not(active))
    def _():
        for n in range(2):
            parts[n, :rows] = saved[n] if last else jnp.zeros((rows, cols), BF16)


def first_out_kernel(rows, masks, scal, group, recv, wout, parts):
    out_kernel(rows, masks, scal, group, recv, None, wout, parts)


def project_out(scal, group, recv, wout, rows, masks, saved=None):
    heads, deep, _ = recv.shape
    cols = wout.shape[1] // N_TENSOR
    kernel = first_out_kernel if saved is None else out_kernel
    extra = () if saved is None else (saved,)
    return pl.pallas_call(
        functools.partial(kernel, rows, masks),
        out_shape=jax.ShapeDtypeStruct((2, deep, cols), BF16),
        in_specs=[pl.BlockSpec(memory_space=pltpu.SMEM)] * 2
        + [pl.BlockSpec(memory_space=VMEM)] * (2 + len(extra)),
        out_specs=pl.BlockSpec(memory_space=VMEM),
        compiler_params=pltpu.CompilerParams(vmem_limit_bytes=6 * 2**20),
        cost_estimate=pl.CostEstimate(
            flops=4 * rows * heads * HD * cols, bytes_accessed=2**22, transcendentals=0
        ),
        name="project_out",
    )(scal, group, recv, *extra, wout)


def pair_kernel(rows, a, b, out):
    total = a[...].astype(F32) + b[...].astype(F32)
    out[...] = total.astype(BF16)
    if out.shape[1] > rows:
        for n in range(2):
            high, low = two_parts(total[n, rows : rows + 1] + total[n, rows + 1 : rows + 2])
            row = lax.broadcasted_iota(jnp.int32, (STATS, out.shape[2]), 0)
            lines = jnp.where(row == 0, high.astype(F32), 0.0)
            lines = jnp.where(row == 1, low.astype(F32), lines)
            out[n, rows:] = lines.astype(BF16)


def add_pair(a, b, rows):
    vmem = pl.BlockSpec(memory_space=VMEM)
    return pl.pallas_call(
        functools.partial(pair_kernel, rows),
        out_shape=jax.ShapeDtypeStruct(a.shape, BF16),
        in_specs=[vmem] * 2,
        out_specs=vmem,
        compiler_params=pltpu.CompilerParams(vmem_limit_bytes=4 * 2**20),
        name="add_pair",
    )(a, b)


def next_kernel(wide0, wide1, same, other, fresh):
    fresh[0] = (
        wide0[...].astype(F32) + (same[0].astype(F32) + other[1].astype(F32))
    ).astype(BF16)
    fresh[1] = (
        wide1[...].astype(F32) + (same[1].astype(F32) + other[0].astype(F32))
    ).astype(BF16)


def add_next(wide0, wide1, same, other):
    vmem = pl.BlockSpec(memory_space=VMEM)
    return pl.pallas_call(
        next_kernel,
        out_shape=jax.ShapeDtypeStruct(same.shape, BF16),
        in_specs=[vmem] * 4,
        out_specs=vmem,
        compiler_params=pltpu.CompilerParams(vmem_limit_bytes=4 * 2**20),
        name="add_next",
    )(wide0, wide1, same, other)


def last_kernel(scal, mine, state, here, there, out, importance):
    rows = mine.shape[0]
    total = here[0].astype(F32) + there[...].astype(F32)
    wide = jnp.where(scal[S_SECTION] == 0, mine[...], state[0]).astype(F32)
    out[...] = (wide + total[:rows]).astype(BF16)
    importance[...] = total[rows : rows + 1, :HD] + total[rows + 1 : rows + 2, :HD]


def add_last(scal, mine, state, here, there):
    vmem = pl.BlockSpec(memory_space=VMEM)
    return pl.pallas_call(
        last_kernel,
        out_shape=(
            jax.ShapeDtypeStruct(mine.shape, BF16),
            jax.ShapeDtypeStruct((1, HD), F32),
        ),
        in_specs=[pl.BlockSpec(memory_space=pltpu.SMEM)] + [vmem] * 4,
        out_specs=(vmem, vmem),
        compiler_params=pltpu.CompilerParams(vmem_limit_bytes=4 * 2**20),
        name="add_last",
    )(scal, mine, state, here, there)


def swap(block, mask):
    return lax.ppermute(block, "tensor", [(t, t ^ mask) for t in range(N_TENSOR)])


def to_next_section(block, mask):
    route = [(t, N_TENSOR + (t ^ mask)) for t in range(N_TENSOR)]
    return lax.ppermute(block, ("pipe", "tensor"), route)


def local(hidden_in, norm_gain, w_query, w_keyval, w_out, head_group):
    section = lax.axis_index("pipe")
    tensor = lax.axis_index("tensor")
    data = lax.axis_index("dp")
    rows, cols = hidden_in.shape[0], hidden_in.shape[3]
    width = cols * N_TENSOR * N_DP
    wq, wkv, wout = w_query[0], w_keyval[0], w_out[0]
    scal = jnp.stack([section, tensor, data]).astype(jnp.int32)
    cosine, sine = map(jnp.asarray, rotary_tables(rows))

    def to_heads(step, pieces, *weights):
        send = project(step, scal, pieces, norm_gain, *weights)
        recv = lax.all_to_all(send, "dp", 0, 0)
        query, kv, gram = combine(step, scal, recv, cosine, sine, width)
        every = lax.all_gather(kv, "tensor")
        mine = choose(scal, head_group, every.reshape(GROUPS, 16, 2 * HD))
        kv_mine = lax.all_to_all(mine, "dp", 0, 0).reshape(rows, 2 * HD)
        return query, kv_mine, gram

    mine = hidden_in.reshape(rows, cols)
    far = swap(mine, 2)
    pieces = (mine, swap(mine, 1), far, swap(mine, 3))
    query, kv, gram0 = to_heads(0, pieces, *load(scal, wq, wkv, wout)[::-1])
    att0 = attend(scal, query, kv)
    recv = lax.all_to_all(att0, "dp", 0, 0)
    other0 = project_out(scal, head_group, recv, wout, rows, (1, 3))
    own0 = project_out(scal, head_group, recv, wout, rows, (0, 2))
    here = add_pair(own0, swap(other0, 1), rows)
    state = add_next(mine, far, to_next_section(here, 0), to_next_section(here, 2))

    beside = swap(state, 1)
    pieces = (state, beside)
    query, kv, gram1 = to_heads(1, pieces, wkv.reshape(wq.shape[0], -1), wq, wout)
    att1 = attend_last(scal, query, kv, att0, gram0, gram1, width)
    recv = lax.all_to_all(att1, "dp", 0, 0)
    other1 = project_out(scal, head_group, recv, wout, rows, (1, 3), other0)
    own1 = project_out(scal, head_group, recv, wout, rows, (0, 2), own0)
    here = add_pair(own1, swap(other1, 1), rows)
    out, importance = add_last(scal, mine, state, here, swap(here[1], 2))
    return out.reshape(1, rows, 1, 1, cols), importance[:, :GROUPS]


def solution(mesh):
    in_specs = (
        P(None, "dp", "tensor", None),
        P("pipe", "dp"),
        P("pipe", "dp", "tensor"),
        P("pipe", "dp", "tensor", None),
        P("pipe", "tensor", "dp"),
        P(),
    )
    out_specs = (P("pipe", None, "dp", "tensor", None), P("pipe", None))
    return jax.shard_map(local, mesh=mesh, in_specs=in_specs, out_specs=out_specs, check_vma=False)
```

time: 185 us -> 177 us (0.957)
  Pallas kernels: 21.3 us -> 18.3 us
  local copies, waits for them, and re-layouts: 5.94 us -> 3.69 us
  waiting for transfers between devices: 23.7 us -> 21.8 us
    pallas_call x4, Pallas kernels: 9 us -> 3.81 us  [project_out(): pl.pallas_call(functools.partial(kernel, rows, masks), out_shape=jax.Shap...]
    ppermute x7, waiting for transfers between devices: 10.1 us -> 7.09 us  [swap(): lax.ppermute(block, 'tensor', [(t, t ^ mask) for t in range(N_TENSOR)])]
    pallas_call x2 -> x3, Pallas kernels: 1.71 us -> 4.43 us  [the longest x1 2.89 us: load(): pl.pallas_call(load_kernel, out_shape=(jax.ShapeDtypeStruct((chunks * dee...]
    unnamed x17, local copies, waits for them, and re-layouts: 5.85 us -> 3.67 us
  transfers between devices with their start and end apart: 9 -> 9, of which waited for: 4 -> 6; matrix products, arithmetic and copies ran while one was open for 1% -> 0% of each run, Pallas kernels for 2% -> 3%
where the time goes in v3:
time: 177 us; the launch traced here: 176 us
  blocking collectives  125 us (71%)
  waiting for transfers between devices  21.8 us (12%)
  Pallas kernels  18.3 us (10%)
  starting transfers between devices  6.36 us (4%)
  local copies, waits for them, and re-layouts  3.69 us (2%)
    all_to_all x2, blocking collectives, to_heads(): recv = lax.all_to_all(send, 'dp', 0, 0)  52.7 us
    all_to_all x2, blocking collectives, to_heads(): kv_mine = lax.all_to_all(mine, 'dp', 0, 0).reshape(rows, 2 * HD)  21.6 us
    all_to_all x1, blocking collectives, local(): recv = lax.all_to_all(att1, 'dp', 0, 0)  20.4 us
    all_to_all x1, blocking collectives, local(): recv = lax.all_to_all(att0, 'dp', 0, 0)  19.6 us
    ppermute x2, waiting for transfers between devices, to_next_section(): return lax.ppermute(block, ('pipe', 'tensor'), route)  14.8 us
    all_gather x2, blocking collectives, to_heads(): every = lax.all_gather(kv, 'tensor')  10.8 us
    ppermute x7, waiting for transfers between devices, swap(): lax.ppermute(block, 'tensor', [(t, t ^ mask) for t in range(N_TENSOR)])  7.09 us
    pallas_call x2, Pallas kernels, project(): pl.pallas_call(functools.partial(project_kernel, step, len(pieces)), out_...  5.46 us
  transfers between devices with their start and end apart: 9, of which 6 were waited for; matrix products, arithmetic and copies ran while one was open for 0% of the time, Pallas kernels for 3%

profile of v3, /device:TPU:4, one launch (start us, length us, event | category | flops | bytes accessed | tf_op | source)
XLA Modules:
  0.0 176.3 jit_solution(7966622133590066181)
XLA Ops:
  0.6 1.3 collective-permute-start
  1.9 0.0 collective-permute-start.1
  1.9 0.9 collective-permute-start.2
  2.9 0.1 pad_add_fusion.scal
  2.9 2.2 %copy-done.1 = bf16[1,1024,2048]{2,1,0:T(8,128)(2,1)S(1)} copy-done((bf16[1,1024,2048]{2,1,0:T(8,128)(2,1)S(1)}, bf16[1,1024,2048]{2,1,0:T(8,128)(2,1)}, u32[]{:S(2)}) %copy-start.1) | copy-done | bytes 4194328
  5.1 1.2 copy-done.2
  6.3 2.9 %load.1 = (bf16[4096,512]{1,0:T(8,128)(2,1)S(1)}, bf16[1024,512]{1,0:T(8,128)(2,1)S(1)}) custom-call(s32[3]{0:T(128)S(1)} %pad_add_fusion.scal, bf16[1024,2048]{1,0:T(8,128)(2,1)S(1)} %bitcast.24, bf16[1024,2,256]{2,1,0:T(2,128)(2,1)S(1)} %bitcast.28, bf16[2048,1024]{1,0:T(8,128)(2,1)} %bitcast.18), custom_call_target="tpu_custom_call" | custom-call | flops 1000000000 | bytes 1 | tf_op jit(solution)/shard_map/load/pallas_call | solution.py:108
  9.2 0.0 collective-permute-done.refs_2_.wide1
  9.3 3.3 %project.2 = bf16[5376,128]{1,0:T(8,128)(2,1)S(1)} custom-call(s32[3]{0:T(128)S(1)} %pad_add_fusion.scal, bf16[256,256]{1,0:T(8,128)(2,1)S(1)} %bitcast.34, bf16[256,256]{1,0:T(8,128)(2,1)S(1)} %collective-permute-done.1.refs_1_, bf16[256,256]{1,0:T(8,128)(2,1)S(1)} %collective-permute-done.refs_2_.wide1, ...), custom_call_target="tpu_custom_call" | custom-call | tf_op jit(solution)/shard_map/project/pallas_call | solution.py:210
  12.6 0.0 copy-start.4
  12.6 0.0 copy-start.5
  12.7 0.0 copy-start.6
  12.7 28.8 %all_to_all.30.recv = bf16[16,336,128]{2,1,0:T(8,128)(2,1)S(1)} all-to-all(bf16[16,336,128]{2,1,0:T(8,128)(2,1)S(1)} %bitcast.26), channel_id=1, replica_groups=mesh['pipe'=2,'tensor'=4,'dp'=16] {'dp'}, dimensions={0} | all-to-all | bytes 2752512 | tf_op jit(solution)/shard_map/all_to_all | solution.py:531
  41.5 0.7 combine.2
  42.2 5.4 %all-gather.kv = bf16[8,16,256]{2,1,0:T(8,128)(2,1)S(1)} all-gather(bf16[2,16,256]{2,1,0:T(8,128)(2,1)S(1)} %get-tuple-element.15), channel_id=2, replica_groups=mesh['pipe'=2,'tensor'=4,'dp'=16] {'tensor'}, dimensions={0}, use_global_device_ids=true | all-gather | bytes 81920 | tf_op jit(solution)/shard_map/all_gather | solution.py:533
  47.6 0.6 choose.2
  48.1 10.8 %all_to_all.31 = bf16[16,16,256]{2,1,0:T(8,128)(2,1)S(1)} all-to-all(bf16[16,16,256]{2,1,0:T(8,128)(2,1)S(1)} %choose.2), channel_id=1, replica_groups=mesh['pipe'=2,'tensor'=4,'dp'=16] {'dp'}, dimensions={0} | all-to-all | bytes 262144 | tf_op jit(solution)/shard_map/all_to_all | solution.py:535
  58.9 0.7 attend.1.before
  59.6 19.6 %all_to_all.32.recv = bf16[16,256,128]{2,1,0:T(8,128)(2,1)S(1)} all-to-all(bf16[16,256,128]{2,1,0:T(8,128)(2,1)S(1)} %attend.1.before), channel_id=1, replica_groups=mesh['pipe'=2,'tensor'=4,'dp'=16] {'dp'}, dimensions={0} | all-to-all | bytes 2097152 | tf_op jit(solution)/shard_map/all_to_all | solution.py:543
  79.3 0.6 project_out.5.saved
  79.9 0.1 collective-permute-start.3
  80.0 0.6 project_out.4.a.saved
  80.6 0.9 collective-permute-done.3.b
  81.5 0.1 add_pair.2
  81.6 1.3 collective-permute-start.4
  82.9 1.3 collective-permute-start.5
  84.2 9.2 %collective-permute-done.4.same = bf16[2,256,256]{2,1,0:T(8,128)(2,1)S(1)} collective-permute-done((bf16[2,256,256]{2,1,0:T(8,128)(2,1)S(1)}, bf16[2,256,256]{2,1,0:T(8,128)(2,1)S(1)}, u32[]{:S(2)}, u32[]{:S(2)}) %collective-permute-start.4) | collective-permute-done | bytes 262176 | tf_op jit(solution)/shard_map/ppermute | solution.py:516
  93.4 5.5 %collective-permute-done.5.other = bf16[2,256,256]{2,1,0:T(8,128)(2,1)S(1)} collective-permute-done((bf16[2,256,256]{2,1,0:T(8,128)(2,1)S(1)}, bf16[2,256,256]{2,1,0:T(8,128)(2,1)S(1)}, u32[]{:S(2)}, u32[]{:S(2)}) %collective-permute-start.5) | collective-permute-done | bytes 262176 | tf_op jit(solution)/shard_map/ppermute | solution.py:516
  98.9 0.1 add_next.1.refs_0_.state
  99.0 0.1 collective-permute-start.6
  99.1 0.2 copy.10
  99.4 1.3 collective-permute-done.6.refs_1_
  100.6 2.1 %project.3 = bf16[5376,128]{1,0:T(8,128)(2,1)S(1)} custom-call(s32[3]{0:T(128)S(1)} %pad_add_fusion.scal, bf16[2,256,256]{2,1,0:T(8,128)(2,1)S(1)} %add_next.1.refs_0_.state, bf16[2,256,256]{2,1,0:T(8,128)(2,1)S(1)} %collective-permute-done.6.refs_1_, bf16[1,1024]{1,0:T(2,128)(2,1)S(1)} %copy-done.7, bf16[1024,512]{1,0:T(8,128)(2,1)S(1)} %bitcast.30, ...), custom_call_target="tpu_custom_call" | custom-call | tf_op jit(solution)/shard_map/project/pallas_call | solution.py:210
  102.8 23.9 %all_to_all.33.recv = bf16[16,336,128]{2,1,0:T(8,128)(2,1)S(1)} all-to-all(bf16[16,336,128]{2,1,0:T(8,128)(2,1)S(1)} %bitcast.27), channel_id=1, replica_groups=mesh['pipe'=2,'tensor'=4,'dp'=16] {'dp'}, dimensions={0} | all-to-all | bytes 2752512 | tf_op jit(solution)/shard_map/all_to_all | solution.py:531
  126.7 0.9 combine.3
  127.6 5.4 %all-gather.1.kv = bf16[8,16,256]{2,1,0:T(8,128)(2,1)S(1)} all-gather(bf16[2,16,256]{2,1,0:T(8,128)(2,1)S(1)} %get-tuple-element.17), channel_id=3, replica_groups=mesh['pipe'=2,'tensor'=4,'dp'=16] {'tensor'}, dimensions={0}, use_global_device_ids=true | all-gather | bytes 81920 | tf_op jit(solution)/shard_map/all_gather | solution.py:533
  133.0 0.6 choose.3
  133.6 10.8 %all_to_all.34 = bf16[16,16,256]{2,1,0:T(8,128)(2,1)S(1)} all-to-all(bf16[16,16,256]{2,1,0:T(8,128)(2,1)S(1)} %choose.3), channel_id=1, replica_groups=mesh['pipe'=2,'tensor'=4,'dp'=16] {'dp'}, dimensions={0} | all-to-all | bytes 262144 | tf_op jit(solution)/shard_map/all_to_all | solution.py:535
  144.4 1.3 attend_last.1
  145.6 20.4 %all_to_all.35.recv = bf16[16,272,128]{2,1,0:T(8,128)(2,1)S(1)} all-to-all(bf16[16,272,128]{2,1,0:T(8,128)(2,1)S(1)} %attend_last.1), channel_id=1, replica_groups=mesh['pipe'=2,'tensor'=4,'dp'=16] {'dp'}, dimensions={0} | all-to-all | bytes 2228224 | tf_op jit(solution)/shard_map/all_to_all | solution.py:553
  166.1 1.3 project_out.7
  167.4 0.1 collective-permute-start.7
  167.5 1.3 project_out.6.a
  168.8 0.2 collective-permute-done.7.b
  169.0 0.1 add_pair.3.here
  169.1 1.3 collective-permute-start.8
  170.4 4.7 %collective-permute-done.8.there = bf16[272,256]{1,0:T(8,128)(2,1)S(1)} collective-permute-done((bf16[272,256]{1,0:T(8,128)(2,1)S(1)}, bf16[272,256]{1,0:T(8,128)(2,1)S(1)}, u32[]{:S(2)}, u32[]{:S(2)}) %collective-permute-start.8) | collective-permute-done | bytes 139296 | tf_op jit(solution)/shard_map/ppermute | solution.py:511
  175.1 1.3 add_last.1
  (14 shorter events, 0.0 us)
Async XLA Ops:
  0.6 8.6 %collective-permute-start = (bf16[256,256]{1,0:T(8,128)(2,1)}, bf16[256,256]{1,0:T(8,128)(2,1)S(1)}, u32[]{:S(2)}, u32[]{:S(2)}) collective-permute-start(bf16[256,256]{1,0:T(8,128)(2,1)} %bitcast.31), channel_id=1, source_target_pairs={{0,32},{16,48},{32,0},{48,16},{1,33},{17,49},{33,1},{49,17},{2,34}... | collective-permute-start | bytes 393224 | tf_op jit(solution)/shard_map/ppermute | solution.py:511
  1.9 7.3 %collective-permute-start.1 = (bf16[256,256]{1,0:T(8,128)(2,1)}, bf16[256,256]{1,0:T(8,128)(2,1)S(1)}, u32[]{:S(2)}, u32[]{:S(2)}) collective-permute-start(bf16[256,256]{1,0:T(8,128)(2,1)} %bitcast.32), channel_id=1, source_target_pairs={{0,16},{16,0},{32,48},{48,32},{1,17},{17,1},{33,49},{49,33},{2,18}... | collective-permute-start | bytes 393224 | tf_op jit(solution)/shard_map/ppermute | solution.py:511
  1.9 7.4 %collective-permute-start.2 = (bf16[256,256]{1,0:T(8,128)(2,1)}, bf16[256,256]{1,0:T(8,128)(2,1)S(1)}, u32[]{:S(2)}, u32[]{:S(2)}) collective-permute-start(bf16[256,256]{1,0:T(8,128)(2,1)} %bitcast.33), channel_id=1, source_target_pairs={{0,48},{16,32},{32,16},{48,0},{1,49},{17,33},{33,17},{49,1},{2,50}... | collective-permute-start | bytes 393224 | tf_op jit(solution)/shard_map/ppermute | solution.py:511
  2.9 2.2 %copy-start.1 = (bf16[1,1024,2048]{2,1,0:T(8,128)(2,1)S(1)}, bf16[1,1024,2048]{2,1,0:T(8,128)(2,1)}, u32[]{:S(2)}) copy-start(bf16[1,1024,2048]{2,1,0:T(8,128)(2,1)} %param.10) | copy-start | bytes 12582916
  5.1 1.2 copy-start.2
  6.3 2.9 %copy-start.3 = (bf16[256,1,1,256]{3,0,2,1:T(8,128)(2,1)S(1)}, bf16[256,1,1,256]{3,0,2,1:T(8,128)(2,1)}, u32[]{:S(2)}) copy-start(bf16[256,1,1,256]{3,0,2,1:T(8,128)(2,1)} %param.8) | copy-start | bytes 393220
  6.3 2.9 %copy-start.7 = (bf16[1,1024]{1,0:T(2,128)(2,1)S(1)}, bf16[1,1024]{1,0:T(2,128)(2,1)}, u32[]{:S(2)}) copy-start(bf16[1,1024]{1,0:T(2,128)(2,1)} %refs_2_.1) | copy-start | bytes 6148
  12.6 28.9 %copy-start.4 = (f32[256,128]{1,0:T(8,128)S(1)}, f32[256,128]{1,0:T(8,128)}, u32[]{:S(2)}) copy-start(f32[256,128]{1,0:T(8,128)} %constant.19.clone.cosine) | copy-start | bytes 393220
  12.6 28.8 %copy-start.5 = (f32[256,128]{1,0:T(8,128)S(1)}, f32[256,128]{1,0:T(8,128)}, u32[]{:S(2)}) copy-start(f32[256,128]{1,0:T(8,128)} %constant.20.clone.sine) | copy-start | bytes 393220
  12.7 34.9 %copy-start.6 = (s32[64]{0:T(128)S(1)}, s32[64]{0:T(128)}, u32[]{:S(2)}) copy-start(s32[64]{0:T(128)} %group.11) | copy-start | bytes 772
  41.5 37.8 %copy-start = (bf16[1,2048,1024]{2,1,0:T(8,128)(2,1)S(1)}, bf16[1,2048,1024]{2,1,0:T(8,128)(2,1)}, u32[]{:S(2)}) copy-start(bf16[1,2048,1024]{2,1,0:T(8,128)(2,1)} %param.12) | copy-start | bytes 12582916
  79.9 1.6 collective-permute-start.3
  81.6 11.8 %collective-permute-start.4 = (bf16[2,256,256]{2,1,0:T(8,128)(2,1)S(1)}, bf16[2,256,256]{2,1,0:T(8,128)(2,1)S(1)}, u32[]{:S(2)}, u32[]{:S(2)}) collective-permute-start(bf16[2,256,256]{2,1,0:T(8,128)(2,1)S(1)} %add_pair.2), channel_id=1, source_target_pairs={{0,64},{16,80},{32,96},{48,112},{1,65},{17,81},{33,97},{49,113},{2... | collective-permute-start | bytes 786440 | tf_op jit(solution)/shard_map/ppermute | solution.py:516
  82.9 16.1 %collective-permute-start.5 = (bf16[2,256,256]{2,1,0:T(8,128)(2,1)S(1)}, bf16[2,256,256]{2,1,0:T(8,128)(2,1)S(1)}, u32[]{:S(2)}, u32[]{:S(2)}) collective-permute-start(bf16[2,256,256]{2,1,0:T(8,128)(2,1)S(1)} %add_pair.2), channel_id=1, source_target_pairs={{0,96},{16,112},{32,64},{48,80},{1,97},{17,113},{33,65},{49,81},{2... | collective-permute-start | bytes 786440 | tf_op jit(solution)/shard_map/ppermute | solution.py:516
  99.0 1.6 collective-permute-start.6
  167.4 1.6 collective-permute-start.7
  169.1 5.9 %collective-permute-start.8 = (bf16[272,256]{1,0:T(8,128)(2,1)S(1)}, bf16[272,256]{1,0:T(8,128)(2,1)S(1)}, u32[]{:S(2)}, u32[]{:S(2)}) collective-permute-start(bf16[272,256]{1,0:T(8,128)(2,1)S(1)} %slice_bitcast_fusion), channel_id=1, source_target_pairs={{0,32},{16,48},{32,0},{48,16},{1,33},{17,49},{33,1},{49,17},{2,34}... | collective-permute-start | bytes 417800 | tf_op jit(solution)/shard_map/ppermute | solution.py:511

commit v4 on v3

v4 whole, which is shorter than its diff:
```python
import functools
import math

import jax
import jax.numpy as jnp
import numpy as np
from jax import lax
from jax.experimental import pallas as pl
from jax.experimental.pallas import tpu as pltpu
from jax.sharding import PartitionSpec as P

HD = 128
GROUPS = 8
N_TENSOR = 4
N_DP = 16
THETA = 500000.0
EPS_NORM = 1e-05
EPS_RMS = 1e-06
STATS = 16

BF16 = jnp.bfloat16
F32 = jnp.float32
VMEM = pltpu.VMEM


def rotary_tables(rows):
    positions = np.arange(rows, dtype=np.float64)[:, None]
    lanes = np.arange(HD)
    angle = positions * THETA ** (-2.0 * (lanes // 2) / HD)[None, :]
    sign = np.where(lanes % 2 == 0, -1.0, 1.0)[None, :]
    return np.cos(angle).astype(np.float32), (np.sin(angle) * sign).astype(np.float32)


def rotated(values, cosine, sine):
    lanes = lax.broadcasted_iota(jnp.int32, values.shape, 1)
    swapped = jnp.where(
        lanes % 2 == 0, pltpu.roll(values, HD - 1, 1), pltpu.roll(values, 1, 1)
    )
    return values * cosine + swapped * sine


def diagonal():
    return lax.broadcasted_iota(jnp.int32, (HD, HD), 0) == lax.broadcasted_iota(
        jnp.int32, (HD, HD), 1
    )


def two_parts(values):
    high = values.astype(BF16)
    return high, (values - high.astype(F32)).astype(BF16)


def load_kernel(wq, wkv, out):
    cols = wkv.shape[2]
    for g in range(wkv.shape[1]):
        out[:, g * cols : (g + 1) * cols] = wkv[:, g, :]


def load(wq, wkv):
    vmem = pl.BlockSpec(memory_space=VMEM)
    return pl.pallas_call(
        load_kernel,
        out_shape=jax.ShapeDtypeStruct((wkv.shape[0], wkv.shape[1] * wkv.shape[2]), BF16),
        in_specs=[vmem] * 2,
        out_specs=vmem,
        compiler_params=pltpu.CompilerParams(vmem_limit_bytes=12 * 2**20),
        cost_estimate=pl.CostEstimate(flops=10**9, bytes_accessed=10**7, transcendentals=0),
        name="load",
    )(wq, wkv)


def gram_parts(wout, target):
    @pl.loop(0, wout.shape[0] // (2 * HD))
    def _(i):
        pair = wout[pl.ds(pl.multiple_of(i * 2 * HD, 2 * HD), 2 * HD), :]
        both = lax.dot_general(pair, pair, (((1,), (1,)), ((), ())), preferred_element_type=F32)
        for n in range(2):
            high, low = two_parts(both[n * HD : (n + 1) * HD, n * HD : (n + 1) * HD])
            ref, first = target(2 * i + n)
            ref[pl.ds(first, HD), :] = high
            ref[pl.ds(first + HD, HD), :] = low


def project_kernel(step, count, *refs):
    pieces, refs = refs[:count], refs[count:]
    gain, wkv, wq, *wout, send, scaled = refs
    rows, cols = pieces[0].shape[-2:]
    per = 4
    heads = N_DP
    pitch = rows + 64 + STATS
    tensor = lax.axis_index("tensor")
    if count == 4:
        by_mask = [ref[...] for ref in pieces]
    else:
        by_mask = [pieces[mask % 2][mask // 2] for mask in range(4)]

    def block(place):
        low = [jnp.where(tensor % 2 == place % 2, by_mask[n], by_mask[n + 1]) for n in (0, 2)]
        return jnp.where(tensor // 2 == place // 2, low[0], low[1])

    active = lax.axis_index("pipe") == step

    @pl.when(active)
    def _():
        total = jnp.zeros((rows, 1), F32)
        for place in range(N_TENSOR):
            at = slice(place * cols, (place + 1) * cols)
            wide = block(place).astype(F32)
            total = total + jnp.sum(wide * wide, axis=1, keepdims=True)
            scaled[:, at] = (wide * gain[:, at].astype(F32)).astype(BF16)
        eye = diagonal()
        row = lax.broadcasted_iota(jnp.int32, (STATS, HD), 0)
        lines = jnp.zeros((STATS, HD), F32)
        for b in range(rows // HD):
            line = jnp.sum(
                jnp.where(eye, total[b * HD : (b + 1) * HD], 0.0), axis=0, keepdims=True
            )
            high, low = two_parts(line)
            lines = jnp.where(row == 2 * b, high.astype(F32), lines)
            lines = jnp.where(row == 2 * b + 1, low.astype(F32), lines)
        lines = lines.astype(BF16)
        part = jnp.dot(scaled[...], wkv[...], preferred_element_type=F32).astype(BF16)
        for j in range(heads):
            first = j * pitch + rows
            for c in range(4):
                send[first + 16 * c : first + 16 * c + 16, :] = part[
                    16 * j : 16 * j + 16, c * HD : (c + 1) * HD
                ]
            send[first + 64 : first + 64 + STATS, :] = lines
        for i in range(heads // per):
            part = jnp.dot(
                scaled[...], wq[:, i * per * HD : (i + 1) * per * HD], preferred_element_type=F32
            ).astype(BF16)
            for j in range(per):
                first = (i * per + j) * pitch
                send[first : first + rows, :] = part[:, j * HD : (j + 1) * HD]

    @pl.when(jnp.logical_not(active))
    def _():
        if wout:
            gram_parts(wout[0], lambda h: (send, pl.multiple_of(h * pitch, 16)))
            for j in range(heads):
                first = j * pitch + rows
                send[first : first + 64 + STATS, :] = jnp.zeros((64 + STATS, HD), BF16)
        else:
            send[...] = jnp.zeros_like(send)


def project(step, pieces, gain, wkv, *weights):
    rows, cols = pieces[0].shape[-2:]
    wide = cols * N_TENSOR
    pitch = rows + 64 + STATS
    vmem = pl.BlockSpec(memory_space=VMEM)
    send = pl.pallas_call(
        functools.partial(project_kernel, step, len(pieces)),
        out_shape=jax.ShapeDtypeStruct((N_DP * pitch, HD), BF16),
        in_specs=[vmem] * (len(pieces) + 2 + len(weights)),
        out_specs=vmem,
        scratch_shapes=[VMEM((rows, wide), BF16)],
        compiler_params=pltpu.CompilerParams(vmem_limit_bytes=8 * 2**20),
        name="project",
    )(*pieces, gain, wkv, *weights)
    return send.reshape(N_DP, pitch, HD)


def combine_kernel(step, width, recv, cosine, sine, query, kv, gram, scale):
    rows = cosine.shape[0]
    active = lax.axis_index("pipe") == step

    def total(first, size):
        at = slice(first, first + size)
        value = recv[0, at, :].astype(F32)
        for s in range(1, N_DP):
            value = value + recv[s, at, :].astype(F32)
        return value

    @pl.when(active)
    def _():
        raw = total(0, rows)
        tail = total(rows, 64 + STATS)
        eye = diagonal()
        for b in range(rows // HD):
            line = tail[64 + 2 * b : 65 + 2 * b, :] + tail[65 + 2 * b : 66 + 2 * b, :]
            column = jnp.sum(jnp.where(eye, line, 0.0), axis=1, keepdims=True)
            factor = lax.rsqrt(column / width + EPS_NORM)
            scale[b * HD : (b + 1) * HD, :] = jnp.broadcast_to(factor, (HD, HD))
        query[...] = rotated(raw * scale[...], cosine[...], sine[...]).astype(BF16)
        first = pl.multiple_of(lax.axis_index("dp") * 16, 16)
        here = scale[pl.ds(first, 16), :]
        cos_here = cosine[pl.ds(first, 16), :]
        sin_here = sine[pl.ds(first, 16), :]
        for g in range(2):
            keys = tail[32 * g : 32 * g + 16] * here
            vals = tail[32 * g + 16 : 32 * g + 32] * here
            kv[g, :, :HD] = rotated(keys, cos_here, sin_here).astype(BF16)
            kv[g, :, HD:] = vals.astype(BF16)
        gram[...] = jnp.zeros_like(gram)

    @pl.when(jnp.logical_not(active))
    def _():
        gram[...] = total(0, HD) + total(HD, HD)
        query[...] = jnp.zeros_like(query)
        kv[...] = jnp.zeros_like(kv)


def combine(step, recv, cosine, sine, width):
    rows = cosine.shape[0]
    vmem = pl.BlockSpec(memory_space=VMEM)
    return pl.pallas_call(
        functools.partial(combine_kernel, step, float(width)),
        out_shape=(
            jax.ShapeDtypeStruct((rows, HD), BF16),
            jax.ShapeDtypeStruct((2, 16, 2 * HD), BF16),
            jax.ShapeDtypeStruct((HD, HD), F32),
        ),
        in_specs=[vmem] * 3,
        out_specs=(vmem, vmem, vmem),
        scratch_shapes=[VMEM((rows, HD), F32)],
        compiler_params=pltpu.CompilerParams(vmem_limit_bytes=8 * 2**20),
        name="combine",
    )(recv, cosine, sine)


def choose_kernel(group, kv, send):
    for j in range(N_DP):
        send[j] = kv[group[lax.axis_index("tensor") * N_DP + j]]


def choose(group, kv):
    vmem = pl.BlockSpec(memory_space=VMEM)
    return pl.pallas_call(
        choose_kernel,
        out_shape=jax.ShapeDtypeStruct((N_DP,) + kv.shape[1:], BF16),
        in_specs=[pl.BlockSpec(memory_space=pltpu.SMEM), vmem],
        out_specs=vmem,
        compiler_params=pltpu.CompilerParams(vmem_limit_bytes=4 * 2**20),
        name="choose",
    )(group, kv)


def attended(query, kv):
    rows = query.shape[0]
    scores = lax.dot_general(
        query, kv[:, :HD], (((1,), (1,)), ((), ())), preferred_element_type=F32
    )
    allowed = lax.broadcasted_iota(jnp.int32, (rows, rows), 0) >= lax.broadcasted_iota(
        jnp.int32, (rows, rows), 1
    )
    expo = jnp.where(allowed, jnp.exp(scores * (1.0 / math.sqrt(HD))), 0.0)
    weights = (expo / jnp.sum(expo, axis=1, keepdims=True)).astype(BF16)
    return jnp.dot(weights, kv[:, HD:], preferred_element_type=F32).astype(BF16)


def attend_kernel(query, kv, wout, send):
    active = lax.axis_index("pipe") == 0

    @pl.when(active)
    def _():
        result = attended(query[...], kv[...])
        for j in range(N_DP):
            send[j] = result

    @pl.when(jnp.logical_not(active))
    def _():
        gram_parts(wout, lambda h: (send.at[h], 0))


def attend(query, kv, wout):
    rows = query.shape[0]
    vmem = pl.BlockSpec(memory_space=VMEM)
    return pl.pallas_call(
        attend_kernel,
        out_shape=jax.ShapeDtypeStruct((N_DP, rows, HD), BF16),
        in_specs=[vmem] * 3,
        out_specs=vmem,
        compiler_params=pltpu.CompilerParams(vmem_limit_bytes=8 * 2**20),
        name="attend",
    )(query, kv, wout)


def attend_last_kernel(width, query, kv, before, gram0, gram1, send):
    rows = query.shape[0]
    result = attended(query[...], kv[...])
    first_section = lax.axis_index("pipe") == 0
    mine = jnp.where(first_section, before[0], result)
    gram = jnp.where(first_section, gram1[...], gram0[...])
    high, low = two_parts(gram)
    image = jnp.dot(mine, high, preferred_element_type=F32) + jnp.dot(
        mine, low, preferred_element_type=F32
    )
    squares = jnp.sum(image * mine.astype(F32), axis=1, keepdims=True)
    spread = jnp.sqrt(jnp.maximum(squares / width, 0.0) + EPS_RMS)
    mean = jnp.sum(spread, axis=0, keepdims=True) / rows
    high, low = two_parts(mean)
    row = lax.broadcasted_iota(jnp.int32, (STATS, HD), 0)
    lines = jnp.where(row == 0, high.astype(F32), jnp.where(row == 1, low.astype(F32), 0.0))
    lines = lines.astype(BF16)
    for j in range(N_DP):
        send[j, :rows] = result
        send[j, rows:] = lines


def attend_last(query, kv, before, gram0, gram1, width):
    rows = query.shape[0]
    vmem = pl.BlockSpec(memory_space=VMEM)
    return pl.pallas_call(
        functools.partial(attend_last_kernel, float(width)),
        out_shape=jax.ShapeDtypeStruct((N_DP, rows + STATS, HD), BF16),
        in_specs=[vmem] * 5,
        out_specs=vmem,
        compiler_params=pltpu.CompilerParams(vmem_limit_bytes=8 * 2**20),
        name="attend_last",
    )(query, kv, before, gram0, gram1)


def out_kernel(rows, masks, last, *refs):
    if last:
        group, recv, saved, wout, parts = refs
    else:
        recv, wout, parts, *gram = refs
    heads = recv.shape[0]
    cols = parts.shape[2]
    tensor = lax.axis_index("tensor")
    active = lax.axis_index("pipe") == (1 if last else 0)
    if last:
        lane = lax.broadcasted_iota(jnp.int32, (1, cols), 1)
        sums = jnp.zeros((1, cols), F32)
        for h in range(heads):
            value = recv[h, rows : rows + 1, :].astype(F32) + recv[
                h, rows + 1 : rows + 2, :
            ].astype(F32)
            value = jnp.concatenate([value] * (cols // HD), axis=1)
            sums = sums + jnp.where(lane == group[tensor * heads + h], value, 0.0)
        high, low = two_parts(sums)
        row = lax.broadcasted_iota(jnp.int32, (STATS, cols), 0)
        lines = jnp.where(
            row == 0, high.astype(F32), jnp.where(row == 1, low.astype(F32), 0.0)
        ).astype(BF16)
        for n in range(2):
            parts[n, rows:] = lines
    for parity in range(2):

        @pl.when(jnp.logical_and(active, (tensor + masks[0] + parity) % 2 == 0))
        def _():
            for place in (parity, parity + 2):
                total = None
                for h in range(0, heads, 2):
                    pair = jnp.concatenate([recv[h, :rows, :], recv[h + 1, :rows, :]], axis=1)
                    one = jnp.dot(
                        pair,
                        wout[h * HD : (h + 2) * HD, place * cols : (place + 1) * cols],
                        preferred_element_type=F32,
                    )
                    total = one if total is None else total + one
                n = lax.bitwise_xor(tensor, place) // 2
                parts[n, :rows] = total.astype(BF16)

    @pl.when(jnp.logical_not(active))
    def _():
        for n in range(2):
            parts[n, :rows] = saved[n] if last else jnp.zeros((rows, cols), BF16)
        if not last and gram:
            total = jnp.zeros((HD, HD), F32)
            for s in range(heads):
                total = total + (recv[s, :HD].astype(F32) + recv[s, HD : 2 * HD].astype(F32))
            gram[0][...] = total

    if not last and gram:

        @pl.when(active)
        def _():
            gram[0][...] = jnp.zeros((HD, HD), F32)


def project_out(recv, wout, rows, masks, group=None, saved=None):
    heads, deep, _ = recv.shape
    cols = wout.shape[1] // N_TENSOR
    last = saved is not None
    vmem = pl.BlockSpec(memory_space=VMEM)
    shapes = (jax.ShapeDtypeStruct((2, deep, cols), BF16),)
    if not last and masks[0] == 0:
        shapes += (jax.ShapeDtypeStruct((HD, HD), F32),)
    operands = (group, recv, saved, wout) if last else (recv, wout)
    return pl.pallas_call(
        functools.partial(out_kernel, rows, masks, last),
        out_shape=shapes,
        in_specs=[pl.BlockSpec(memory_space=pltpu.SMEM)] * last
        + [vmem] * (len(operands) - last),
        out_specs=(vmem,) * len(shapes),
        compiler_params=pltpu.CompilerParams(vmem_limit_bytes=6 * 2**20),
        cost_estimate=pl.CostEstimate(
            flops=4 * rows * heads * HD * cols, bytes_accessed=2**22, transcendentals=0
        ),
        name="project_out",
    )(*operands)


def pair_kernel(rows, a, b, out):
    total = a[...].astype(F32) + b[...].astype(F32)
    out[...] = total.astype(BF16)
    if out.shape[1] > rows:
        for n in range(2):
            high, low = two_parts(total[n, rows : rows + 1] + total[n, rows + 1 : rows + 2])
            row = lax.broadcasted_iota(jnp.int32, (STATS, out.shape[2]), 0)
            lines = jnp.where(row == 0, high.astype(F32), 0.0)
            lines = jnp.where(row == 1, low.astype(F32), lines)
            out[n, rows:] = lines.astype(BF16)


def add_pair(a, b, rows):
    vmem = pl.BlockSpec(memory_space=VMEM)
    return pl.pallas_call(
        functools.partial(pair_kernel, rows),
        out_shape=jax.ShapeDtypeStruct(a.shape, BF16),
        in_specs=[vmem] * 2,
        out_specs=vmem,
        compiler_params=pltpu.CompilerParams(vmem_limit_bytes=4 * 2**20),
        name="add_pair",
    )(a, b)


def next_kernel(wide0, wide1, same, other, fresh):
    fresh[0] = (
        wide0[...].astype(F32) + (same[0].astype(F32) + other[1].astype(F32))
    ).astype(BF16)
    fresh[1] = (
        wide1[...].astype(F32) + (same[1].astype(F32) + other[0].astype(F32))
    ).astype(BF16)


def add_next(wide0, wide1, same, other):
    vmem = pl.BlockSpec(memory_space=VMEM)
    return pl.pallas_call(
        next_kernel,
        out_shape=jax.ShapeDtypeStruct(same.shape, BF16),
        in_specs=[vmem] * 4,
        out_specs=vmem,
        compiler_params=pltpu.CompilerParams(vmem_limit_bytes=4 * 2**20),
        name="add_next",
    )(wide0, wide1, same, other)


def last_kernel(mine, state, here, there, out, importance):
    rows = mine.shape[0]
    total = here[0].astype(F32) + there[...].astype(F32)
    wide = jnp.where(lax.axis_index("pipe") == 0, mine[...], state[0]).astype(F32)
    out[...] = (wide + total[:rows]).astype(BF16)
    importance[...] = total[rows : rows + 1, :HD] + total[rows + 1 : rows + 2, :HD]


def add_last(mine, state, here, there):
    vmem = pl.BlockSpec(memory_space=VMEM)
    return pl.pallas_call(
        last_kernel,
        out_shape=(
            jax.ShapeDtypeStruct(mine.shape, BF16),
            jax.ShapeDtypeStruct((1, HD), F32),
        ),
        in_specs=[vmem] * 4,
        out_specs=(vmem, vmem),
        compiler_params=pltpu.CompilerParams(vmem_limit_bytes=4 * 2**20),
        name="add_last",
    )(mine, state, here, there)


def swap(block, mask):
    return lax.ppermute(block, "tensor", [(t, t ^ mask) for t in range(N_TENSOR)])


def to_next_section(block, mask):
    route = [(t, N_TENSOR + (t ^ mask)) for t in range(N_TENSOR)]
    return lax.ppermute(block, ("pipe", "tensor"), route)


def local(hidden_in, norm_gain, w_query, w_keyval, w_out, head_group):
    rows, cols = hidden_in.shape[0], hidden_in.shape[3]
    width = cols * N_TENSOR * N_DP
    wq, wout = w_query[0], w_out[0]
    wkv = load(wq, w_keyval[0])
    cosine, sine = map(jnp.asarray, rotary_tables(rows))

    def to_heads(step, pieces, *weights):
        send = project(step, pieces, norm_gain, wkv, wq, *weights)
        recv = lax.all_to_all(send, "dp", 0, 0)
        query, kv, gram = combine(step, recv, cosine, sine, width)
        every = lax.all_gather(kv, "tensor")
        mine = choose(head_group, every.reshape(GROUPS, 16, 2 * HD))
        kv_mine = lax.all_to_all(mine, "dp", 0, 0).reshape(rows, 2 * HD)
        return query, kv_mine, gram

    mine = hidden_in.reshape(rows, cols)
    far = swap(mine, 2)
    query, kv, _ = to_heads(0, (mine, swap(mine, 1), far, swap(mine, 3)))
    att0 = attend(query, kv, wout)
    recv = lax.all_to_all(att0, "dp", 0, 0)
    (other0,) = project_out(recv, wout, rows, (1, 3))
    own0, gram0 = project_out(recv, wout, rows, (0, 2))
    here = add_pair(own0, swap(other0, 1), rows)
    state = add_next(mine, far, to_next_section(here, 0), to_next_section(here, 2))

    query, kv, gram1 = to_heads(1, (state, swap(state, 1)), wout)
    att1 = attend_last(query, kv, att0, gram0, gram1, width)
    recv = lax.all_to_all(att1, "dp", 0, 0)
    (other1,) = project_out(recv, wout, rows, (1, 3), head_group, other0)
    (own1,) = project_out(recv, wout, rows, (0, 2), head_group, own0)
    here = add_pair(own1, swap(other1, 1), rows)
    out, importance = add_last(mine, state, here, swap(here[1], 2))
    return out.reshape(1, rows, 1, 1, cols), importance[:, :GROUPS]


def solution(mesh):
    in_specs = (
        P(None, "dp", "tensor", None),
        P("pipe", "dp"),
        P("pipe", "dp", "tensor"),
        P("pipe", "dp", "tensor", None),
        P("pipe", "tensor", "dp"),
        P(),
    )
    out_specs = (P("pipe", None, "dp", "tensor", None), P("pipe", None))
    return jax.shard_map(local, mesh=mesh, in_specs=in_specs, out_specs=out_specs, check_vma=False)
```

time: 177 us -> 173 us (0.977)
  Pallas kernels: 18.3 us -> 13.4 us
    pallas_call x2, Pallas kernels: 5.46 us -> 1.83 us  [project(): pl.pallas_call(functools.partial(project_kernel, step, len(pieces)), out_...]
    pallas_call x1, Pallas kernels: 0.68 us -> 2.72 us  [attend(): pl.pallas_call(attend_kernel, out_shape=jax.ShapeDtypeStruct((N_DP, rows,...]
    unnamed x17 -> x18, local copies, waits for them, and re-layouts: 3.67 us -> 3.45 us
  transfers between devices with their start and end apart: 9 -> 9, of which waited for: 6 -> 6; matrix products, arithmetic and copies ran while one was open for 0% -> 0% of each run, Pallas kernels for 3% -> 2%
where the time goes in v4:
time: 173 us; the launch traced here: 172 us
  blocking collectives  126 us (73%)
  waiting for transfers between devices  21.5 us (12%)
  Pallas kernels  13.4 us (8%)
  starting transfers between devices  7.16 us (4%)
  local copies, waits for them, and re-layouts  3.46 us (2%)
    all_to_all x2, blocking collectives, to_heads(): recv = lax.all_to_all(send, 'dp', 0, 0)  53 us
    all_to_all x2, blocking collectives, to_heads(): kv_mine = lax.all_to_all(mine, 'dp', 0, 0).reshape(rows, 2 * HD)  21.6 us
    all_to_all x1, blocking collectives, local(): recv = lax.all_to_all(att1, 'dp', 0, 0)  20.5 us
    all_to_all x1, blocking collectives, local(): recv = lax.all_to_all(att0, 'dp', 0, 0)  19.6 us
    ppermute x2, waiting for transfers between devices, to_next_section(): return lax.ppermute(block, ('pipe', 'tensor'), route)  13.3 us
    all_gather x2, blocking collectives, to_heads(): every = lax.all_gather(kv, 'tensor')  10.9 us
    ppermute x7, waiting for transfers between devices, swap(): lax.ppermute(block, 'tensor', [(t, t ^ mask) for t in range(N_TENSOR)])  8.27 us
    ppermute x7, starting transfers between devices, swap(): lax.ppermute(block, 'tensor', [(t, t ^ mask) for t in range(N_TENSOR)])  4.58 us
  transfers between devices with their start and end apart: 9, of which 6 were waited for; matrix products, arithmetic and copies ran while one was open for 0% of the time, Pallas kernels for 2%

profile of v4, /device:TPU:4, one launch (start us, length us, event | category | flops | bytes accessed | tf_op | source)
XLA Modules:
  0.0 172.0 jit_solution(16456663689116326336)
XLA Ops:
  0.6 0.7 collective-permute-start.2
  1.3 0.7 collective-permute-start.1
  2.0 0.8 collective-permute-start
  2.9 2.2 %copy-done.1 = bf16[1,1024,2048]{2,1,0:T(8,128)(2,1)S(1)} copy-done((bf16[1,1024,2048]{2,1,0:T(8,128)(2,1)S(1)}, bf16[1,1024,2048]{2,1,0:T(8,128)(2,1)}, u32[]{:S(2)}) %copy-start.1) | copy-done | bytes 4194328
  5.0 1.2 copy-done.4
  6.3 2.2 %load.1.refs_5_.refs_3_ = bf16[1024,512]{1,0:T(8,128)(2,1)S(1)} custom-call(bf16[1024,2048]{1,0:T(8,128)(2,1)S(1)} %bitcast.18, bf16[1024,2,256]{2,1,0:T(2,128)(2,1)S(1)} %bitcast.29), custom_call_target="tpu_custom_call" | custom-call | flops 1000000000 | bytes 10000000 | tf_op jit(solution)/shard_map/load/pallas_call | solution.py:61
  8.4 0.0 collective-permute-done.2.refs_3_
  8.5 0.0 collective-permute-done.1.refs_1_
  8.5 1.1 collective-permute-done.refs_2_.wide1
  9.5 0.0 copy-done.3
  9.5 0.0 copy-start.5
  9.6 0.0 copy-start.6
  9.6 0.2 project.2
  9.8 0.0 copy-start
  9.8 29.0 %all_to_all.30.recv = bf16[16,336,128]{2,1,0:T(8,128)(2,1)S(1)} all-to-all(bf16[16,336,128]{2,1,0:T(8,128)(2,1)S(1)} %bitcast.22), channel_id=1, replica_groups=mesh['pipe'=2,'tensor'=4,'dp'=16] {'dp'}, dimensions={0} | all-to-all | bytes 2752512 | tf_op jit(solution)/shard_map/all_to_all | solution.py:484
  38.8 0.8 combine.2
  39.6 5.2 %all-gather.kv = bf16[8,16,256]{2,1,0:T(8,128)(2,1)S(1)} all-gather(bf16[2,16,256]{2,1,0:T(8,128)(2,1)S(1)} %get-tuple-element.12), channel_id=2, replica_groups=mesh['pipe'=2,'tensor'=4,'dp'=16] {'tensor'}, dimensions={0}, use_global_device_ids=true | all-gather | bytes 81920 | tf_op jit(solution)/shard_map/all_gather | solution.py:486
  44.9 0.6 choose.2
  45.4 10.8 %all_to_all.31 = bf16[16,16,256]{2,1,0:T(8,128)(2,1)S(1)} all-to-all(bf16[16,16,256]{2,1,0:T(8,128)(2,1)S(1)} %choose.2), channel_id=1, replica_groups=mesh['pipe'=2,'tensor'=4,'dp'=16] {'dp'}, dimensions={0} | all-to-all | bytes 262144 | tf_op jit(solution)/shard_map/all_to_all | solution.py:488
  56.2 2.7 %attend.1.before = bf16[16,256,128]{2,1,0:T(8,128)(2,1)S(1)} custom-call(bf16[256,128]{1,0:T(8,128)(2,1)S(1)} %get-tuple-element.11.query, bf16[256,256]{1,0:T(8,128)(2,1)S(1)} %bitcast.31, bf16[2048,1024]{1,0:T(8,128)(2,1)S(1)} %bitcast.12), custom_call_target="tpu_custom_call" | custom-call | tf_op jit(solution)/shard_map/attend/pallas_call | solution.py:271
  59.0 19.6 %all_to_all.32.refs_0_ = bf16[16,256,128]{2,1,0:T(8,128)(2,1)S(1)} all-to-all(bf16[16,256,128]{2,1,0:T(8,128)(2,1)S(1)} %attend.1.before), channel_id=1, replica_groups=mesh['pipe'=2,'tensor'=4,'dp'=16] {'dp'}, dimensions={0} | all-to-all | bytes 2097152 | tf_op jit(solution)/shard_map/all_to_all | solution.py:495
  78.6 0.1 collective-permute-start.3
  78.7 0.2 project_out.4
  78.9 1.3 collective-permute-done.3.b
  80.3 0.1 add_pair.2
  80.3 1.3 collective-permute-start.5
  81.6 1.3 collective-permute-start.4
  82.9 13.3 %collective-permute-done.5.other = bf16[2,256,256]{2,1,0:T(8,128)(2,1)S(1)} collective-permute-done((bf16[2,256,256]{2,1,0:T(8,128)(2,1)S(1)}, bf16[2,256,256]{2,1,0:T(8,128)(2,1)S(1)}, u32[]{:S(2)}, u32[]{:S(2)}) %collective-permute-start.5) | collective-permute-done | bytes 262176 | tf_op jit(solution)/shard_map/ppermute | solution.py:472
  96.2 0.0 collective-permute-done.4.same
  96.2 0.1 add_next.1.refs_0_.state
  96.3 0.1 collective-permute-start.6
  96.4 1.5 collective-permute-done.6.refs_1_
  97.9 1.6 project.3
  99.5 23.9 %all_to_all.33.recv = bf16[16,336,128]{2,1,0:T(8,128)(2,1)S(1)} all-to-all(bf16[16,336,128]{2,1,0:T(8,128)(2,1)S(1)} %bitcast.21), channel_id=1, replica_groups=mesh['pipe'=2,'tensor'=4,'dp'=16] {'dp'}, dimensions={0} | all-to-all | bytes 2752512 | tf_op jit(solution)/shard_map/all_to_all | solution.py:484
  123.4 0.3 combine.3
  123.8 5.6 %all-gather.1.kv = bf16[8,16,256]{2,1,0:T(8,128)(2,1)S(1)} all-gather(bf16[2,16,256]{2,1,0:T(8,128)(2,1)S(1)} %get-tuple-element.15), channel_id=3, replica_groups=mesh['pipe'=2,'tensor'=4,'dp'=16] {'tensor'}, dimensions={0}, use_global_device_ids=true | all-gather | bytes 81920 | tf_op jit(solution)/shard_map/all_gather | solution.py:486
  129.4 0.6 choose.3
  130.0 10.8 %all_to_all.34 = bf16[16,16,256]{2,1,0:T(8,128)(2,1)S(1)} all-to-all(bf16[16,16,256]{2,1,0:T(8,128)(2,1)S(1)} %choose.3), channel_id=1, replica_groups=mesh['pipe'=2,'tensor'=4,'dp'=16] {'dp'}, dimensions={0} | all-to-all | bytes 262144 | tf_op jit(solution)/shard_map/all_to_all | solution.py:488
  140.8 0.7 attend_last.1
  141.5 20.5 %all_to_all.35.refs_1_ = bf16[16,272,128]{2,1,0:T(8,128)(2,1)S(1)} all-to-all(bf16[16,272,128]{2,1,0:T(8,128)(2,1)S(1)} %attend_last.1), channel_id=1, replica_groups=mesh['pipe'=2,'tensor'=4,'dp'=16] {'dp'}, dimensions={0} | all-to-all | bytes 2228224 | tf_op jit(solution)/shard_map/all_to_all | solution.py:503
  162.0 1.3 project_out.7
  163.3 0.1 collective-permute-start.7
  163.4 1.3 project_out.6.a
  164.8 0.2 collective-permute-done.7.b
  165.0 0.1 add_pair.3.here
  165.1 2.1 %collective-permute-start.8 = (bf16[272,256]{1,0:T(8,128)(2,1)S(1)}, bf16[272,256]{1,0:T(8,128)(2,1)S(1)}, u32[]{:S(2)}, u32[]{:S(2)}) collective-permute-start(bf16[272,256]{1,0:T(8,128)(2,1)S(1)} %slice_bitcast_fusion), channel_id=1, source_target_pairs={{0,32},{16,48},{32,0},{48,16},{1,33},{17,49},{33,1},{49,17},{2,34}... | collective-permute-start | bytes 417800 | tf_op jit(solution)/shard_map/ppermute | solution.py:467
  167.2 4.1 %collective-permute-done.8.there = bf16[272,256]{1,0:T(8,128)(2,1)S(1)} collective-permute-done((bf16[272,256]{1,0:T(8,128)(2,1)S(1)}, bf16[272,256]{1,0:T(8,128)(2,1)S(1)}, u32[]{:S(2)}, u32[]{:S(2)}) %collective-permute-start.8) | collective-permute-done | bytes 139296 | tf_op jit(solution)/shard_map/ppermute | solution.py:467
  171.3 0.7 add_last.1
  (14 shorter events, 0.1 us)
Async XLA Ops:
  0.6 7.8 %collective-permute-start.2 = (bf16[256,256]{1,0:T(8,128)(2,1)}, bf16[256,256]{1,0:T(8,128)(2,1)S(1)}, u32[]{:S(2)}, u32[]{:S(2)}) collective-permute-start(bf16[256,256]{1,0:T(8,128)(2,1)} %bitcast.23), channel_id=1, source_target_pairs={{0,48},{16,32},{32,16},{48,0},{1,49},{17,33},{33,17},{49,1},{2,50}... | collective-permute-start | bytes 393224 | tf_op jit(solution)/shard_map/ppermute | solution.py:467
  1.3 7.1 %collective-permute-start.1 = (bf16[256,256]{1,0:T(8,128)(2,1)}, bf16[256,256]{1,0:T(8,128)(2,1)S(1)}, u32[]{:S(2)}, u32[]{:S(2)}) collective-permute-start(bf16[256,256]{1,0:T(8,128)(2,1)} %bitcast.24), channel_id=1, source_target_pairs={{0,16},{16,0},{32,48},{48,32},{1,17},{17,1},{33,49},{49,33},{2,18}... | collective-permute-start | bytes 393224 | tf_op jit(solution)/shard_map/ppermute | solution.py:467
  2.0 7.5 %collective-permute-start = (bf16[256,256]{1,0:T(8,128)(2,1)}, bf16[256,256]{1,0:T(8,128)(2,1)S(1)}, u32[]{:S(2)}, u32[]{:S(2)}) collective-permute-start(bf16[256,256]{1,0:T(8,128)(2,1)} %bitcast.25), channel_id=1, source_target_pairs={{0,32},{16,48},{32,0},{48,16},{1,33},{17,49},{33,1},{49,17},{2,34}... | collective-permute-start | bytes 393224 | tf_op jit(solution)/shard_map/ppermute | solution.py:467
  2.9 2.2 %copy-start.1 = (bf16[1,1024,2048]{2,1,0:T(8,128)(2,1)S(1)}, bf16[1,1024,2048]{2,1,0:T(8,128)(2,1)}, u32[]{:S(2)}) copy-start(bf16[1,1024,2048]{2,1,0:T(8,128)(2,1)} %param.10) | copy-start | bytes 12582916
  5.0 1.2 copy-start.4
  6.3 3.3 %copy-start.2 = (bf16[1,1024,2048]{2,1,0:T(8,128)(2,1)S(1)}, bf16[1,1024,2048]{2,1,0:T(8,128)(2,1)}, u32[]{:S(2)}) copy-start(bf16[1,1024,2048]{2,1,0:T(8,128)(2,1)} %param.10) | copy-start | bytes 12582916
  6.3 3.3 %copy-start.3 = (bf16[256,1,1,256]{3,0,2,1:T(8,128)(2,1)S(1)}, bf16[256,1,1,256]{3,0,2,1:T(8,128)(2,1)}, u32[]{:S(2)}) copy-start(bf16[256,1,1,256]{3,0,2,1:T(8,128)(2,1)} %param.8) | copy-start | bytes 393220
  6.3 3.3 %copy-start.7 = (bf16[1,1024]{1,0:T(2,128)(2,1)S(1)}, bf16[1,1024]{1,0:T(2,128)(2,1)}, u32[]{:S(2)}) copy-start(bf16[1,1024]{1,0:T(2,128)(2,1)} %refs_2_.1) | copy-start | bytes 6148
  9.5 29.3 %copy-start.5 = (f32[256,128]{1,0:T(8,128)S(1)}, f32[256,128]{1,0:T(8,128)}, u32[]{:S(2)}) copy-start(f32[256,128]{1,0:T(8,128)} %constant.5.clone.sine) | copy-start | bytes 393220
  9.6 29.3 %copy-start.6 = (f32[256,128]{1,0:T(8,128)S(1)}, f32[256,128]{1,0:T(8,128)}, u32[]{:S(2)}) copy-start(f32[256,128]{1,0:T(8,128)} %constant.4.clone.cosine) | copy-start | bytes 393220
  9.8 46.5 %copy-start = (bf16[1,2048,1024]{2,1,0:T(8,128)(2,1)S(1)}, bf16[1,2048,1024]{2,1,0:T(8,128)(2,1)}, u32[]{:S(2)}) copy-start(bf16[1,2048,1024]{2,1,0:T(8,128)(2,1)} %param.12) | copy-start | bytes 12582916
  38.8 6.0 %copy-start.8 = (s32[64]{0:T(128)S(1)}, s32[64]{0:T(128)}, u32[]{:S(2)}) copy-start(s32[64]{0:T(128)} %refs_0_.3) | copy-start | bytes 772
  78.6 1.6 collective-permute-start.3
  80.3 15.9 %collective-permute-start.5 = (bf16[2,256,256]{2,1,0:T(8,128)(2,1)S(1)}, bf16[2,256,256]{2,1,0:T(8,128)(2,1)S(1)}, u32[]{:S(2)}, u32[]{:S(2)}) collective-permute-start(bf16[2,256,256]{2,1,0:T(8,128)(2,1)S(1)} %add_pair.2), channel_id=1, source_target_pairs={{0,96},{16,112},{32,64},{48,80},{1,97},{17,113},{33,65},{49,81},{2... | collective-permute-start | bytes 786440 | tf_op jit(solution)/shard_map/ppermute | solution.py:472
  81.6 14.6 %collective-permute-start.4 = (bf16[2,256,256]{2,1,0:T(8,128)(2,1)S(1)}, bf16[2,256,256]{2,1,0:T(8,128)(2,1)S(1)}, u32[]{:S(2)}, u32[]{:S(2)}) collective-permute-start(bf16[2,256,256]{2,1,0:T(8,128)(2,1)S(1)} %add_pair.2), channel_id=1, source_target_pairs={{0,64},{16,80},{32,96},{48,112},{1,65},{17,81},{33,97},{49,113},{2... | collective-permute-start | bytes 786440 | tf_op jit(solution)/shard_map/ppermute | solution.py:472
  96.3 1.6 collective-permute-start.6
  163.3 1.6 collective-permute-start.7
  165.1 6.2 %collective-permute-start.8 = (bf16[272,256]{1,0:T(8,128)(2,1)S(1)}, bf16[272,256]{1,0:T(8,128)(2,1)S(1)}, u32[]{:S(2)}, u32[]{:S(2)}) collective-permute-start(bf16[272,256]{1,0:T(8,128)(2,1)S(1)} %slice_bitcast_fusion), channel_id=1, source_target_pairs={{0,32},{16,48},{32,0},{48,16},{1,33},{17,49},{33,1},{49,17},{2,34}... | collective-permute-start | bytes 417800 | tf_op jit(solution)/shard_map/ppermute | solution.py:467

commit v5 on v4

--- a/solution.py
+++ b/solution.py
@@ -221,25 +221,43 @@
     )(recv, cosine, sine)
 
 
-def choose_kernel(group, kv, send):
-    for j in range(N_DP):
-        send[j] = kv[group[lax.axis_index("tensor") * N_DP + j]]
-
-
-def choose(group, kv):
+def choose_kernel(group, own, other, send, picked, four):
+    tensor, data = lax.axis_index("tensor"), lax.axis_index("dp")
+    chip, core = tensor // 2, tensor % 2
+    for n in range(2):
+        four[2 * core + n] = own[n]
+        four[2 * (1 - core) + n] = other[n]
+    for d in range(N_DP):
+        for a in range(2):
+            wanted = group[(2 * a + core) * N_DP + d]
+            block = four[wanted % 4]
+            send[2 * d + a] = jnp.where(wanted // 4 == chip, block, jnp.zeros_like(block))
+    lane = lax.broadcasted_iota(jnp.int32, picked.shape, 1)
+    picked[...] = jnp.where(lane == group[tensor * N_DP + data], 1.0, 0.0).astype(F32)
+
+
+def choose(group, own, other):
     vmem = pl.BlockSpec(memory_space=VMEM)
     return pl.pallas_call(
         choose_kernel,
-        out_shape=jax.ShapeDtypeStruct((N_DP,) + kv.shape[1:], BF16),
-        in_specs=[pl.BlockSpec(memory_space=pltpu.SMEM), vmem],
-        out_specs=vmem,
+        out_shape=(
+            jax.ShapeDtypeStruct((2 * N_DP,) + own.shape[1:], BF16),
+            jax.ShapeDtypeStruct((8, HD), F32),
+        ),
+        in_specs=[pl.BlockSpec(memory_space=pltpu.SMEM), vmem, vmem],
+        out_specs=(vmem,) * 2,
+        scratch_shapes=[VMEM((4,) + own.shape[1:], BF16)],
         compiler_params=pltpu.CompilerParams(vmem_limit_bytes=4 * 2**20),
         name="choose",
-    )(group, kv)
-
-
-def attended(query, kv):
+    )(group, own, other)
+
+
+def attended(query, recv, kv):
     rows = query.shape[0]
+    few = rows // N_DP
+    for d in range(N_DP):
+        both = recv[2 * d].astype(F32) + recv[2 * d + 1].astype(F32)
+        kv[d * few : (d + 1) * few, :] = both.astype(BF16)
     scores = lax.dot_general(
         query, kv[:, :HD], (((1,), (1,)), ((), ())), preferred_element_type=F32
     )
@@ -251,12 +269,12 @@
     return jnp.dot(weights, kv[:, HD:], preferred_element_type=F32).astype(BF16)
 
 
-def attend_kernel(query, kv, wout, send):
+def attend_kernel(query, recv, wout, send, kv):
     active = lax.axis_index("pipe") == 0
 
     @pl.when(active)
     def _():
-        result = attended(query[...], kv[...])
+        result = attended(query[...], recv, kv)
         for j in range(N_DP):
             send[j] = result
 
@@ -265,7 +283,7 @@
         gram_parts(wout, lambda h: (send.at[h], 0))
 
 
-def attend(query, kv, wout):
+def attend(query, recv, wout):
     rows = query.shape[0]
     vmem = pl.BlockSpec(memory_space=VMEM)
     return pl.pallas_call(
@@ -273,14 +291,15 @@
         out_shape=jax.ShapeDtypeStruct((N_DP, rows, HD), BF16),
         in_specs=[vmem] * 3,
         out_specs=vmem,
+        scratch_shapes=[VMEM((rows, 2 * HD), BF16)],
         compiler_params=pltpu.CompilerParams(vmem_limit_bytes=8 * 2**20),
         name="attend",
-    )(query, kv, wout)
-
-
-def attend_last_kernel(width, query, kv, before, gram0, gram1, send):
+    )(query, recv, wout)
+
+
+def attend_last_kernel(width, query, recv, before, gram0, gram1, picked, send, kv):
     rows = query.shape[0]
-    result = attended(query[...], kv[...])
+    result = attended(query[...], recv, kv)
     first_section = lax.axis_index("pipe") == 0
     mine = jnp.where(first_section, before[0], result)
     gram = jnp.where(first_section, gram1[...], gram0[...])
@@ -291,7 +310,7 @@
     squares = jnp.sum(image * mine.astype(F32), axis=1, keepdims=True)
     spread = jnp.sqrt(jnp.maximum(squares / width, 0.0) + EPS_RMS)
     mean = jnp.sum(spread, axis=0, keepdims=True) / rows
-    high, low = two_parts(mean)
+    high, low = two_parts(mean * picked[0:1, :])
     row = lax.broadcasted_iota(jnp.int32, (STATS, HD), 0)
     lines = jnp.where(row == 0, high.astype(F32), jnp.where(row == 1, low.astype(F32), 0.0))
     lines = lines.astype(BF16)
@@ -300,22 +319,23 @@
         send[j, rows:] = lines
 
 
-def attend_last(query, kv, before, gram0, gram1, width):
+def attend_last(query, recv, before, gram0, gram1, picked, width):
     rows = query.shape[0]
     vmem = pl.BlockSpec(memory_space=VMEM)
     return pl.pallas_call(
         functools.partial(attend_last_kernel, float(width)),
         out_shape=jax.ShapeDtypeStruct((N_DP, rows + STATS, HD), BF16),
-        in_specs=[vmem] * 5,
+        in_specs=[vmem] * 6,
         out_specs=vmem,
+        scratch_shapes=[VMEM((rows, 2 * HD), BF16)],
         compiler_params=pltpu.CompilerParams(vmem_limit_bytes=8 * 2**20),
         name="attend_last",
-    )(query, kv, before, gram0, gram1)
+    )(query, recv, before, gram0, gram1, picked)
 
 
 def out_kernel(rows, masks, last, *refs):
     if last:
-        group, recv, saved, wout, parts = refs
+        recv, saved, wout, parts = refs
     else:
         recv, wout, parts, *gram = refs
     heads = recv.shape[0]
@@ -323,14 +343,13 @@
     tensor = lax.axis_index("tensor")
     active = lax.axis_index("pipe") == (1 if last else 0)
     if last:
-        lane = lax.broadcasted_iota(jnp.int32, (1, cols), 1)
-        sums = jnp.zeros((1, cols), F32)
+        sums = jnp.zeros((1, HD), F32)
         for h in range(heads):
-            value = recv[h, rows : rows + 1, :].astype(F32) + recv[
-                h, rows + 1 : rows + 2, :
-            ].astype(F32)
-            value = jnp.concatenate([value] * (cols // HD), axis=1)
-            sums = sums + jnp.where(lane == group[tensor * heads + h], value, 0.0)
+            sums = sums + (
+                recv[h, rows : rows + 1, :].astype(F32)
+                + recv[h, rows + 1 : rows + 2, :].astype(F32)
+            )
+        sums = jnp.concatenate([sums, jnp.zeros((1, cols - HD), F32)], axis=1)
         high, low = two_parts(sums)
         row = lax.broadcasted_iota(jnp.int32, (STATS, cols), 0)
         lines = jnp.where(
@@ -372,7 +391,7 @@
             gram[0][...] = jnp.zeros((HD, HD), F32)
 
 
-def project_out(recv, wout, rows, masks, group=None, saved=None):
+def project_out(recv, wout, rows, masks, saved=None):
     heads, deep, _ = recv.shape
     cols = wout.shape[1] // N_TENSOR
     last = saved is not None
@@ -380,12 +399,11 @@
     shapes = (jax.ShapeDtypeStruct((2, deep, cols), BF16),)
     if not last and masks[0] == 0:
         shapes += (jax.ShapeDtypeStruct((HD, HD), F32),)
-    operands = (group, recv, saved, wout) if last else (recv, wout)
+    operands = (recv, saved, wout) if last else (recv, wout)
     return pl.pallas_call(
         functools.partial(out_kernel, rows, masks, last),
         out_shape=shapes,
-        in_specs=[pl.BlockSpec(memory_space=pltpu.SMEM)] * last
-        + [vmem] * (len(operands) - last),
+        in_specs=[vmem] * len(operands),
         out_specs=(vmem,) * len(shapes),
         compiler_params=pltpu.CompilerParams(vmem_limit_bytes=6 * 2**20),
         cost_estimate=pl.CostEstimate(
@@ -395,27 +413,41 @@
     )(*operands)
 
 
-def pair_kernel(rows, a, b, out):
-    total = a[...].astype(F32) + b[...].astype(F32)
-    out[...] = total.astype(BF16)
-    if out.shape[1] > rows:
-        for n in range(2):
-            high, low = two_parts(total[n, rows : rows + 1] + total[n, rows + 1 : rows + 2])
-            row = lax.broadcasted_iota(jnp.int32, (STATS, out.shape[2]), 0)
-            lines = jnp.where(row == 0, high.astype(F32), 0.0)
-            lines = jnp.where(row == 1, low.astype(F32), lines)
-            out[n, rows:] = lines.astype(BF16)
-
-
-def add_pair(a, b, rows):
-    vmem = pl.BlockSpec(memory_space=VMEM)
-    return pl.pallas_call(
-        functools.partial(pair_kernel, rows),
+def pair_kernel(a, b, out):
+    out[...] = (a[...].astype(F32) + b[...].astype(F32)).astype(BF16)
+
+
+def add_pair(a, b):
+    vmem = pl.BlockSpec(memory_space=VMEM)
+    return pl.pallas_call(
+        pair_kernel,
         out_shape=jax.ShapeDtypeStruct(a.shape, BF16),
         in_specs=[vmem] * 2,
         out_specs=vmem,
         compiler_params=pltpu.CompilerParams(vmem_limit_bytes=4 * 2**20),
         name="add_pair",
+    )(a, b)
+
+
+def last_pair_kernel(rows, a, b, out0, out1):
+    for n, out in enumerate((out0, out1)):
+        total = a[n].astype(F32) + b[n].astype(F32)
+        out[:rows] = total[:rows].astype(BF16)
+        high, low = two_parts(total[rows : rows + 1] + total[rows + 1 : rows + 2])
+        row = lax.broadcasted_iota(jnp.int32, (STATS, out.shape[1]), 0)
+        lines = jnp.where(row == 0, high.astype(F32), 0.0)
+        out[rows:] = jnp.where(row == 1, low.astype(F32), lines).astype(BF16)
+
+
+def add_last_pair(a, b, rows):
+    vmem = pl.BlockSpec(memory_space=VMEM)
+    return pl.pallas_call(
+        functools.partial(last_pair_kernel, rows),
+        out_shape=(jax.ShapeDtypeStruct(a.shape[1:], BF16),) * 2,
+        in_specs=[vmem] * 2,
+        out_specs=(vmem,) * 2,
+        compiler_params=pltpu.CompilerParams(vmem_limit_bytes=4 * 2**20),
+        name="add_last_pair",
     )(a, b)
 
 
@@ -442,7 +474,7 @@
 
 def last_kernel(mine, state, here, there, out, importance):
     rows = mine.shape[0]
-    total = here[0].astype(F32) + there[...].astype(F32)
+    total = here[...].astype(F32) + there[...].astype(F32)
     wide = jnp.where(lax.axis_index("pipe") == 0, mine[...], state[0]).astype(F32)
     out[...] = (wide + total[:rows]).astype(BF16)
     importance[...] = total[rows : rows + 1, :HD] + total[rows + 1 : rows + 2, :HD]
@@ -479,32 +511,35 @@
     wkv = load(wq, w_keyval[0])
     cosine, sine = map(jnp.asarray, rotary_tables(rows))
 
+    runs = [
+        [d * N_TENSOR + 2 * a + core for d in range(N_DP) for a in range(2)] for core in range(2)
+    ]
+
     def to_heads(step, pieces, *weights):
         send = project(step, pieces, norm_gain, wkv, wq, *weights)
         recv = lax.all_to_all(send, "dp", 0, 0)
         query, kv, gram = combine(step, recv, cosine, sine, width)
-        every = lax.all_gather(kv, "tensor")
-        mine = choose(head_group, every.reshape(GROUPS, 16, 2 * HD))
-        kv_mine = lax.all_to_all(mine, "dp", 0, 0).reshape(rows, 2 * HD)
-        return query, kv_mine, gram
+        send, picked = choose(head_group, kv, swap(kv, 1))
+        recv = lax.all_to_all(send, ("dp", "tensor"), 0, 0, axis_index_groups=runs)
+        return query, recv, gram, picked
 
     mine = hidden_in.reshape(rows, cols)
     far = swap(mine, 2)
-    query, kv, _ = to_heads(0, (mine, swap(mine, 1), far, swap(mine, 3)))
+    query, kv, _, _ = to_heads(0, (mine, swap(mine, 1), far, swap(mine, 3)))
     att0 = attend(query, kv, wout)
     recv = lax.all_to_all(att0, "dp", 0, 0)
     (other0,) = project_out(recv, wout, rows, (1, 3))
     own0, gram0 = project_out(recv, wout, rows, (0, 2))
-    here = add_pair(own0, swap(other0, 1), rows)
+    here = add_pair(own0, swap(other0, 1))
     state = add_next(mine, far, to_next_section(here, 0), to_next_section(here, 2))
 
-    query, kv, gram1 = to_heads(1, (state, swap(state, 1)), wout)
-    att1 = attend_last(query, kv, att0, gram0, gram1, width)
+    query, kv, gram1, picked = to_heads(1, (state, swap(state, 1)), wout)
+    att1 = attend_last(query, kv, att0, gram0, gram1, picked, width)
     recv = lax.all_to_all(att1, "dp", 0, 0)
-    (other1,) = project_out(recv, wout, rows, (1, 3), head_group, other0)
-    (own1,) = project_out(recv, wout, rows, (0, 2), head_group, own0)
-    here = add_pair(own1, swap(other1, 1), rows)
-    out, importance = add_last(mine, state, here, swap(here[1], 2))
+    (other1,) = project_out(recv, wout, rows, (1, 3), other0)
+    (own1,) = project_out(recv, wout, rows, (0, 2), own0)
+    here, away = add_last_pair(own1, swap(other1, 1), rows)
+    out, importance = add_last(mine, state, here, swap(away, 2))
     return out.reshape(1, rows, 1, 1, cols), importance[:, :GROUPS]
 
 

time: 173 us -> 170 us (0.983)
  blocking collectives: 126 us -> 120 us
  waiting for transfers between devices: 21.5 us -> 25.5 us
    all_gather x2 -> x0, blocking collectives: 10.9 us -> none  [to_heads(): every = lax.all_gather(kv, 'tensor')]
    all_to_all x2, blocking collectives: 21.6 us -> 27.4 us  [to_heads(): recv = lax.all_to_all(send, ('dp', 'tensor'), 0, 0, axis_index_groups=runs)]
    ppermute x7 -> x9, waiting for transfers between devices: 8.27 us -> 12.3 us  [swap(): lax.ppermute(block, 'tensor', [(t, t ^ mask) for t in range(N_TENSOR)])]
    ppermute x7 -> x9, starting transfers between devices: 4.58 us -> 3.12 us  [swap(): lax.ppermute(block, 'tensor', [(t, t ^ mask) for t in range(N_TENSOR)])]
  transfers between devices with their start and end apart: 9 -> 11, of which waited for: 6 -> 8; matrix products, arithmetic and copies ran while one was open for 0% -> 0% of each run, Pallas kernels for 2% -> 2%
where the time goes in v5:
time: 170 us; the launch traced here: 169 us
  blocking collectives  120 us (71%)
  waiting for transfers between devices  25.5 us (15%)
  Pallas kernels  13.5 us (8%)
  starting transfers between devices  5.7 us (3%)
  local copies, waits for them, and re-layouts  3.45 us (2%)
    all_to_all x2, blocking collectives, to_heads(): recv = lax.all_to_all(send, 'dp', 0, 0)  52.9 us
    all_to_all x2, blocking collectives, to_heads(): recv = lax.all_to_all(send, ('dp', 'tensor'), 0, 0, axis_index_groups=runs)  27.4 us
    all_to_all x1, blocking collectives, local(): recv = lax.all_to_all(att1, 'dp', 0, 0)  20.2 us
    all_to_all x1, blocking collectives, local(): recv = lax.all_to_all(att0, 'dp', 0, 0)  19.5 us
    ppermute x2, waiting for transfers between devices, to_next_section(): return lax.ppermute(block, ('pipe', 'tensor'), route)  13.3 us
    ppermute x9, waiting for transfers between devices, swap(): lax.ppermute(block, 'tensor', [(t, t ^ mask) for t in range(N_TENSOR)])  12.3 us
    unnamed x18, local copies, waits for them, and re-layouts  3.45 us
  transfers between devices with their start and end apart: 11, of which 8 were waited for; matrix products, arithmetic and copies ran while one was open for 0% of the time, Pallas kernels for 2%

profile of v5, /device:TPU:4, one launch (start us, length us, event | category | flops | bytes accessed | tf_op | source)
XLA Modules:
  0.0 169.1 jit_solution(1591394288379573153)
XLA Ops:
  0.6 0.7 collective-permute-start.2
  1.3 0.7 collective-permute-start.1
  2.0 0.8 collective-permute-start
  2.9 2.2 %copy-done.1 = bf16[1,1024,2048]{2,1,0:T(8,128)(2,1)S(1)} copy-done((bf16[1,1024,2048]{2,1,0:T(8,128)(2,1)S(1)}, bf16[1,1024,2048]{2,1,0:T(8,128)(2,1)}, u32[]{:S(2)}) %copy-start.1) | copy-done | bytes 4194328
  5.0 1.2 copy-done.4
  6.3 2.2 %load.1.refs_5_.refs_3_ = bf16[1024,512]{1,0:T(8,128)(2,1)S(1)} custom-call(bf16[1024,2048]{1,0:T(8,128)(2,1)S(1)} %bitcast.14, bf16[1024,2,256]{2,1,0:T(2,128)(2,1)S(1)} %bitcast.25), custom_call_target="tpu_custom_call" | custom-call | flops 1000000000 | bytes 10000000 | tf_op jit(solution)/shard_map/load/pallas_call | solution.py:61
  8.4 0.0 collective-permute-done.2.refs_3_
  8.5 0.0 collective-permute-done.1.refs_1_
  8.5 1.1 collective-permute-done.refs_2_.wide1
  9.5 0.0 copy-start.5
  9.6 0.0 copy-start.6
  9.6 0.2 project.2
  9.8 0.0 copy-start
  9.8 29.0 %all_to_all.30.recv = bf16[16,336,128]{2,1,0:T(8,128)(2,1)S(1)} all-to-all(bf16[16,336,128]{2,1,0:T(8,128)(2,1)S(1)} %bitcast.18), channel_id=1, replica_groups=mesh['pipe'=2,'tensor'=4,'dp'=16] {'dp'}, dimensions={0} | all-to-all | bytes 2752512 | tf_op jit(solution)/shard_map/all_to_all | solution.py:520
  38.8 0.8 combine.2
  39.6 0.0 collective-permute-start.3
  39.6 1.2 collective-permute-done.3.other
  40.8 1.4 choose.2
  42.2 13.5 %all_to_all.31.recv = bf16[32,16,256]{2,1,0:T(8,128)(2,1)S(1)} all-to-all(bf16[32,16,256]{2,1,0:T(8,128)(2,1)S(1)} %get-tuple-element.18), channel_id=1, replica_groups={{0,32,1,33,2,34,3,35,4,36,5,37,6,38,7,39,8,40,9,41,10,42,11,43,12,44,13..., dimensions={0} | all-to-all | bytes 524288 | tf_op jit(solution)/shard_map/all_to_all | solution.py:523
  55.6 2.7 %attend.1.before = bf16[16,256,128]{2,1,0:T(8,128)(2,1)S(1)} custom-call(bf16[256,128]{1,0:T(8,128)(2,1)S(1)} %get-tuple-element.16.query, bf16[32,16,256]{2,1,0:T(8,128)(2,1)S(1)} %all_to_all.31.recv, bf16[2048,1024]{1,0:T(8,128)(2,1)S(1)} %bitcast.8), custom_call_target="tpu_custom_call" | custom-call | tf_op jit(solution)/shard_map/attend/pallas_call | solution.py:289
  58.4 19.5 %all_to_all.32.refs_0_ = bf16[16,256,128]{2,1,0:T(8,128)(2,1)S(1)} all-to-all(bf16[16,256,128]{2,1,0:T(8,128)(2,1)S(1)} %attend.1.before), channel_id=1, replica_groups=mesh['pipe'=2,'tensor'=4,'dp'=16] {'dp'}, dimensions={0} | all-to-all | bytes 2097152 | tf_op jit(solution)/shard_map/all_to_all | solution.py:530
  77.9 0.1 collective-permute-start.4
  78.0 0.2 project_out.4
  78.2 1.3 collective-permute-done.4.b
  79.5 0.1 add_pair.1
  79.6 1.3 collective-permute-start.6
  80.9 1.3 collective-permute-start.5
  82.2 13.3 %collective-permute-done.6.other = bf16[2,256,256]{2,1,0:T(8,128)(2,1)S(1)} collective-permute-done((bf16[2,256,256]{2,1,0:T(8,128)(2,1)S(1)}, bf16[2,256,256]{2,1,0:T(8,128)(2,1)S(1)}, u32[]{:S(2)}, u32[]{:S(2)}) %collective-permute-start.6) | collective-permute-done | bytes 262176 | tf_op jit(solution)/shard_map/ppermute | solution.py:504
  95.5 0.1 add_next.1.refs_0_.state
  95.6 0.1 collective-permute-start.7
  95.6 1.5 collective-permute-done.7.refs_1_
  97.2 1.6 project.3
  98.8 23.9 %all_to_all.33.recv = bf16[16,336,128]{2,1,0:T(8,128)(2,1)S(1)} all-to-all(bf16[16,336,128]{2,1,0:T(8,128)(2,1)S(1)} %bitcast.17), channel_id=1, replica_groups=mesh['pipe'=2,'tensor'=4,'dp'=16] {'dp'}, dimensions={0} | all-to-all | bytes 2752512 | tf_op jit(solution)/shard_map/all_to_all | solution.py:520
  122.7 0.5 combine.3
  123.1 0.1 collective-permute-start.8
  123.2 1.2 collective-permute-done.8.other
  124.4 0.8 choose.3
  125.2 14.0 %all_to_all.34.recv = bf16[32,16,256]{2,1,0:T(8,128)(2,1)S(1)} all-to-all(bf16[32,16,256]{2,1,0:T(8,128)(2,1)S(1)} %get-tuple-element.22), channel_id=1, replica_groups={{0,32,1,33,2,34,3,35,4,36,5,37,6,38,7,39,8,40,9,41,10,42,11,43,12,44,13..., dimensions={0} | all-to-all | bytes 524288 | tf_op jit(solution)/shard_map/all_to_all | solution.py:523
  139.2 0.7 attend_last.1
  139.9 20.2 %all_to_all.35.refs_0_ = bf16[16,272,128]{2,1,0:T(8,128)(2,1)S(1)} all-to-all(bf16[16,272,128]{2,1,0:T(8,128)(2,1)S(1)} %attend_last.1), channel_id=1, replica_groups=mesh['pipe'=2,'tensor'=4,'dp'=16] {'dp'}, dimensions={0} | all-to-all | bytes 2228224 | tf_op jit(solution)/shard_map/all_to_all | solution.py:538
  160.2 0.8 project_out.7
  160.9 0.1 collective-permute-start.9
  161.0 0.8 project_out.6.a
  161.8 0.8 collective-permute-done.9.b
  162.6 0.1 add_last_pair.1
  162.6 0.6 collective-permute-start.10
  163.2 5.2 %collective-permute-done.10.there = bf16[272,256]{1,0:T(8,128)(2,1)S(1)} collective-permute-done((bf16[272,256]{1,0:T(8,128)(2,1)S(1)}, bf16[272,256]{1,0:T(8,128)(2,1)S(1)}, u32[]{:S(2)}, u32[]{:S(2)}) %collective-permute-start.10) | collective-permute-done | bytes 139296 | tf_op jit(solution)/shard_map/ppermute | solution.py:499
  168.4 0.7 add_last.1
  (15 shorter events, 0.0 us)
Async XLA Ops:
  0.6 7.8 %collective-permute-start.2 = (bf16[256,256]{1,0:T(8,128)(2,1)}, bf16[256,256]{1,0:T(8,128)(2,1)S(1)}, u32[]{:S(2)}, u32[]{:S(2)}) collective-permute-start(bf16[256,256]{1,0:T(8,128)(2,1)} %bitcast.19), channel_id=1, source_target_pairs={{0,48},{16,32},{32,16},{48,0},{1,49},{17,33},{33,17},{49,1},{2,50}... | collective-permute-start | bytes 393224 | tf_op jit(solution)/shard_map/ppermute | solution.py:499
  1.3 7.1 %collective-permute-start.1 = (bf16[256,256]{1,0:T(8,128)(2,1)}, bf16[256,256]{1,0:T(8,128)(2,1)S(1)}, u32[]{:S(2)}, u32[]{:S(2)}) collective-permute-start(bf16[256,256]{1,0:T(8,128)(2,1)} %bitcast.20), channel_id=1, source_target_pairs={{0,16},{16,0},{32,48},{48,32},{1,17},{17,1},{33,49},{49,33},{2,18}... | collective-permute-start | bytes 393224 | tf_op jit(solution)/shard_map/ppermute | solution.py:499
  2.0 7.5 %collective-permute-start = (bf16[256,256]{1,0:T(8,128)(2,1)}, bf16[256,256]{1,0:T(8,128)(2,1)S(1)}, u32[]{:S(2)}, u32[]{:S(2)}) collective-permute-start(bf16[256,256]{1,0:T(8,128)(2,1)} %bitcast.21), channel_id=1, source_target_pairs={{0,32},{16,48},{32,0},{48,16},{1,33},{17,49},{33,1},{49,17},{2,34}... | collective-permute-start | bytes 393224 | tf_op jit(solution)/shard_map/ppermute | solution.py:499
  2.9 2.2 %copy-start.1 = (bf16[1,1024,2048]{2,1,0:T(8,128)(2,1)S(1)}, bf16[1,1024,2048]{2,1,0:T(8,128)(2,1)}, u32[]{:S(2)}) copy-start(bf16[1,1024,2048]{2,1,0:T(8,128)(2,1)} %param.10) | copy-start | bytes 12582916
  5.0 1.2 copy-start.4
  6.3 3.3 %copy-start.2 = (bf16[1,1024,2048]{2,1,0:T(8,128)(2,1)S(1)}, bf16[1,1024,2048]{2,1,0:T(8,128)(2,1)}, u32[]{:S(2)}) copy-start(bf16[1,1024,2048]{2,1,0:T(8,128)(2,1)} %param.10) | copy-start | bytes 12582916
  6.3 3.3 %copy-start.3 = (bf16[256,1,1,256]{3,0,2,1:T(8,128)(2,1)S(1)}, bf16[256,1,1,256]{3,0,2,1:T(8,128)(2,1)}, u32[]{:S(2)}) copy-start(bf16[256,1,1,256]{3,0,2,1:T(8,128)(2,1)} %param.8) | copy-start | bytes 393220
  6.3 3.3 %copy-start.7 = (bf16[1,1024]{1,0:T(2,128)(2,1)S(1)}, bf16[1,1024]{1,0:T(2,128)(2,1)}, u32[]{:S(2)}) copy-start(bf16[1,1024]{1,0:T(2,128)(2,1)} %refs_2_.1) | copy-start | bytes 6148
  9.5 29.3 %copy-start.5 = (f32[256,128]{1,0:T(8,128)S(1)}, f32[256,128]{1,0:T(8,128)}, u32[]{:S(2)}) copy-start(f32[256,128]{1,0:T(8,128)} %constant.5.clone.sine) | copy-start | bytes 393220
  9.6 29.3 %copy-start.6 = (f32[256,128]{1,0:T(8,128)S(1)}, f32[256,128]{1,0:T(8,128)}, u32[]{:S(2)}) copy-start(f32[256,128]{1,0:T(8,128)} %constant.4.clone.cosine) | copy-start | bytes 393220
  9.8 45.9 %copy-start = (bf16[1,2048,1024]{2,1,0:T(8,128)(2,1)S(1)}, bf16[1,2048,1024]{2,1,0:T(8,128)(2,1)}, u32[]{:S(2)}) copy-start(bf16[1,2048,1024]{2,1,0:T(8,128)(2,1)} %param.12) | copy-start | bytes 12582916
  38.8 2.0 %copy-start.8 = (s32[64]{0:T(128)S(1)}, s32[64]{0:T(128)}, u32[]{:S(2)}) copy-start(s32[64]{0:T(128)} %group.3) | copy-start | bytes 772
  39.6 1.2 collective-permute-start.3
  77.9 1.6 collective-permute-start.4
  79.6 15.9 %collective-permute-start.6 = (bf16[2,256,256]{2,1,0:T(8,128)(2,1)S(1)}, bf16[2,256,256]{2,1,0:T(8,128)(2,1)S(1)}, u32[]{:S(2)}, u32[]{:S(2)}) collective-permute-start(bf16[2,256,256]{2,1,0:T(8,128)(2,1)S(1)} %add_pair.1), channel_id=1, source_target_pairs={{0,96},{16,112},{32,64},{48,80},{1,97},{17,113},{33,65},{49,81},{2... | collective-permute-start | bytes 786440 | tf_op jit(solution)/shard_map/ppermute | solution.py:504
  80.9 14.6 %collective-permute-start.5 = (bf16[2,256,256]{2,1,0:T(8,128)(2,1)S(1)}, bf16[2,256,256]{2,1,0:T(8,128)(2,1)S(1)}, u32[]{:S(2)}, u32[]{:S(2)}) collective-permute-start(bf16[2,256,256]{2,1,0:T(8,128)(2,1)S(1)} %add_pair.1), channel_id=1, source_target_pairs={{0,64},{16,80},{32,96},{48,112},{1,65},{17,81},{33,97},{49,113},{2... | collective-permute-start | bytes 786440 | tf_op jit(solution)/shard_map/ppermute | solution.py:504
  95.6 1.6 collective-permute-start.7
  123.1 1.3 collective-permute-start.8
  160.9 1.6 collective-permute-start.9
  162.6 5.8 %collective-permute-start.10 = (bf16[272,256]{1,0:T(8,128)(2,1)S(1)}, bf16[272,256]{1,0:T(8,128)(2,1)S(1)}, u32[]{:S(2)}, u32[]{:S(2)}) collective-permute-start(bf16[272,256]{1,0:T(8,128)(2,1)S(1)} %get-tuple-element.27), channel_id=1, source_target_pairs={{0,32},{16,48},{32,0},{48,16},{1,33},{17,49},{33,1},{49,17},{2,34}... | collective-permute-start | bytes 417800 | tf_op jit(solution)/shard_map/ppermute | solution.py:499

commit v6 on v5

--- a/solution.py
+++ b/solution.py
@@ -413,17 +413,18 @@
     )(*operands)
 
 
-def pair_kernel(a, b, out):
-    out[...] = (a[...].astype(F32) + b[...].astype(F32)).astype(BF16)
+def pair_kernel(a, b, out0, out1):
+    for n, out in enumerate((out0, out1)):
+        out[...] = (a[n].astype(F32) + b[n].astype(F32)).astype(BF16)
 
 
 def add_pair(a, b):
     vmem = pl.BlockSpec(memory_space=VMEM)
     return pl.pallas_call(
         pair_kernel,
-        out_shape=jax.ShapeDtypeStruct(a.shape, BF16),
+        out_shape=(jax.ShapeDtypeStruct(a.shape[1:], BF16),) * 2,
         in_specs=[vmem] * 2,
-        out_specs=vmem,
+        out_specs=(vmem,) * 2,
         compiler_params=pltpu.CompilerParams(vmem_limit_bytes=4 * 2**20),
         name="add_pair",
     )(a, b)
@@ -451,31 +452,28 @@
     )(a, b)
 
 
-def next_kernel(wide0, wide1, same, other, fresh):
-    fresh[0] = (
-        wide0[...].astype(F32) + (same[0].astype(F32) + other[1].astype(F32))
+def next_kernel(wide, here, there, fresh):
+    fresh[...] = (
+        wide[...].astype(F32) + (here[...].astype(F32) + there[...].astype(F32))
     ).astype(BF16)
-    fresh[1] = (
-        wide1[...].astype(F32) + (same[1].astype(F32) + other[0].astype(F32))
-    ).astype(BF16)
-
-
-def add_next(wide0, wide1, same, other):
+
+
+def add_next(wide, here, there):
     vmem = pl.BlockSpec(memory_space=VMEM)
     return pl.pallas_call(
         next_kernel,
-        out_shape=jax.ShapeDtypeStruct(same.shape, BF16),
-        in_specs=[vmem] * 4,
+        out_shape=jax.ShapeDtypeStruct(wide.shape, BF16),
+        in_specs=[vmem] * 3,
         out_specs=vmem,
         compiler_params=pltpu.CompilerParams(vmem_limit_bytes=4 * 2**20),
         name="add_next",
-    )(wide0, wide1, same, other)
+    )(wide, here, there)
 
 
 def last_kernel(mine, state, here, there, out, importance):
     rows = mine.shape[0]
     total = here[...].astype(F32) + there[...].astype(F32)
-    wide = jnp.where(lax.axis_index("pipe") == 0, mine[...], state[0]).astype(F32)
+    wide = jnp.where(lax.axis_index("pipe") == 0, mine[...], state[...]).astype(F32)
     out[...] = (wide + total[:rows]).astype(BF16)
     importance[...] = total[rows : rows + 1, :HD] + total[rows + 1 : rows + 2, :HD]
 
@@ -495,8 +493,13 @@
     )(mine, state, here, there)
 
 
-def swap(block, mask):
-    return lax.ppermute(block, "tensor", [(t, t ^ mask) for t in range(N_TENSOR)])
+def swap(block, *masks):
+    route = [
+        (p * N_TENSOR + t, p * N_TENSOR + (t ^ masks[min(p, len(masks) - 1)]))
+        for p in range(2)
+        for t in range(N_TENSOR)
+    ]
+    return lax.ppermute(block, ("pipe", "tensor"), route)
 
 
 def to_next_section(block, mask):
@@ -524,22 +527,24 @@
         return query, recv, gram, picked
 
     mine = hidden_in.reshape(rows, cols)
-    far = swap(mine, 2)
-    query, kv, _, _ = to_heads(0, (mine, swap(mine, 1), far, swap(mine, 3)))
+    pieces = (mine, swap(mine, 1), swap(mine, 2, 1), swap(mine, 3, 1))
+    query, kv, _, _ = to_heads(0, pieces)
     att0 = attend(query, kv, wout)
     recv = lax.all_to_all(att0, "dp", 0, 0)
     (other0,) = project_out(recv, wout, rows, (1, 3))
     own0, gram0 = project_out(recv, wout, rows, (0, 2))
-    here = add_pair(own0, swap(other0, 1))
-    state = add_next(mine, far, to_next_section(here, 0), to_next_section(here, 2))
-
-    query, kv, gram1, picked = to_heads(1, (state, swap(state, 1)), wout)
+    here, away = add_pair(own0, swap(other0, 1))
+    fresh = add_next(mine, here, swap(away, 2, 1))
+    far = to_next_section(fresh, 2)
+    near = to_next_section(fresh, 0)
+
+    query, kv, gram1, picked = to_heads(1, (near, swap(near, 1), far, swap(far, 1)), wout)
     att1 = attend_last(query, kv, att0, gram0, gram1, picked, width)
     recv = lax.all_to_all(att1, "dp", 0, 0)
     (other1,) = project_out(recv, wout, rows, (1, 3), other0)
     (own1,) = project_out(recv, wout, rows, (0, 2), own0)
     here, away = add_last_pair(own1, swap(other1, 1), rows)
-    out, importance = add_last(mine, state, here, swap(away, 2))
+    out, importance = add_last(mine, near, here, swap(away, 2))
     return out.reshape(1, rows, 1, 1, cols), importance[:, :GROUPS]
 
 

time: 170 us -> 167 us (0.982)
  waiting for transfers between devices: 25.5 us -> 22.7 us
    ppermute x2, waiting for transfers between devices: 13.3 us -> 10.7 us  [to_next_section(): return lax.ppermute(block, ('pipe', 'tensor'), route)]
    ppermute x9 -> x11, waiting for transfers between devices: 12.3 us -> 11.9 us  [swap(): return lax.ppermute(block, ('pipe', 'tensor'), route)]
  transfers between devices with their start and end apart: 11 -> 13, of which waited for: 8 -> 9; matrix products, arithmetic and copies ran while one was open for 0% -> 0% of each run, Pallas kernels for 2% -> 2%
where the time goes in v6:
time: 167 us; the launch traced here: 166 us
  blocking collectives  121 us (72%)
  waiting for transfers between devices  22.7 us (14%)
  Pallas kernels  13.3 us (8%)
  starting transfers between devices  4.79 us (3%)
  local copies, waits for them, and re-layouts  3.45 us (2%)
    all_to_all x2, blocking collectives, to_heads(): recv = lax.all_to_all(send, 'dp', 0, 0)  53.7 us
    all_to_all x2, blocking collectives, to_heads(): recv = lax.all_to_all(send, ('dp', 'tensor'), 0, 0, axis_index_groups=runs)  27.9 us
    all_to_all x1, blocking collectives, local(): recv = lax.all_to_all(att1, 'dp', 0, 0)  20.2 us
    all_to_all x1, blocking collectives, local(): recv = lax.all_to_all(att0, 'dp', 0, 0)  19.5 us
    ppermute x11, waiting for transfers between devices, swap(): return lax.ppermute(block, ('pipe', 'tensor'), route)  11.9 us
    ppermute x2, waiting for transfers between devices, to_next_section(): return lax.ppermute(block, ('pipe', 'tensor'), route)  10.7 us
    unnamed x18, local copies, waits for them, and re-layouts  3.45 us
  transfers between devices with their start and end apart: 13, of which 9 were waited for; matrix products, arithmetic and copies ran while one was open for 0% of the time, Pallas kernels for 2%

profile of v6, /device:TPU:4, one launch (start us, length us, event | category | flops | bytes accessed | tf_op | source)
XLA Modules:
  0.0 166.4 jit_solution(18302604850535810969)
XLA Ops:
  0.6 0.1 collective-permute-start.2
  0.7 0.5 collective-permute-start.1
  1.2 0.1 collective-permute-start
  1.3 2.2 %copy-done.1 = bf16[1,1024,2048]{2,1,0:T(8,128)(2,1)S(1)} copy-done((bf16[1,1024,2048]{2,1,0:T(8,128)(2,1)S(1)}, bf16[1,1024,2048]{2,1,0:T(8,128)(2,1)}, u32[]{:S(2)}) %copy-start.1) | copy-done | bytes 4194328
  3.5 1.2 copy-done.4
  4.7 2.2 %load.1.refs_5_ = bf16[1024,512]{1,0:T(8,128)(2,1)S(1)} custom-call(bf16[1024,2048]{1,0:T(8,128)(2,1)S(1)} %bitcast.14, bf16[1024,2,256]{2,1,0:T(2,128)(2,1)S(1)} %bitcast.25), custom_call_target="tpu_custom_call" | custom-call | flops 1000000000 | bytes 10000000 | tf_op jit(solution)/shard_map/load/pallas_call | solution.py:61
  6.9 0.0 collective-permute-done.2.refs_3_
  7.0 0.0 copy-start.5
  7.0 0.0 copy-start.6
  7.0 0.2 project.2
  7.2 0.0 copy-start
  7.2 29.4 %all_to_all.30.recv = bf16[16,336,128]{2,1,0:T(8,128)(2,1)S(1)} all-to-all(bf16[16,336,128]{2,1,0:T(8,128)(2,1)S(1)} %bitcast.18), channel_id=1, replica_groups=mesh['pipe'=2,'tensor'=4,'dp'=16] {'dp'}, dimensions={0} | all-to-all | bytes 2752512 | tf_op jit(solution)/shard_map/all_to_all | solution.py:523
  36.6 0.8 combine.2
  37.4 1.2 collective-permute-done.3.other
  38.6 1.4 choose.2
  40.0 13.5 %all_to_all.31.recv = bf16[32,16,256]{2,1,0:T(8,128)(2,1)S(1)} all-to-all(bf16[32,16,256]{2,1,0:T(8,128)(2,1)S(1)} %get-tuple-element.20), channel_id=1, replica_groups={{0,32,1,33,2,34,3,35,4,36,5,37,6,38,7,39,8,40,9,41,10,42,11,43,12,44,13..., dimensions={0} | all-to-all | bytes 524288 | tf_op jit(solution)/shard_map/all_to_all | solution.py:526
  53.4 2.7 %attend.1.before = bf16[16,256,128]{2,1,0:T(8,128)(2,1)S(1)} custom-call(bf16[256,128]{1,0:T(8,128)(2,1)S(1)} %get-tuple-element.18.query, bf16[32,16,256]{2,1,0:T(8,128)(2,1)S(1)} %all_to_all.31.recv, bf16[2048,1024]{1,0:T(8,128)(2,1)S(1)} %bitcast.8), custom_call_target="tpu_custom_call" | custom-call | tf_op jit(solution)/shard_map/attend/pallas_call | solution.py:289
  56.2 19.5 %all_to_all.32.refs_0_ = bf16[16,256,128]{2,1,0:T(8,128)(2,1)S(1)} all-to-all(bf16[16,256,128]{2,1,0:T(8,128)(2,1)S(1)} %attend.1.before), channel_id=1, replica_groups=mesh['pipe'=2,'tensor'=4,'dp'=16] {'dp'}, dimensions={0} | all-to-all | bytes 2097152 | tf_op jit(solution)/shard_map/all_to_all | solution.py:533
  75.7 0.1 collective-permute-start.4
  75.8 0.2 project_out.4
  76.0 1.3 collective-permute-done.4.b
  77.3 0.1 add_pair.1
  77.4 0.2 collective-permute-start.5
  77.6 1.2 collective-permute-done.5.there
  78.8 0.1 add_next.1
  78.9 1.3 collective-permute-start.8
  80.2 1.3 collective-permute-start.6
  81.5 10.7 %collective-permute-done.8.refs_2_ = bf16[256,256]{1,0:T(8,128)(2,1)S(1)} collective-permute-done((bf16[256,256]{1,0:T(8,128)(2,1)S(1)}, bf16[256,256]{1,0:T(8,128)(2,1)S(1)}, u32[]{:S(2)}, u32[]{:S(2)}) %collective-permute-start.8) | collective-permute-done | bytes 131104 | tf_op jit(solution)/shard_map/ppermute | solution.py:507
  92.2 0.5 collective-permute-start.7
  92.7 0.8 collective-permute-done.9.refs_3_
  93.5 0.2 collective-permute-done.7.refs_1_
  93.7 1.6 project.3
  95.4 24.3 %all_to_all.33.recv = bf16[16,336,128]{2,1,0:T(8,128)(2,1)S(1)} all-to-all(bf16[16,336,128]{2,1,0:T(8,128)(2,1)S(1)} %bitcast.17), channel_id=1, replica_groups=mesh['pipe'=2,'tensor'=4,'dp'=16] {'dp'}, dimensions={0} | all-to-all | bytes 2752512 | tf_op jit(solution)/shard_map/all_to_all | solution.py:523
  119.6 0.3 combine.3
  119.9 0.1 collective-permute-start.10
  120.0 1.2 collective-permute-done.10.other
  121.2 0.8 choose.3
  122.0 14.4 %all_to_all.34.recv = bf16[32,16,256]{2,1,0:T(8,128)(2,1)S(1)} all-to-all(bf16[32,16,256]{2,1,0:T(8,128)(2,1)S(1)} %get-tuple-element.26), channel_id=1, replica_groups={{0,32,1,33,2,34,3,35,4,36,5,37,6,38,7,39,8,40,9,41,10,42,11,43,12,44,13..., dimensions={0} | all-to-all | bytes 524288 | tf_op jit(solution)/shard_map/all_to_all | solution.py:526
  136.4 0.7 attend_last.1
  137.1 20.2 %all_to_all.35.refs_0_ = bf16[16,272,128]{2,1,0:T(8,128)(2,1)S(1)} all-to-all(bf16[16,272,128]{2,1,0:T(8,128)(2,1)S(1)} %attend_last.1), channel_id=1, replica_groups=mesh['pipe'=2,'tensor'=4,'dp'=16] {'dp'}, dimensions={0} | all-to-all | bytes 2228224 | tf_op jit(solution)/shard_map/all_to_all | solution.py:543
  157.4 0.8 project_out.7
  158.2 0.1 collective-permute-start.11
  158.3 0.8 project_out.6.a
  159.0 0.8 collective-permute-done.11.b
  159.8 0.1 add_last_pair.1
  159.9 0.5 collective-permute-start.12
  160.4 5.2 %collective-permute-done.12.there = bf16[272,256]{1,0:T(8,128)(2,1)S(1)} collective-permute-done((bf16[272,256]{1,0:T(8,128)(2,1)S(1)}, bf16[272,256]{1,0:T(8,128)(2,1)S(1)}, u32[]{:S(2)}, u32[]{:S(2)}) %collective-permute-start.12) | collective-permute-done | bytes 139296 | tf_op jit(solution)/shard_map/ppermute | solution.py:502
  165.7 0.7 add_last.1
  (19 shorter events, 0.1 us)
Async XLA Ops:
  0.6 6.3 %collective-permute-start.2 = (bf16[256,256]{1,0:T(8,128)(2,1)}, bf16[256,256]{1,0:T(8,128)(2,1)S(1)}, u32[]{:S(2)}, u32[]{:S(2)}) collective-permute-start(bf16[256,256]{1,0:T(8,128)(2,1)} %bitcast.19), channel_id=1, source_target_pairs={{0,48},{16,32},{32,16},{48,0},{64,80},{80,64},{96,112},{112,96},{1... | collective-permute-start | bytes 393224 | tf_op jit(solution)/shard_map/ppermute | solution.py:502
  0.7 6.2 %collective-permute-start.1 = (bf16[256,256]{1,0:T(8,128)(2,1)}, bf16[256,256]{1,0:T(8,128)(2,1)S(1)}, u32[]{:S(2)}, u32[]{:S(2)}) collective-permute-start(bf16[256,256]{1,0:T(8,128)(2,1)} %bitcast.20), channel_id=1, source_target_pairs={{0,32},{16,48},{32,0},{48,16},{64,80},{80,64},{96,112},{112,96},{1... | collective-permute-start | bytes 393224 | tf_op jit(solution)/shard_map/ppermute | solution.py:502
  1.2 5.7 %collective-permute-start = (bf16[256,256]{1,0:T(8,128)(2,1)}, bf16[256,256]{1,0:T(8,128)(2,1)S(1)}, u32[]{:S(2)}, u32[]{:S(2)}) collective-permute-start(bf16[256,256]{1,0:T(8,128)(2,1)} %bitcast.21), channel_id=1, source_target_pairs={{0,16},{16,0},{32,48},{48,32},{64,80},{80,64},{96,112},{112,96},{1... | collective-permute-start | bytes 393224 | tf_op jit(solution)/shard_map/ppermute | solution.py:502
  1.3 2.2 %copy-start.1 = (bf16[1,1024,2048]{2,1,0:T(8,128)(2,1)S(1)}, bf16[1,1024,2048]{2,1,0:T(8,128)(2,1)}, u32[]{:S(2)}) copy-start(bf16[1,1024,2048]{2,1,0:T(8,128)(2,1)} %param.10) | copy-start | bytes 12582916
  3.5 1.2 copy-start.4
  4.7 2.2 %copy-start.2 = (bf16[1,1024,2048]{2,1,0:T(8,128)(2,1)S(1)}, bf16[1,1024,2048]{2,1,0:T(8,128)(2,1)}, u32[]{:S(2)}) copy-start(bf16[1,1024,2048]{2,1,0:T(8,128)(2,1)} %param.10) | copy-start | bytes 12582916
  4.7 2.2 %copy-start.3 = (bf16[256,1,1,256]{3,0,2,1:T(8,128)(2,1)S(1)}, bf16[256,1,1,256]{3,0,2,1:T(8,128)(2,1)}, u32[]{:S(2)}) copy-start(bf16[256,1,1,256]{3,0,2,1:T(8,128)(2,1)} %param.8) | copy-start | bytes 393220
  4.7 2.2 %copy-start.7 = (bf16[1,1024]{1,0:T(2,128)(2,1)S(1)}, bf16[1,1024]{1,0:T(2,128)(2,1)}, u32[]{:S(2)}) copy-start(bf16[1,1024]{1,0:T(2,128)(2,1)} %refs_4_.3) | copy-start | bytes 6148
  7.0 29.7 %copy-start.5 = (f32[256,128]{1,0:T(8,128)S(1)}, f32[256,128]{1,0:T(8,128)}, u32[]{:S(2)}) copy-start(f32[256,128]{1,0:T(8,128)} %constant.5.clone.sine) | copy-start | bytes 393220
  7.0 29.7 %copy-start.6 = (f32[256,128]{1,0:T(8,128)S(1)}, f32[256,128]{1,0:T(8,128)}, u32[]{:S(2)}) copy-start(f32[256,128]{1,0:T(8,128)} %constant.4.clone.cosine) | copy-start | bytes 393220
  7.2 46.2 %copy-start = (bf16[1,2048,1024]{2,1,0:T(8,128)(2,1)S(1)}, bf16[1,2048,1024]{2,1,0:T(8,128)(2,1)}, u32[]{:S(2)}) copy-start(bf16[1,2048,1024]{2,1,0:T(8,128)(2,1)} %param.12) | copy-start | bytes 12582916
  36.6 2.0 %copy-start.8 = (s32[64]{0:T(128)S(1)}, s32[64]{0:T(128)}, u32[]{:S(2)}) copy-start(s32[64]{0:T(128)} %group.3) | copy-start | bytes 772
  37.4 1.2 collective-permute-start.3
  75.7 1.6 collective-permute-start.4
  77.4 1.4 collective-permute-start.5
  78.9 13.3 %collective-permute-start.8 = (bf16[256,256]{1,0:T(8,128)(2,1)S(1)}, bf16[256,256]{1,0:T(8,128)(2,1)S(1)}, u32[]{:S(2)}, u32[]{:S(2)}) collective-permute-start(bf16[256,256]{1,0:T(8,128)(2,1)S(1)} %add_next.1), channel_id=1, source_target_pairs={{0,96},{16,112},{32,64},{48,80},{1,97},{17,113},{33,65},{49,81},{2... | collective-permute-start | bytes 393224 | tf_op jit(solution)/shard_map/ppermute | solution.py:507
  80.2 12.0 %collective-permute-start.6 = (bf16[256,256]{1,0:T(8,128)(2,1)S(1)}, bf16[256,256]{1,0:T(8,128)(2,1)S(1)}, u32[]{:S(2)}, u32[]{:S(2)}) collective-permute-start(bf16[256,256]{1,0:T(8,128)(2,1)S(1)} %add_next.1), channel_id=1, source_target_pairs={{0,64},{16,80},{32,96},{48,112},{1,65},{17,81},{33,97},{49,113},{2... | collective-permute-start | bytes 393224 | tf_op jit(solution)/shard_map/ppermute | solution.py:507
  92.2 1.3 collective-permute-start.9
  92.2 1.5 collective-permute-start.7
  119.9 1.3 collective-permute-start.10
  158.2 1.6 collective-permute-start.11
  159.9 5.8 %collective-permute-start.12 = (bf16[272,256]{1,0:T(8,128)(2,1)S(1)}, bf16[272,256]{1,0:T(8,128)(2,1)S(1)}, u32[]{:S(2)}, u32[]{:S(2)}) collective-permute-start(bf16[272,256]{1,0:T(8,128)(2,1)S(1)} %get-tuple-element.31), channel_id=1, source_target_pairs={{0,32},{16,48},{32,0},{48,16},{64,96},{80,112},{96,64},{112,80},{1... | collective-permute-start | bytes 417800 | tf_op jit(solution)/shard_map/ppermute | solution.py:502

commit v7 on v6

--- a/solution.py
+++ b/solution.py
@@ -50,23 +50,37 @@
     return high, (values - high.astype(F32)).astype(BF16)
 
 
-def load_kernel(wq, wkv, out):
-    cols = wkv.shape[2]
-    for g in range(wkv.shape[1]):
-        out[:, g * cols : (g + 1) * cols] = wkv[:, g, :]
-
-
-def load(wq, wkv):
-    vmem = pl.BlockSpec(memory_space=VMEM)
-    return pl.pallas_call(
-        load_kernel,
-        out_shape=jax.ShapeDtypeStruct((wkv.shape[0], wkv.shape[1] * wkv.shape[2]), BF16),
-        in_specs=[vmem] * 2,
+def ready_kernel(gain, wq, wkv, out):
+    out[...] = jnp.zeros_like(out)
+
+
+def ready(gain, wq, wkv):
+    vmem = pl.BlockSpec(memory_space=VMEM)
+    return pl.pallas_call(
+        ready_kernel,
+        out_shape=jax.ShapeDtypeStruct((16, HD), BF16),
+        in_specs=[vmem] * 3,
         out_specs=vmem,
         compiler_params=pltpu.CompilerParams(vmem_limit_bytes=12 * 2**20),
         cost_estimate=pl.CostEstimate(flops=10**9, bytes_accessed=10**7, transcendentals=0),
-        name="load",
-    )(wq, wkv)
+        name="ready",
+    )(gain, wq, wkv)
+
+
+def hand_on_kernel(block, tile, out):
+    out[...] = block[...]
+
+
+def hand_on(block, tile):
+    vmem = pl.BlockSpec(memory_space=VMEM)
+    return pl.pallas_call(
+        hand_on_kernel,
+        out_shape=jax.ShapeDtypeStruct(block.shape, BF16),
+        in_specs=[vmem] * 2,
+        out_specs=vmem,
+        compiler_params=pltpu.CompilerParams(vmem_limit_bytes=2 * 2**20),
+        name="hand_on",
+    )(block, tile)
 
 
 def gram_parts(wout, target):
@@ -511,7 +525,7 @@
     rows, cols = hidden_in.shape[0], hidden_in.shape[3]
     width = cols * N_TENSOR * N_DP
     wq, wout = w_query[0], w_out[0]
-    wkv = load(wq, w_keyval[0])
+    wkv = w_keyval[0].reshape(wq.shape[0], -1)
     cosine, sine = map(jnp.asarray, rotary_tables(rows))
 
     runs = [
@@ -527,7 +541,8 @@
         return query, recv, gram, picked
 
     mine = hidden_in.reshape(rows, cols)
-    pieces = (mine, swap(mine, 1), swap(mine, 2, 1), swap(mine, 3, 1))
+    far = hand_on(swap(mine, 2, 1), ready(norm_gain, wq, wkv))
+    pieces = (mine, swap(mine, 1), far, swap(far, 1))
     query, kv, _, _ = to_heads(0, pieces)
     att0 = attend(query, kv, wout)
     recv = lax.all_to_all(att0, "dp", 0, 0)

time: 167 us -> 165 us (0.988)
  Pallas kernels: 13.3 us -> 11.2 us
    pallas_call x1 -> x2, Pallas kernels: 2.17 us -> 0.01 us  [the longest x1 0.01 us: hand_on(): pl.pallas_call(hand_on_kernel, out_shape=jax.ShapeDtypeStruct(block.shape...]
    unnamed x18 -> x17, local copies, waits for them, and re-layouts: 3.45 us -> 4.39 us
  transfers between devices with their start and end apart: 13 -> 13, of which waited for: 9 -> 10; matrix products, arithmetic and copies ran while one was open for 0% -> 1% of each run, Pallas kernels for 2% -> 1%
where the time goes in v7:
time: 165 us; the launch traced here: 164 us
  blocking collectives  121 us (73%)
  waiting for transfers between devices  22.3 us (14%)
  Pallas kernels  11.2 us (7%)
  starting transfers between devices  4.87 us (3%)
  local copies, waits for them, and re-layouts  4.39 us (3%)
    all_to_all x2, blocking collectives, to_heads(): recv = lax.all_to_all(send, 'dp', 0, 0)  53.1 us
    all_to_all x2, blocking collectives, to_heads(): recv = lax.all_to_all(send, ('dp', 'tensor'), 0, 0, axis_index_groups=runs)  28 us
    all_to_all x1, blocking collectives, local(): recv = lax.all_to_all(att1, 'dp', 0, 0)  20.2 us
    all_to_all x1, blocking collectives, local(): recv = lax.all_to_all(att0, 'dp', 0, 0)  19.5 us
    ppermute x11, waiting for transfers between devices, swap(): return lax.ppermute(block, ('pipe', 'tensor'), route)  13.2 us
    ppermute x2, waiting for transfers between devices, to_next_section(): return lax.ppermute(block, ('pipe', 'tensor'), route)  9.12 us
    unnamed x17, local copies, waits for them, and re-layouts  4.39 us
  transfers between devices with their start and end apart: 13, of which 10 were waited for; matrix products, arithmetic and copies ran while one was open for 1% of the time, Pallas kernels for 1%

profile of v7, /device:TPU:4, one launch (start us, length us, event | category | flops | bytes accessed | tf_op | source)
XLA Modules:
  0.0 164.5 jit_solution(5628976654994238781)
XLA Ops:
  0.6 0.1 collective-permute-start.1
  0.7 0.5 collective-permute-start
  1.2 1.4 copy.10
  2.7 0.0 copy-start.1
  2.7 2.2 %copy-done.1 = bf16[1,1024,2048]{2,1,0:T(8,128)(2,1)S(1)} copy-done((bf16[1,1024,2048]{2,1,0:T(8,128)(2,1)S(1)}, bf16[1,1024,2048]{2,1,0:T(8,128)(2,1)}, u32[]{:S(2)}) %copy-start.1) | copy-done | bytes 4194328
  4.9 0.0 collective-permute-done.1.block
  4.9 0.2 collective-permute-start.2
  5.1 1.2 collective-permute-done.2.refs_3_
  6.3 0.7 copy-done.2
  7.1 0.2 project.2
  7.3 0.0 copy-start
  7.3 29.0 %all_to_all.30.recv = bf16[16,336,128]{2,1,0:T(8,128)(2,1)S(1)} all-to-all(bf16[16,336,128]{2,1,0:T(8,128)(2,1)S(1)} %bitcast.23), channel_id=1, replica_groups=mesh['pipe'=2,'tensor'=4,'dp'=16] {'dp'}, dimensions={0} | all-to-all | bytes 2752512 | tf_op jit(solution)/shard_map/all_to_all | solution.py:537
  36.3 0.8 combine.2
  37.1 1.2 collective-permute-done.3.other
  38.3 1.4 choose.2
  39.7 13.5 %all_to_all.31.recv = bf16[32,16,256]{2,1,0:T(8,128)(2,1)S(1)} all-to-all(bf16[32,16,256]{2,1,0:T(8,128)(2,1)S(1)} %get-tuple-element.20), channel_id=1, replica_groups={{0,32,1,33,2,34,3,35,4,36,5,37,6,38,7,39,8,40,9,41,10,42,11,43,12,44,13..., dimensions={0} | all-to-all | bytes 524288 | tf_op jit(solution)/shard_map/all_to_all | solution.py:540
  53.2 2.7 %attend.1.before = bf16[16,256,128]{2,1,0:T(8,128)(2,1)S(1)} custom-call(bf16[256,128]{1,0:T(8,128)(2,1)S(1)} %get-tuple-element.18.query, bf16[32,16,256]{2,1,0:T(8,128)(2,1)S(1)} %all_to_all.31.recv, bf16[2048,1024]{1,0:T(8,128)(2,1)S(1)} %bitcast.10), custom_call_target="tpu_custom_call" | custom-call | tf_op jit(solution)/shard_map/attend/pallas_call | solution.py:303
  55.9 19.5 %all_to_all.32.refs_0_ = bf16[16,256,128]{2,1,0:T(8,128)(2,1)S(1)} all-to-all(bf16[16,256,128]{2,1,0:T(8,128)(2,1)S(1)} %attend.1.before), channel_id=1, replica_groups=mesh['pipe'=2,'tensor'=4,'dp'=16] {'dp'}, dimensions={0} | all-to-all | bytes 2097152 | tf_op jit(solution)/shard_map/all_to_all | solution.py:548
  75.4 0.1 collective-permute-start.4
  75.5 0.2 project_out.4
  75.7 1.3 collective-permute-done.4.b
  77.0 0.1 add_pair.1
  77.1 0.2 collective-permute-start.5
  77.3 1.2 collective-permute-done.5.there
  78.5 0.1 add_next.1
  78.6 1.3 collective-permute-start.8
  79.9 1.3 collective-permute-start.6
  81.2 9.1 %collective-permute-done.8.refs_2_ = bf16[256,256]{1,0:T(8,128)(2,1)S(1)} collective-permute-done((bf16[256,256]{1,0:T(8,128)(2,1)S(1)}, bf16[256,256]{1,0:T(8,128)(2,1)S(1)}, u32[]{:S(2)}, u32[]{:S(2)}) %collective-permute-start.8) | collective-permute-done | bytes 131104 | tf_op jit(solution)/shard_map/ppermute | solution.py:521
  90.3 0.5 collective-permute-start.7
  90.8 0.8 collective-permute-done.9.refs_3_
  91.6 0.2 collective-permute-done.7.refs_1_
  91.8 1.6 project.3
  93.5 24.1 %all_to_all.33.recv = bf16[16,336,128]{2,1,0:T(8,128)(2,1)S(1)} all-to-all(bf16[16,336,128]{2,1,0:T(8,128)(2,1)S(1)} %bitcast.22), channel_id=1, replica_groups=mesh['pipe'=2,'tensor'=4,'dp'=16] {'dp'}, dimensions={0} | all-to-all | bytes 2752512 | tf_op jit(solution)/shard_map/all_to_all | solution.py:537
  117.5 0.3 combine.3
  117.9 0.1 collective-permute-start.10
  117.9 1.2 collective-permute-done.10.other
  119.1 0.8 choose.3
  119.9 14.6 %all_to_all.34.recv = bf16[32,16,256]{2,1,0:T(8,128)(2,1)S(1)} all-to-all(bf16[32,16,256]{2,1,0:T(8,128)(2,1)S(1)} %get-tuple-element.26), channel_id=1, replica_groups={{0,32,1,33,2,34,3,35,4,36,5,37,6,38,7,39,8,40,9,41,10,42,11,43,12,44,13..., dimensions={0} | all-to-all | bytes 524288 | tf_op jit(solution)/shard_map/all_to_all | solution.py:540
  134.5 0.7 attend_last.1
  135.2 20.2 %all_to_all.35.refs_0_ = bf16[16,272,128]{2,1,0:T(8,128)(2,1)S(1)} all-to-all(bf16[16,272,128]{2,1,0:T(8,128)(2,1)S(1)} %attend_last.1), channel_id=1, replica_groups=mesh['pipe'=2,'tensor'=4,'dp'=16] {'dp'}, dimensions={0} | all-to-all | bytes 2228224 | tf_op jit(solution)/shard_map/all_to_all | solution.py:558
  155.5 0.8 project_out.7
  156.2 0.1 collective-permute-start.11
  156.3 0.8 project_out.6.a
  157.1 0.8 collective-permute-done.11.b
  157.9 0.1 add_last_pair.1
  157.9 0.5 collective-permute-start.12
  158.5 5.2 %collective-permute-done.12.there = bf16[272,256]{1,0:T(8,128)(2,1)S(1)} collective-permute-done((bf16[272,256]{1,0:T(8,128)(2,1)S(1)}, bf16[272,256]{1,0:T(8,128)(2,1)S(1)}, u32[]{:S(2)}, u32[]{:S(2)}) %collective-permute-start.12) | collective-permute-done | bytes 139296 | tf_op jit(solution)/shard_map/ppermute | solution.py:516
  163.7 0.7 add_last.1
  (19 shorter events, 0.1 us)
Async XLA Ops:
  0.6 2.1 %copy-start.6 = (bf16[1,1024]{1,0:T(2,128)(2,1)S(1)}, bf16[1,1024]{1,0:T(2,128)(2,1)}, u32[]{:S(2)}) copy-start(bf16[1,1024]{1,0:T(2,128)(2,1)} %refs_4_.3) | copy-start | bytes 6148
  0.6 4.3 %collective-permute-start.1 = (bf16[256,256]{1,0:T(8,128)(2,1)}, bf16[256,256]{1,0:T(8,128)(2,1)S(1)}, u32[]{:S(2)}, u32[]{:S(2)}) collective-permute-start(bf16[256,256]{1,0:T(8,128)(2,1)} %bitcast.24), channel_id=1, source_target_pairs={{0,32},{16,48},{32,0},{48,16},{64,80},{80,64},{96,112},{112,96},{1... | collective-permute-start | bytes 393224 | tf_op jit(solution)/shard_map/ppermute | solution.py:516
  0.7 4.4 %collective-permute-start = (bf16[256,256]{1,0:T(8,128)(2,1)}, bf16[256,256]{1,0:T(8,128)(2,1)S(1)}, u32[]{:S(2)}, u32[]{:S(2)}) collective-permute-start(bf16[256,256]{1,0:T(8,128)(2,1)} %bitcast.25), channel_id=1, source_target_pairs={{0,16},{16,0},{32,48},{48,32},{64,80},{80,64},{96,112},{112,96},{1... | collective-permute-start | bytes 393224 | tf_op jit(solution)/shard_map/ppermute | solution.py:516
  2.7 2.2 %copy-start.1 = (bf16[1,1024,2048]{2,1,0:T(8,128)(2,1)S(1)}, bf16[1,1024,2048]{2,1,0:T(8,128)(2,1)}, u32[]{:S(2)}) copy-start(bf16[1,1024,2048]{2,1,0:T(8,128)(2,1)} %param.10) | copy-start | bytes 12582916
  4.9 2.2 %copy-start.2 = (bf16[1,1024,2048]{2,1,0:T(8,128)(2,1)S(1)}, bf16[1,1024,2048]{2,1,0:T(8,128)(2,1)}, u32[]{:S(2)}) copy-start(bf16[1,1024,2048]{2,1,0:T(8,128)(2,1)} %param.10) | copy-start | bytes 12582916
  4.9 2.2 %copy-start.3 = (bf16[256,1,1,256]{3,0,2,1:T(8,128)(2,1)S(1)}, bf16[256,1,1,256]{3,0,2,1:T(8,128)(2,1)}, u32[]{:S(2)}) copy-start(bf16[256,1,1,256]{3,0,2,1:T(8,128)(2,1)} %param.8) | copy-start | bytes 393220
  4.9 1.4 collective-permute-start.2
  7.1 29.3 %copy-start.4 = (f32[256,128]{1,0:T(8,128)S(1)}, f32[256,128]{1,0:T(8,128)}, u32[]{:S(2)}) copy-start(f32[256,128]{1,0:T(8,128)} %constant.5.clone.sine) | copy-start | bytes 393220
  7.1 29.3 %copy-start.5 = (f32[256,128]{1,0:T(8,128)S(1)}, f32[256,128]{1,0:T(8,128)}, u32[]{:S(2)}) copy-start(f32[256,128]{1,0:T(8,128)} %constant.4.clone.cosine) | copy-start | bytes 393220
  7.3 45.9 %copy-start = (bf16[1,2048,1024]{2,1,0:T(8,128)(2,1)S(1)}, bf16[1,2048,1024]{2,1,0:T(8,128)(2,1)}, u32[]{:S(2)}) copy-start(bf16[1,2048,1024]{2,1,0:T(8,128)(2,1)} %param.12) | copy-start | bytes 12582916
  36.3 2.0 %copy-start.7 = (s32[64]{0:T(128)S(1)}, s32[64]{0:T(128)}, u32[]{:S(2)}) copy-start(s32[64]{0:T(128)} %group.3) | copy-start | bytes 772
  37.1 1.2 collective-permute-start.3
  75.4 1.6 collective-permute-start.4
  77.1 1.4 collective-permute-start.5
  78.6 11.7 %collective-permute-start.8 = (bf16[256,256]{1,0:T(8,128)(2,1)S(1)}, bf16[256,256]{1,0:T(8,128)(2,1)S(1)}, u32[]{:S(2)}, u32[]{:S(2)}) collective-permute-start(bf16[256,256]{1,0:T(8,128)(2,1)S(1)} %add_next.1), channel_id=1, source_target_pairs={{0,96},{16,112},{32,64},{48,80},{1,97},{17,113},{33,65},{49,81},{2... | collective-permute-start | bytes 393224 | tf_op jit(solution)/shard_map/ppermute | solution.py:521
  79.9 10.4 %collective-permute-start.6 = (bf16[256,256]{1,0:T(8,128)(2,1)S(1)}, bf16[256,256]{1,0:T(8,128)(2,1)S(1)}, u32[]{:S(2)}, u32[]{:S(2)}) collective-permute-start(bf16[256,256]{1,0:T(8,128)(2,1)S(1)} %add_next.1), channel_id=1, source_target_pairs={{0,64},{16,80},{32,96},{48,112},{1,65},{17,81},{33,97},{49,113},{2... | collective-permute-start | bytes 393224 | tf_op jit(solution)/shard_map/ppermute | solution.py:521
  90.3 1.3 collective-permute-start.9
  90.3 1.5 collective-permute-start.7
  117.9 1.3 collective-permute-start.10
  156.2 1.6 collective-permute-start.11
  157.9 5.8 %collective-permute-start.12 = (bf16[272,256]{1,0:T(8,128)(2,1)S(1)}, bf16[272,256]{1,0:T(8,128)(2,1)S(1)}, u32[]{:S(2)}, u32[]{:S(2)}) collective-permute-start(bf16[272,256]{1,0:T(8,128)(2,1)S(1)} %get-tuple-element.31), channel_id=1, source_target_pairs={{0,32},{16,48},{32,0},{48,16},{64,96},{80,112},{96,64},{112,80},{1... | collective-permute-start | bytes 417800 | tf_op jit(solution)/shard_map/ppermute | solution.py:516

commit v8 on v7

--- a/solution.py
+++ b/solution.py
@@ -50,21 +50,22 @@
     return high, (values - high.astype(F32)).astype(BF16)
 
 
-def ready_kernel(gain, wq, wkv, out):
+def ready_kernel(*refs):
+    out = refs[-1]
     out[...] = jnp.zeros_like(out)
 
 
-def ready(gain, wq, wkv):
+def ready(*arrays):
     vmem = pl.BlockSpec(memory_space=VMEM)
     return pl.pallas_call(
         ready_kernel,
         out_shape=jax.ShapeDtypeStruct((16, HD), BF16),
-        in_specs=[vmem] * 3,
+        in_specs=[vmem] * len(arrays),
         out_specs=vmem,
         compiler_params=pltpu.CompilerParams(vmem_limit_bytes=12 * 2**20),
         cost_estimate=pl.CostEstimate(flops=10**9, bytes_accessed=10**7, transcendentals=0),
         name="ready",
-    )(gain, wq, wkv)
+    )(*arrays)
 
 
 def hand_on_kernel(block, tile, out):
@@ -177,7 +178,8 @@
     return send.reshape(N_DP, pitch, HD)
 
 
-def combine_kernel(step, width, recv, cosine, sine, query, kv, gram, scale):
+def combine_kernel(step, width, recv, cosine, sine, query, kv, *rest):
+    *gram, scale = rest
     rows = cosine.shape[0]
     active = lax.axis_index("pipe") == step
 
@@ -208,11 +210,13 @@
             vals = tail[32 * g + 16 : 32 * g + 32] * here
             kv[g, :, :HD] = rotated(keys, cos_here, sin_here).astype(BF16)
             kv[g, :, HD:] = vals.astype(BF16)
-        gram[...] = jnp.zeros_like(gram)
+        for ref in gram:
+            ref[...] = jnp.zeros_like(ref)
 
     @pl.when(jnp.logical_not(active))
     def _():
-        gram[...] = total(0, HD) + total(HD, HD)
+        for ref in gram:
+            ref[...] = total(0, HD) + total(HD, HD)
         query[...] = jnp.zeros_like(query)
         kv[...] = jnp.zeros_like(kv)
 
@@ -220,22 +224,24 @@
 def combine(step, recv, cosine, sine, width):
     rows = cosine.shape[0]
     vmem = pl.BlockSpec(memory_space=VMEM)
+    shapes = (
+        jax.ShapeDtypeStruct((rows, HD), BF16),
+        jax.ShapeDtypeStruct((2, 16, 2 * HD), BF16),
+        jax.ShapeDtypeStruct((HD, HD), F32),
+    )[: 2 + step]
     return pl.pallas_call(
         functools.partial(combine_kernel, step, float(width)),
-        out_shape=(
-            jax.ShapeDtypeStruct((rows, HD), BF16),
-            jax.ShapeDtypeStruct((2, 16, 2 * HD), BF16),
-            jax.ShapeDtypeStruct((HD, HD), F32),
-        ),
+        out_shape=shapes,
         in_specs=[vmem] * 3,
-        out_specs=(vmem, vmem, vmem),
+        out_specs=(vmem,) * len(shapes),
         scratch_shapes=[VMEM((rows, HD), F32)],
         compiler_params=pltpu.CompilerParams(vmem_limit_bytes=8 * 2**20),
         name="combine",
     )(recv, cosine, sine)
 
 
-def choose_kernel(group, own, other, send, picked, four):
+def choose_kernel(group, own, other, send, *rest):
+    *picked, four = rest
     tensor, data = lax.axis_index("tensor"), lax.axis_index("dp")
     chip, core = tensor // 2, tensor % 2
     for n in range(2):
@@ -246,20 +252,22 @@
             wanted = group[(2 * a + core) * N_DP + d]
             block = four[wanted % 4]
             send[2 * d + a] = jnp.where(wanted // 4 == chip, block, jnp.zeros_like(block))
-    lane = lax.broadcasted_iota(jnp.int32, picked.shape, 1)
-    picked[...] = jnp.where(lane == group[tensor * N_DP + data], 1.0, 0.0).astype(F32)
-
-
-def choose(group, own, other):
-    vmem = pl.BlockSpec(memory_space=VMEM)
+    for ref in picked:
+        lane = lax.broadcasted_iota(jnp.int32, ref.shape, 1)
+        ref[...] = jnp.where(lane == group[tensor * N_DP + data], 1.0, 0.0).astype(F32)
+
+
+def choose(step, group, own, other):
+    vmem = pl.BlockSpec(memory_space=VMEM)
+    shapes = (
+        jax.ShapeDtypeStruct((2 * N_DP,) + own.shape[1:], BF16),
+        jax.ShapeDtypeStruct((8, HD), F32),
+    )[: 1 + step]
     return pl.pallas_call(
         choose_kernel,
-        out_shape=(
-            jax.ShapeDtypeStruct((2 * N_DP,) + own.shape[1:], BF16),
-            jax.ShapeDtypeStruct((8, HD), F32),
-        ),
+        out_shape=shapes,
         in_specs=[pl.BlockSpec(memory_space=pltpu.SMEM), vmem, vmem],
-        out_specs=(vmem,) * 2,
+        out_specs=(vmem,) * len(shapes),
         scratch_shapes=[VMEM((4,) + own.shape[1:], BF16)],
         compiler_params=pltpu.CompilerParams(vmem_limit_bytes=4 * 2**20),
         name="choose",
@@ -535,15 +543,16 @@
     def to_heads(step, pieces, *weights):
         send = project(step, pieces, norm_gain, wkv, wq, *weights)
         recv = lax.all_to_all(send, "dp", 0, 0)
-        query, kv, gram = combine(step, recv, cosine, sine, width)
-        send, picked = choose(head_group, kv, swap(kv, 1))
+        query, kv, *gram = combine(step, recv, cosine, sine, width)
+        send, *picked = choose(step, head_group, kv, swap(kv, 1))
         recv = lax.all_to_all(send, ("dp", "tensor"), 0, 0, axis_index_groups=runs)
-        return query, recv, gram, picked
+        return query, recv, *gram, *picked
 
     mine = hidden_in.reshape(rows, cols)
-    far = hand_on(swap(mine, 2, 1), ready(norm_gain, wq, wkv))
+    tile = ready(mine, norm_gain, wkv, cosine, sine, head_group)
+    far = hand_on(swap(mine, 2, 1), tile)
     pieces = (mine, swap(mine, 1), far, swap(far, 1))
-    query, kv, _, _ = to_heads(0, pieces)
+    query, kv = to_heads(0, pieces)
     att0 = attend(query, kv, wout)
     recv = lax.all_to_all(att0, "dp", 0, 0)
     (other0,) = project_out(recv, wout, rows, (1, 3))

time: 165 us -> 164 us (level)
  waiting for transfers between devices: 22.3 us -> 25.1 us
  local copies, waits for them, and re-layouts: 4.39 us -> 1.63 us
    ppermute x2, waiting for transfers between devices: 9.12 us -> 11.9 us  [to_next_section(): return lax.ppermute(block, ('pipe', 'tensor'), route)]
    unnamed x17 -> x15, local copies, waits for them, and re-layouts: 4.39 us -> 1.63 us
where the time goes in v8:
time: 164 us; the launch traced here: 163 us
  blocking collectives  121 us (74%)
  waiting for transfers between devices  25.1 us (15%)
  Pallas kernels  9.8 us (6%)
  starting transfers between devices  4.95 us (3%)
    all_to_all x2, blocking collectives, to_heads(): recv = lax.all_to_all(send, 'dp', 0, 0)  53.2 us
    all_to_all x2, blocking collectives, to_heads(): recv = lax.all_to_all(send, ('dp', 'tensor'), 0, 0, axis_index_groups=runs)  27.9 us
    all_to_all x1, blocking collectives, local(): recv = lax.all_to_all(att1, 'dp', 0, 0)  20.2 us
    all_to_all x1, blocking collectives, local(): recv = lax.all_to_all(att0, 'dp', 0, 0)  19.5 us
    ppermute x11, waiting for transfers between devices, swap(): return lax.ppermute(block, ('pipe', 'tensor'), route)  13.2 us
    ppermute x2, waiting for transfers between devices, to_next_section(): return lax.ppermute(block, ('pipe', 'tensor'), route)  11.9 us
  transfers between devices with their start and end apart: 13, of which 10 were waited for; matrix products, arithmetic and copies ran while one was open for 1% of the time, Pallas kernels for 1%

profile of v8, /device:TPU:4, one launch (start us, length us, event | category | flops | bytes accessed | tf_op | source)
XLA Modules:
  0.0 163.2 jit_solution(16265634657659286660)
XLA Ops:
  0.6 0.0 copy-start.3
  0.6 0.0 copy-start.4
  0.7 0.1 collective-permute-start.1
  0.8 0.5 collective-permute-start
  1.3 1.6 copy.10
  2.9 0.0 collective-permute-done.1.block
  3.0 0.2 collective-permute-start.2
  3.1 0.0 collective-permute-done.refs_1_
  3.2 1.3 collective-permute-done.2.refs_3_
  4.4 0.2 project.2
  4.6 0.0 copy-start
  4.6 29.1 %all_to_all.30.recv = bf16[16,336,128]{2,1,0:T(8,128)(2,1)S(1)} all-to-all(bf16[16,336,128]{2,1,0:T(8,128)(2,1)S(1)} %bitcast.22), channel_id=1, replica_groups=mesh['pipe'=2,'tensor'=4,'dp'=16] {'dp'}, dimensions={0} | all-to-all | bytes 2752512 | tf_op jit(solution)/shard_map/all_to_all | solution.py:545
  33.7 0.1 collective-permute-start.3
  33.8 1.2 collective-permute-done.3.other
  35.0 0.8 choose.2
  35.8 13.5 %all_to_all.31.recv = bf16[32,16,256]{2,1,0:T(8,128)(2,1)S(1)} all-to-all(bf16[32,16,256]{2,1,0:T(8,128)(2,1)S(1)} %choose.2), channel_id=1, replica_groups={{0,32,1,33,2,34,3,35,4,36,5,37,6,38,7,39,8,40,9,41,10,42,11,43,12,44,13..., dimensions={0} | all-to-all | bytes 524288 | tf_op jit(solution)/shard_map/all_to_all | solution.py:548
  49.3 2.7 %attend.1.before = bf16[16,256,128]{2,1,0:T(8,128)(2,1)S(1)} custom-call(bf16[256,128]{1,0:T(8,128)(2,1)S(1)} %get-tuple-element.17.query, bf16[32,16,256]{2,1,0:T(8,128)(2,1)S(1)} %all_to_all.31.recv, bf16[2048,1024]{1,0:T(8,128)(2,1)S(1)} %bitcast.10), custom_call_target="tpu_custom_call" | custom-call | tf_op jit(solution)/shard_map/attend/pallas_call | solution.py:311
  52.0 19.5 %all_to_all.32.refs_0_ = bf16[16,256,128]{2,1,0:T(8,128)(2,1)S(1)} all-to-all(bf16[16,256,128]{2,1,0:T(8,128)(2,1)S(1)} %attend.1.before), channel_id=1, replica_groups=mesh['pipe'=2,'tensor'=4,'dp'=16] {'dp'}, dimensions={0} | all-to-all | bytes 2097152 | tf_op jit(solution)/shard_map/all_to_all | solution.py:557
  71.5 0.1 collective-permute-start.4
  71.6 0.2 project_out.4
  71.8 1.3 collective-permute-done.4.b
  73.1 0.1 add_pair.1
  73.2 0.2 collective-permute-start.5
  73.4 1.2 collective-permute-done.5.there
  74.6 0.1 add_next.1
  74.7 1.3 collective-permute-start.8
  76.0 1.3 collective-permute-start.6
  77.3 11.9 %collective-permute-done.8.refs_2_ = bf16[256,256]{1,0:T(8,128)(2,1)S(1)} collective-permute-done((bf16[256,256]{1,0:T(8,128)(2,1)S(1)}, bf16[256,256]{1,0:T(8,128)(2,1)S(1)}, u32[]{:S(2)}, u32[]{:S(2)}) %collective-permute-start.8) | collective-permute-done | bytes 131104 | tf_op jit(solution)/shard_map/ppermute | solution.py:529
  89.2 0.5 collective-permute-start.7
  89.7 0.8 collective-permute-done.9.refs_3_
  90.5 0.2 collective-permute-done.7.refs_1_
  90.7 1.6 project.3
  92.3 24.1 %all_to_all.33.recv = bf16[16,336,128]{2,1,0:T(8,128)(2,1)S(1)} all-to-all(bf16[16,336,128]{2,1,0:T(8,128)(2,1)S(1)} %bitcast.21), channel_id=1, replica_groups=mesh['pipe'=2,'tensor'=4,'dp'=16] {'dp'}, dimensions={0} | all-to-all | bytes 2752512 | tf_op jit(solution)/shard_map/all_to_all | solution.py:545
  116.4 0.3 combine.3
  116.7 0.1 collective-permute-start.10
  116.8 1.2 collective-permute-done.10.other
  118.0 0.8 choose.3
  118.8 14.4 %all_to_all.34.recv = bf16[32,16,256]{2,1,0:T(8,128)(2,1)S(1)} all-to-all(bf16[32,16,256]{2,1,0:T(8,128)(2,1)S(1)} %get-tuple-element.24), channel_id=1, replica_groups={{0,32,1,33,2,34,3,35,4,36,5,37,6,38,7,39,8,40,9,41,10,42,11,43,12,44,13..., dimensions={0} | all-to-all | bytes 524288 | tf_op jit(solution)/shard_map/all_to_all | solution.py:548
  133.2 0.7 attend_last.1
  134.0 20.2 %all_to_all.35.refs_0_ = bf16[16,272,128]{2,1,0:T(8,128)(2,1)S(1)} all-to-all(bf16[16,272,128]{2,1,0:T(8,128)(2,1)S(1)} %attend_last.1), channel_id=1, replica_groups=mesh['pipe'=2,'tensor'=4,'dp'=16] {'dp'}, dimensions={0} | all-to-all | bytes 2228224 | tf_op jit(solution)/shard_map/all_to_all | solution.py:567
  154.2 0.8 project_out.7
  155.0 0.1 collective-permute-start.11
  155.1 0.8 project_out.6.a
  155.8 0.8 collective-permute-done.11.b
  156.6 0.1 add_last_pair.1
  156.7 0.5 collective-permute-start.12
  157.2 5.2 %collective-permute-done.12.there = bf16[272,256]{1,0:T(8,128)(2,1)S(1)} collective-permute-done((bf16[272,256]{1,0:T(8,128)(2,1)S(1)}, bf16[272,256]{1,0:T(8,128)(2,1)S(1)}, u32[]{:S(2)}, u32[]{:S(2)}) %collective-permute-start.12) | collective-permute-done | bytes 139296 | tf_op jit(solution)/shard_map/ppermute | solution.py:524
  162.5 0.7 add_last.1
  (17 shorter events, 0.1 us)
Async XLA Ops:
  0.6 2.3 %copy-start.3 = (f32[256,128]{1,0:T(8,128)S(1)}, f32[256,128]{1,0:T(8,128)}, u32[]{:S(2)}) copy-start(f32[256,128]{1,0:T(8,128)} %constant.5.clone.refs_4_.sine) | copy-start | bytes 393220
  0.6 2.3 %copy-start.4 = (f32[256,128]{1,0:T(8,128)S(1)}, f32[256,128]{1,0:T(8,128)}, u32[]{:S(2)}) copy-start(f32[256,128]{1,0:T(8,128)} %constant.4.clone.refs_3_.cosine) | copy-start | bytes 393220
  0.7 2.3 %copy-start.2 = (bf16[256,1,1,256]{3,0,2,1:T(8,128)(2,1)S(1)}, bf16[256,1,1,256]{3,0,2,1:T(8,128)(2,1)}, u32[]{:S(2)}) copy-start(bf16[256,1,1,256]{3,0,2,1:T(8,128)(2,1)} %param.8) | copy-start | bytes 393220
  0.7 2.3 %copy-start.6 = (s32[64]{0:T(128)S(1)}, s32[64]{0:T(128)}, u32[]{:S(2)}) copy-start(s32[64]{0:T(128)} %group.3) | copy-start | bytes 772
  0.7 2.3 %copy-start.5 = (bf16[1,1024]{1,0:T(2,128)(2,1)S(1)}, bf16[1,1024]{1,0:T(2,128)(2,1)}, u32[]{:S(2)}) copy-start(bf16[1,1024]{1,0:T(2,128)(2,1)} %refs_4_.4) | copy-start | bytes 6148
  0.7 2.3 %collective-permute-start.1 = (bf16[256,256]{1,0:T(8,128)(2,1)}, bf16[256,256]{1,0:T(8,128)(2,1)S(1)}, u32[]{:S(2)}, u32[]{:S(2)}) collective-permute-start(bf16[256,256]{1,0:T(8,128)(2,1)} %bitcast.23), channel_id=1, source_target_pairs={{0,32},{16,48},{32,0},{48,16},{64,80},{80,64},{96,112},{112,96},{1... | collective-permute-start | bytes 393224 | tf_op jit(solution)/shard_map/ppermute | solution.py:524
  0.8 2.4 %collective-permute-start = (bf16[256,256]{1,0:T(8,128)(2,1)}, bf16[256,256]{1,0:T(8,128)(2,1)S(1)}, u32[]{:S(2)}, u32[]{:S(2)}) collective-permute-start(bf16[256,256]{1,0:T(8,128)(2,1)} %bitcast.24), channel_id=1, source_target_pairs={{0,16},{16,0},{32,48},{48,32},{64,80},{80,64},{96,112},{112,96},{1... | collective-permute-start | bytes 393224 | tf_op jit(solution)/shard_map/ppermute | solution.py:524
  1.3 3.1 %copy-start.1 = (bf16[1,1024,2048]{2,1,0:T(8,128)(2,1)S(1)}, bf16[1,1024,2048]{2,1,0:T(8,128)(2,1)}, u32[]{:S(2)}) copy-start(bf16[1,1024,2048]{2,1,0:T(8,128)(2,1)} %param.10) | copy-start | bytes 12582916
  3.0 1.4 collective-permute-start.2
  4.6 44.6 %copy-start = (bf16[1,2048,1024]{2,1,0:T(8,128)(2,1)S(1)}, bf16[1,2048,1024]{2,1,0:T(8,128)(2,1)}, u32[]{:S(2)}) copy-start(bf16[1,2048,1024]{2,1,0:T(8,128)(2,1)} %param.12) | copy-start | bytes 12582916
  33.7 1.3 collective-permute-start.3
  71.5 1.6 collective-permute-start.4
  73.2 1.4 collective-permute-start.5
  74.7 14.5 %collective-permute-start.8 = (bf16[256,256]{1,0:T(8,128)(2,1)S(1)}, bf16[256,256]{1,0:T(8,128)(2,1)S(1)}, u32[]{:S(2)}, u32[]{:S(2)}) collective-permute-start(bf16[256,256]{1,0:T(8,128)(2,1)S(1)} %add_next.1), channel_id=1, source_target_pairs={{0,96},{16,112},{32,64},{48,80},{1,97},{17,113},{33,65},{49,81},{2... | collective-permute-start | bytes 393224 | tf_op jit(solution)/shard_map/ppermute | solution.py:529
  76.0 13.2 %collective-permute-start.6 = (bf16[256,256]{1,0:T(8,128)(2,1)S(1)}, bf16[256,256]{1,0:T(8,128)(2,1)S(1)}, u32[]{:S(2)}, u32[]{:S(2)}) collective-permute-start(bf16[256,256]{1,0:T(8,128)(2,1)S(1)} %add_next.1), channel_id=1, source_target_pairs={{0,64},{16,80},{32,96},{48,112},{1,65},{17,81},{33,97},{49,113},{2... | collective-permute-start | bytes 393224 | tf_op jit(solution)/shard_map/ppermute | solution.py:529
  89.2 1.3 collective-permute-start.9
  89.2 1.5 collective-permute-start.7
  116.7 1.3 collective-permute-start.10
  155.0 1.6 %collective-permute-start.11 = (bf16[2,272,256]{2,1,0:T(8,128)(2,1)S(1)}, bf16[2,272,256]{2,1,0:T(8,128)(2,1)S(1)}, u32[]{:S(2)}, u32[]{:S(2)}) collective-permute-start(bf16[2,272,256]{2,1,0:T(8,128)(2,1)S(1)} %project_out.7), channel_id=1, source_target_pairs={{0,16},{16,0},{32,48},{48,32},{64,80},{80,64},{96,112},{112,96},{1... | collective-permute-start | bytes 835592 | tf_op jit(solution)/shard_map/ppermute | solution.py:524
  156.7 5.8 %collective-permute-start.12 = (bf16[272,256]{1,0:T(8,128)(2,1)S(1)}, bf16[272,256]{1,0:T(8,128)(2,1)S(1)}, u32[]{:S(2)}, u32[]{:S(2)}) collective-permute-start(bf16[272,256]{1,0:T(8,128)(2,1)S(1)} %get-tuple-element.29), channel_id=1, source_target_pairs={{0,32},{16,48},{32,0},{48,16},{64,96},{80,112},{96,64},{112,80},{1... | collective-permute-start | bytes 417800 | tf_op jit(solution)/shard_map/ppermute | solution.py:524

commit v9 on v8

--- a/solution.py
+++ b/solution.py
@@ -240,38 +240,54 @@
     )(recv, cosine, sine)
 
 
-def choose_kernel(group, own, other, send, *rest):
-    *picked, four = rest
+def plan_kernel(group, choice, picked):
     tensor, data = lax.axis_index("tensor"), lax.axis_index("dp")
     chip, core = tensor // 2, tensor % 2
-    for n in range(2):
-        four[2 * core + n] = own[n]
-        four[2 * (1 - core) + n] = other[n]
+    row = lax.broadcasted_iota(jnp.int32, (16, 64), 0)
+    col = lax.broadcasted_iota(jnp.int32, (16, 64), 1)
     for d in range(N_DP):
         for a in range(2):
             wanted = group[(2 * a + core) * N_DP + d]
-            block = four[wanted % 4]
-            send[2 * d + a] = jnp.where(wanted // 4 == chip, block, jnp.zeros_like(block))
-    for ref in picked:
-        lane = lax.broadcasted_iota(jnp.int32, ref.shape, 1)
-        ref[...] = jnp.where(lane == group[tensor * N_DP + data], 1.0, 0.0).astype(F32)
-
-
-def choose(step, group, own, other):
-    vmem = pl.BlockSpec(memory_space=VMEM)
-    shapes = (
-        jax.ShapeDtypeStruct((2 * N_DP,) + own.shape[1:], BF16),
-        jax.ShapeDtypeStruct((8, HD), F32),
-    )[: 1 + step]
-    return pl.pallas_call(
+            place = jnp.where(wanted % 4 // 2 == core, 0, 2) + wanted % 2
+            place = jnp.where(wanted // 4 == chip, place, 4)
+            first = (2 * d + a) * 16
+            hit = col == place * 16 + row
+            choice[first : first + 16, :] = jnp.where(hit, 1.0, 0.0).astype(BF16)
+    lane = lax.broadcasted_iota(jnp.int32, picked.shape, 1)
+    picked[...] = jnp.where(lane == group[tensor * N_DP + data], 1.0, 0.0).astype(F32)
+
+
+def plan(group):
+    vmem = pl.BlockSpec(memory_space=VMEM)
+    return pl.pallas_call(
+        plan_kernel,
+        out_shape=(
+            jax.ShapeDtypeStruct((2 * N_DP * 16, 64), BF16),
+            jax.ShapeDtypeStruct((8, HD), F32),
+        ),
+        in_specs=[pl.BlockSpec(memory_space=pltpu.SMEM)],
+        out_specs=(vmem,) * 2,
+        compiler_params=pltpu.CompilerParams(vmem_limit_bytes=2 * 2**20),
+        name="plan",
+    )(group)
+
+
+def choose_kernel(choice, own, other, send):
+    four = jnp.concatenate([own[0], own[1], other[0], other[1]], axis=0)
+    send[...] = jnp.dot(choice[...], four, preferred_element_type=F32).astype(BF16)
+
+
+def choose(choice, own, other):
+    vmem = pl.BlockSpec(memory_space=VMEM)
+    send = pl.pallas_call(
         choose_kernel,
-        out_shape=shapes,
-        in_specs=[pl.BlockSpec(memory_space=pltpu.SMEM), vmem, vmem],
-        out_specs=(vmem,) * len(shapes),
-        scratch_shapes=[VMEM((4,) + own.shape[1:], BF16)],
+        out_shape=jax.ShapeDtypeStruct((choice.shape[0], own.shape[2]), BF16),
+        in_specs=[vmem] * 3,
+        out_specs=vmem,
         compiler_params=pltpu.CompilerParams(vmem_limit_bytes=4 * 2**20),
         name="choose",
-    )(group, own, other)
+    )(choice, own, other)
+    return send.reshape((2 * N_DP,) + own.shape[1:])
 
 
 def attended(query, recv, kv):
@@ -535,6 +551,7 @@
     wq, wout = w_query[0], w_out[0]
     wkv = w_keyval[0].reshape(wq.shape[0], -1)
     cosine, sine = map(jnp.asarray, rotary_tables(rows))
+    choice, picked = plan(head_group)
 
     runs = [
         [d * N_TENSOR + 2 * a + core for d in range(N_DP) for a in range(2)] for core in range(2)
@@ -544,12 +561,12 @@
         send = project(step, pieces, norm_gain, wkv, wq, *weights)
         recv = lax.all_to_all(send, "dp", 0, 0)
         query, kv, *gram = combine(step, recv, cosine, sine, width)
-        send, *picked = choose(step, head_group, kv, swap(kv, 1))
+        send = choose(choice, kv, swap(kv, 1))
         recv = lax.all_to_all(send, ("dp", "tensor"), 0, 0, axis_index_groups=runs)
-        return query, recv, *gram, *picked
+        return query, recv, *gram
 
     mine = hidden_in.reshape(rows, cols)
-    tile = ready(mine, norm_gain, wkv, cosine, sine, head_group)
+    tile = ready(mine, norm_gain, wkv, cosine, sine, choice)
     far = hand_on(swap(mine, 2, 1), tile)
     pieces = (mine, swap(mine, 1), far, swap(far, 1))
     query, kv = to_heads(0, pieces)
@@ -562,7 +579,7 @@
     far = to_next_section(fresh, 2)
     near = to_next_section(fresh, 0)
 
-    query, kv, gram1, picked = to_heads(1, (near, swap(near, 1), far, swap(far, 1)), wout)
+    query, kv, gram1 = to_heads(1, (near, swap(near, 1), far, swap(far, 1)), wout)
     att1 = attend_last(query, kv, att0, gram0, gram1, picked, width)
     recv = lax.all_to_all(att1, "dp", 0, 0)
     (other1,) = project_out(recv, wout, rows, (1, 3), other0)

time: 164 us -> 162 us (0.988)
  waiting for transfers between devices: 25.1 us -> 23.4 us
where the time goes in v9:
time: 162 us
  blocking collectives  121 us (75%)
  waiting for transfers between devices  23.4 us (14%)
  Pallas kernels  9.62 us (6%)
  starting transfers between devices  4.95 us (3%)
  local copies, waits for them, and re-layouts  2.29 us (1%)
    all_to_all x2, blocking collectives, to_heads(): recv = lax.all_to_all(send, 'dp', 0, 0)  53.2 us
    all_to_all x2, blocking collectives, to_heads(): recv = lax.all_to_all(send, ('dp', 'tensor'), 0, 0, axis_index_groups=runs)  27.9 us
    all_to_all x1, blocking collectives, local(): recv = lax.all_to_all(att1, 'dp', 0, 0)  20.2 us
    all_to_all x1, blocking collectives, local(): recv = lax.all_to_all(att0, 'dp', 0, 0)  19.5 us
    ppermute x11, waiting for transfers between devices, swap(): return lax.ppermute(block, ('pipe', 'tensor'), route)  13.2 us
    ppermute x2, waiting for transfers between devices, to_next_section(): return lax.ppermute(block, ('pipe', 'tensor'), route)  10.3 us
  transfers between devices with their start and end apart: 13, of which 10 were waited for; matrix products, arithmetic and copies ran while one was open for 1% of the time, Pallas kernels for 1%

profile of v9, /device:TPU:4, one launch (start us, length us, event | category | flops | bytes accessed | tf_op | source)
XLA Modules:
  0.0 162.0 jit_solution(8067655508388487491)
XLA Ops:
  0.6 0.0 copy-start.3
  0.6 0.0 copy-start.4
  0.7 0.1 collective-permute-start.1
  0.8 0.5 collective-permute-start
  1.3 0.7 copy-done.6
  1.9 1.0 plan.1
  2.9 1.6 copy.10
  4.6 0.2 collective-permute-start.2
  4.8 1.3 collective-permute-done.2.refs_3_
  6.0 0.2 project.2
  6.3 0.0 copy-start
  6.3 29.1 %all_to_all.30.recv = bf16[16,336,128]{2,1,0:T(8,128)(2,1)S(1)} all-to-all(bf16[16,336,128]{2,1,0:T(8,128)(2,1)S(1)} %bitcast.24), channel_id=1, replica_groups=mesh['pipe'=2,'tensor'=4,'dp'=16] {'dp'}, dimensions={0} | all-to-all | bytes 2752512 | tf_op jit(solution)/shard_map/all_to_all | solution.py:562
  35.4 0.1 collective-permute-start.3
  35.5 1.2 collective-permute-done.3.other
  36.6 0.2 choose.2
  36.8 13.5 %all_to_all.31.recv = bf16[32,16,256]{2,1,0:T(8,128)(2,1)S(1)} all-to-all(bf16[32,16,256]{2,1,0:T(8,128)(2,1)S(1)} %bitcast.32), channel_id=1, replica_groups={{0,32,1,33,2,34,3,35,4,36,5,37,6,38,7,39,8,40,9,41,10,42,11,43,12,44,13..., dimensions={0} | all-to-all | bytes 524288 | tf_op jit(solution)/shard_map/all_to_all | solution.py:565
  50.3 2.7 %attend.1.before = bf16[16,256,128]{2,1,0:T(8,128)(2,1)S(1)} custom-call(bf16[256,128]{1,0:T(8,128)(2,1)S(1)} %get-tuple-element.18.query, bf16[32,16,256]{2,1,0:T(8,128)(2,1)S(1)} %all_to_all.31.recv, bf16[2048,1024]{1,0:T(8,128)(2,1)S(1)} %bitcast.12), custom_call_target="tpu_custom_call" | custom-call | tf_op jit(solution)/shard_map/attend/pallas_call | solution.py:327
  53.0 19.5 %all_to_all.32.refs_0_ = bf16[16,256,128]{2,1,0:T(8,128)(2,1)S(1)} all-to-all(bf16[16,256,128]{2,1,0:T(8,128)(2,1)S(1)} %attend.1.before), channel_id=1, replica_groups=mesh['pipe'=2,'tensor'=4,'dp'=16] {'dp'}, dimensions={0} | all-to-all | bytes 2097152 | tf_op jit(solution)/shard_map/all_to_all | solution.py:574
  72.6 0.1 collective-permute-start.4
  72.7 0.2 project_out.4
  72.9 1.3 collective-permute-done.4.b
  74.2 0.1 add_pair.1
  74.3 0.2 collective-permute-start.5
  74.5 1.2 collective-permute-done.5.there
  75.7 0.1 add_next.1
  75.7 1.3 collective-permute-start.8
  77.0 1.3 collective-permute-start.6
  78.3 10.3 %collective-permute-done.8.refs_2_ = bf16[256,256]{1,0:T(8,128)(2,1)S(1)} collective-permute-done((bf16[256,256]{1,0:T(8,128)(2,1)S(1)}, bf16[256,256]{1,0:T(8,128)(2,1)S(1)}, u32[]{:S(2)}, u32[]{:S(2)}) %collective-permute-start.8) | collective-permute-done | bytes 131104 | tf_op jit(solution)/shard_map/ppermute | solution.py:545
  88.6 0.5 collective-permute-start.7
  89.1 0.8 collective-permute-done.9.refs_3_
  90.0 0.2 collective-permute-done.7.refs_1_
  90.1 1.6 project.3
  91.7 24.1 %all_to_all.33.recv = bf16[16,336,128]{2,1,0:T(8,128)(2,1)S(1)} all-to-all(bf16[16,336,128]{2,1,0:T(8,128)(2,1)S(1)} %bitcast.23), channel_id=1, replica_groups=mesh['pipe'=2,'tensor'=4,'dp'=16] {'dp'}, dimensions={0} | all-to-all | bytes 2752512 | tf_op jit(solution)/shard_map/all_to_all | solution.py:562
  115.8 0.3 combine.3
  116.2 0.1 collective-permute-start.10
  116.2 1.2 collective-permute-done.10.other
  117.4 0.2 choose.3
  117.6 14.4 %all_to_all.34.recv = bf16[32,16,256]{2,1,0:T(8,128)(2,1)S(1)} all-to-all(bf16[32,16,256]{2,1,0:T(8,128)(2,1)S(1)} %bitcast.31), channel_id=1, replica_groups={{0,32,1,33,2,34,3,35,4,36,5,37,6,38,7,39,8,40,9,41,10,42,11,43,12,44,13..., dimensions={0} | all-to-all | bytes 524288 | tf_op jit(solution)/shard_map/all_to_all | solution.py:565
  132.0 0.7 attend_last.1
  132.8 20.2 %all_to_all.35.refs_0_ = bf16[16,272,128]{2,1,0:T(8,128)(2,1)S(1)} all-to-all(bf16[16,272,128]{2,1,0:T(8,128)(2,1)S(1)} %attend_last.1), channel_id=1, replica_groups=mesh['pipe'=2,'tensor'=4,'dp'=16] {'dp'}, dimensions={0} | all-to-all | bytes 2228224 | tf_op jit(solution)/shard_map/all_to_all | solution.py:584
  153.0 0.8 project_out.7
  153.8 0.1 collective-permute-start.11
  153.9 0.8 project_out.6.a
  154.7 0.8 collective-permute-done.11.b
  155.4 0.1 add_last_pair.1
  155.5 0.5 collective-permute-start.12
  156.1 5.2 %collective-permute-done.12.there = bf16[272,256]{1,0:T(8,128)(2,1)S(1)} collective-permute-done((bf16[272,256]{1,0:T(8,128)(2,1)S(1)}, bf16[272,256]{1,0:T(8,128)(2,1)S(1)}, u32[]{:S(2)}, u32[]{:S(2)}) %collective-permute-start.12) | collective-permute-done | bytes 139296 | tf_op jit(solution)/shard_map/ppermute | solution.py:540
  161.3 0.7 add_last.1
  (18 shorter events, 0.1 us)
Async XLA Ops:
  0.6 3.9 %copy-start.3 = (f32[256,128]{1,0:T(8,128)S(1)}, f32[256,128]{1,0:T(8,128)}, u32[]{:S(2)}) copy-start(f32[256,128]{1,0:T(8,128)} %constant.5.clone.refs_4_.sine) | copy-start | bytes 393220
  0.6 3.9 %copy-start.4 = (f32[256,128]{1,0:T(8,128)S(1)}, f32[256,128]{1,0:T(8,128)}, u32[]{:S(2)}) copy-start(f32[256,128]{1,0:T(8,128)} %constant.4.clone.refs_3_.cosine) | copy-start | bytes 393220
  0.7 3.9 %copy-start.2 = (bf16[256,1,1,256]{3,0,2,1:T(8,128)(2,1)S(1)}, bf16[256,1,1,256]{3,0,2,1:T(8,128)(2,1)}, u32[]{:S(2)}) copy-start(bf16[256,1,1,256]{3,0,2,1:T(8,128)(2,1)} %param.8) | copy-start | bytes 393220
  0.7 3.9 %copy-start.5 = (bf16[1,1024]{1,0:T(2,128)(2,1)S(1)}, bf16[1,1024]{1,0:T(2,128)(2,1)}, u32[]{:S(2)}) copy-start(bf16[1,1024]{1,0:T(2,128)(2,1)} %refs_4_.4) | copy-start | bytes 6148
  0.7 3.9 %collective-permute-start.1 = (bf16[256,256]{1,0:T(8,128)(2,1)}, bf16[256,256]{1,0:T(8,128)(2,1)S(1)}, u32[]{:S(2)}, u32[]{:S(2)}) collective-permute-start(bf16[256,256]{1,0:T(8,128)(2,1)} %bitcast.25), channel_id=1, source_target_pairs={{0,32},{16,48},{32,0},{48,16},{64,80},{80,64},{96,112},{112,96},{1... | collective-permute-start | bytes 393224 | tf_op jit(solution)/shard_map/ppermute | solution.py:540
  0.8 4.0 %collective-permute-start = (bf16[256,256]{1,0:T(8,128)(2,1)}, bf16[256,256]{1,0:T(8,128)(2,1)S(1)}, u32[]{:S(2)}, u32[]{:S(2)}) collective-permute-start(bf16[256,256]{1,0:T(8,128)(2,1)} %bitcast.26), channel_id=1, source_target_pairs={{0,16},{16,0},{32,48},{48,32},{64,80},{80,64},{96,112},{112,96},{1... | collective-permute-start | bytes 393224 | tf_op jit(solution)/shard_map/ppermute | solution.py:540
  1.3 0.7 copy-start.6
  2.9 3.1 %copy-start.1 = (bf16[1,1024,2048]{2,1,0:T(8,128)(2,1)S(1)}, bf16[1,1024,2048]{2,1,0:T(8,128)(2,1)}, u32[]{:S(2)}) copy-start(bf16[1,1024,2048]{2,1,0:T(8,128)(2,1)} %param.10) | copy-start | bytes 12582916
  4.6 1.4 collective-permute-start.2
  6.3 44.1 %copy-start = (bf16[1,2048,1024]{2,1,0:T(8,128)(2,1)S(1)}, bf16[1,2048,1024]{2,1,0:T(8,128)(2,1)}, u32[]{:S(2)}) copy-start(bf16[1,2048,1024]{2,1,0:T(8,128)(2,1)} %param.12) | copy-start | bytes 12582916
  35.4 1.3 collective-permute-start.3
  72.6 1.6 collective-permute-start.4
  74.3 1.4 collective-permute-start.5
  75.7 12.9 %collective-permute-start.8 = (bf16[256,256]{1,0:T(8,128)(2,1)S(1)}, bf16[256,256]{1,0:T(8,128)(2,1)S(1)}, u32[]{:S(2)}, u32[]{:S(2)}) collective-permute-start(bf16[256,256]{1,0:T(8,128)(2,1)S(1)} %add_next.1), channel_id=1, source_target_pairs={{0,96},{16,112},{32,64},{48,80},{1,97},{17,113},{33,65},{49,81},{2... | collective-permute-start | bytes 393224 | tf_op jit(solution)/shard_map/ppermute | solution.py:545
  77.0 11.6 %collective-permute-start.6 = (bf16[256,256]{1,0:T(8,128)(2,1)S(1)}, bf16[256,256]{1,0:T(8,128)(2,1)S(1)}, u32[]{:S(2)}, u32[]{:S(2)}) collective-permute-start(bf16[256,256]{1,0:T(8,128)(2,1)S(1)} %add_next.1), channel_id=1, source_target_pairs={{0,64},{16,80},{32,96},{48,112},{1,65},{17,81},{33,97},{49,113},{2... | collective-permute-start | bytes 393224 | tf_op jit(solution)/shard_map/ppermute | solution.py:545
  88.6 1.3 collective-permute-start.9
  88.6 1.5 collective-permute-start.7
  116.2 1.3 collective-permute-start.10
  153.8 1.6 %collective-permute-start.11 = (bf16[2,272,256]{2,1,0:T(8,128)(2,1)S(1)}, bf16[2,272,256]{2,1,0:T(8,128)(2,1)S(1)}, u32[]{:S(2)}, u32[]{:S(2)}) collective-permute-start(bf16[2,272,256]{2,1,0:T(8,128)(2,1)S(1)} %project_out.7), channel_id=1, source_target_pairs={{0,16},{16,0},{32,48},{48,32},{64,80},{80,64},{96,112},{112,96},{1... | collective-permute-start | bytes 835592 | tf_op jit(solution)/shard_map/ppermute | solution.py:540
  155.5 5.8 %collective-permute-start.12 = (bf16[272,256]{1,0:T(8,128)(2,1)S(1)}, bf16[272,256]{1,0:T(8,128)(2,1)S(1)}, u32[]{:S(2)}, u32[]{:S(2)}) collective-permute-start(bf16[272,256]{1,0:T(8,128)(2,1)S(1)} %get-tuple-element.29), channel_id=1, source_target_pairs={{0,32},{16,48},{32,0},{48,16},{64,96},{80,112},{96,64},{112,80},{1... | collective-permute-start | bytes 417800 | tf_op jit(solution)/shard_map/ppermute | solution.py:540

commit v10 on v9

--- a/solution.py
+++ b/solution.py
@@ -576,10 +576,11 @@
     own0, gram0 = project_out(recv, wout, rows, (0, 2))
     here, away = add_pair(own0, swap(other0, 1))
     fresh = add_next(mine, here, swap(away, 2, 1))
-    far = to_next_section(fresh, 2)
     near = to_next_section(fresh, 0)
-
-    query, kv, gram1 = to_heads(1, (near, swap(near, 1), far, swap(far, 1)), wout)
+    beside = swap(near, 1)
+    far = hand_on(to_next_section(fresh, 2), beside)
+
+    query, kv, gram1 = to_heads(1, (near, beside, far, swap(far, 1)), wout)
     att1 = attend_last(query, kv, att0, gram0, gram1, picked, width)
     recv = lax.all_to_all(att1, "dp", 0, 0)
     (other1,) = project_out(recv, wout, rows, (1, 3), other0)

time: 162 us -> 162 us (level)
  no operation moved by 1% of the time
where the time goes in v10:
time: 162 us
  blocking collectives  120 us (74%)
  waiting for transfers between devices  24.7 us (15%)
  Pallas kernels  9.64 us (6%)
  starting transfers between devices  4.54 us (3%)
  local copies, waits for them, and re-layouts  2.29 us (1%)
    all_to_all x2, blocking collectives, to_heads(): recv = lax.all_to_all(send, 'dp', 0, 0)  53 us
    all_to_all x2, blocking collectives, to_heads(): recv = lax.all_to_all(send, ('dp', 'tensor'), 0, 0, axis_index_groups=runs)  26.8 us
    all_to_all x1, blocking collectives, local(): recv = lax.all_to_all(att1, 'dp', 0, 0)  20.2 us
    all_to_all x1, blocking collectives, local(): recv = lax.all_to_all(att0, 'dp', 0, 0)  19.5 us
    ppermute x11, waiting for transfers between devices, swap(): return lax.ppermute(block, ('pipe', 'tensor'), route)  13.5 us
    ppermute x2, waiting for transfers between devices, to_next_section(): return lax.ppermute(block, ('pipe', 'tensor'), route)  11.2 us
  transfers between devices with their start and end apart: 13, of which 10 were waited for; matrix products, arithmetic and copies ran while one was open for 1% of the time, Pallas kernels for 1%

profile of v10, /device:TPU:4, one launch (start us, length us, event | category | flops | bytes accessed | tf_op | source)
XLA Modules:
  0.0 161.7 jit_solution(8351834393888753240)
XLA Ops:
  0.6 0.0 copy-start.3
  0.6 0.0 copy-start.4
  0.7 0.1 collective-permute-start.1
  0.8 0.5 collective-permute-start
  1.3 0.7 copy-done.6
  1.9 1.0 plan.1
  2.9 1.6 copy.10
  4.6 0.2 collective-permute-start.2
  4.8 1.3 collective-permute-done.2.refs_3_
  6.0 0.2 project.2
  6.3 0.0 copy-start
  6.3 29.1 %all_to_all.30.recv = bf16[16,336,128]{2,1,0:T(8,128)(2,1)S(1)} all-to-all(bf16[16,336,128]{2,1,0:T(8,128)(2,1)S(1)} %bitcast.24), channel_id=1, replica_groups=mesh['pipe'=2,'tensor'=4,'dp'=16] {'dp'}, dimensions={0} | all-to-all | bytes 2752512 | tf_op jit(solution)/shard_map/all_to_all | solution.py:562
  35.4 0.1 collective-permute-start.3
  35.5 1.2 collective-permute-done.3.other
  36.6 0.2 choose.2
  36.8 13.5 %all_to_all.31.recv = bf16[32,16,256]{2,1,0:T(8,128)(2,1)S(1)} all-to-all(bf16[32,16,256]{2,1,0:T(8,128)(2,1)S(1)} %bitcast.32), channel_id=1, replica_groups={{0,32,1,33,2,34,3,35,4,36,5,37,6,38,7,39,8,40,9,41,10,42,11,43,12,44,13..., dimensions={0} | all-to-all | bytes 524288 | tf_op jit(solution)/shard_map/all_to_all | solution.py:565
  50.3 2.7 %attend.1.before = bf16[16,256,128]{2,1,0:T(8,128)(2,1)S(1)} custom-call(bf16[256,128]{1,0:T(8,128)(2,1)S(1)} %get-tuple-element.18.query, bf16[32,16,256]{2,1,0:T(8,128)(2,1)S(1)} %all_to_all.31.recv, bf16[2048,1024]{1,0:T(8,128)(2,1)S(1)} %bitcast.12), custom_call_target="tpu_custom_call" | custom-call | tf_op jit(solution)/shard_map/attend/pallas_call | solution.py:327
  53.0 19.5 %all_to_all.32.refs_0_ = bf16[16,256,128]{2,1,0:T(8,128)(2,1)S(1)} all-to-all(bf16[16,256,128]{2,1,0:T(8,128)(2,1)S(1)} %attend.1.before), channel_id=1, replica_groups=mesh['pipe'=2,'tensor'=4,'dp'=16] {'dp'}, dimensions={0} | all-to-all | bytes 2097152 | tf_op jit(solution)/shard_map/all_to_all | solution.py:574
  72.6 0.1 collective-permute-start.4
  72.7 0.2 project_out.4
  72.9 1.3 collective-permute-done.4.b
  74.2 0.1 add_pair.1
  74.3 0.2 collective-permute-start.5
  74.5 1.2 collective-permute-done.5.there
  75.7 0.1 add_next.1
  75.7 1.3 collective-permute-start.6
  77.0 1.3 collective-permute-start.8
  78.3 8.5 %collective-permute-done.6.refs_0_.state = bf16[256,256]{1,0:T(8,128)(2,1)S(1)} collective-permute-done((bf16[256,256]{1,0:T(8,128)(2,1)S(1)}, bf16[256,256]{1,0:T(8,128)(2,1)S(1)}, u32[]{:S(2)}, u32[]{:S(2)}) %collective-permute-start.6) | collective-permute-done | bytes 131104 | tf_op jit(solution)/shard_map/ppermute | solution.py:545
  86.9 2.7 %collective-permute-done.8.block = bf16[256,256]{1,0:T(8,128)(2,1)S(1)} collective-permute-done((bf16[256,256]{1,0:T(8,128)(2,1)S(1)}, bf16[256,256]{1,0:T(8,128)(2,1)S(1)}, u32[]{:S(2)}, u32[]{:S(2)}) %collective-permute-start.8) | collective-permute-done | bytes 131104 | tf_op jit(solution)/shard_map/ppermute | solution.py:545
  89.6 0.1 collective-permute-start.9
  89.7 1.3 collective-permute-done.9.refs_3_
  91.0 1.6 project.3
  92.6 23.9 %all_to_all.33.recv = bf16[16,336,128]{2,1,0:T(8,128)(2,1)S(1)} all-to-all(bf16[16,336,128]{2,1,0:T(8,128)(2,1)S(1)} %bitcast.23), channel_id=1, replica_groups=mesh['pipe'=2,'tensor'=4,'dp'=16] {'dp'}, dimensions={0} | all-to-all | bytes 2752512 | tf_op jit(solution)/shard_map/all_to_all | solution.py:562
  116.5 0.3 combine.3
  116.8 0.1 collective-permute-start.10
  116.9 1.2 collective-permute-done.10.other
  118.1 0.2 choose.3
  118.3 13.4 %all_to_all.34.recv = bf16[32,16,256]{2,1,0:T(8,128)(2,1)S(1)} all-to-all(bf16[32,16,256]{2,1,0:T(8,128)(2,1)S(1)} %bitcast.31), channel_id=1, replica_groups={{0,32,1,33,2,34,3,35,4,36,5,37,6,38,7,39,8,40,9,41,10,42,11,43,12,44,13..., dimensions={0} | all-to-all | bytes 524288 | tf_op jit(solution)/shard_map/all_to_all | solution.py:565
  131.7 0.7 attend_last.1
  132.4 20.2 %all_to_all.35.refs_0_ = bf16[16,272,128]{2,1,0:T(8,128)(2,1)S(1)} all-to-all(bf16[16,272,128]{2,1,0:T(8,128)(2,1)S(1)} %attend_last.1), channel_id=1, replica_groups=mesh['pipe'=2,'tensor'=4,'dp'=16] {'dp'}, dimensions={0} | all-to-all | bytes 2228224 | tf_op jit(solution)/shard_map/all_to_all | solution.py:585
  152.6 0.8 project_out.7
  153.4 0.1 collective-permute-start.11
  153.5 0.8 project_out.6.a
  154.3 0.8 collective-permute-done.11.b
  155.0 0.1 add_last_pair.1
  155.1 0.5 collective-permute-start.12
  155.7 5.2 %collective-permute-done.12.there = bf16[272,256]{1,0:T(8,128)(2,1)S(1)} collective-permute-done((bf16[272,256]{1,0:T(8,128)(2,1)S(1)}, bf16[272,256]{1,0:T(8,128)(2,1)S(1)}, u32[]{:S(2)}, u32[]{:S(2)}) %collective-permute-start.12) | collective-permute-done | bytes 139296 | tf_op jit(solution)/shard_map/ppermute | solution.py:540
  160.9 0.7 add_last.1
  (19 shorter events, 0.1 us)
Async XLA Ops:
  0.6 3.9 %copy-start.3 = (f32[256,128]{1,0:T(8,128)S(1)}, f32[256,128]{1,0:T(8,128)}, u32[]{:S(2)}) copy-start(f32[256,128]{1,0:T(8,128)} %constant.5.clone.refs_4_.sine) | copy-start | bytes 393220
  0.6 3.9 %copy-start.4 = (f32[256,128]{1,0:T(8,128)S(1)}, f32[256,128]{1,0:T(8,128)}, u32[]{:S(2)}) copy-start(f32[256,128]{1,0:T(8,128)} %constant.4.clone.refs_3_.cosine) | copy-start | bytes 393220
  0.7 3.9 %copy-start.2 = (bf16[256,1,1,256]{3,0,2,1:T(8,128)(2,1)S(1)}, bf16[256,1,1,256]{3,0,2,1:T(8,128)(2,1)}, u32[]{:S(2)}) copy-start(bf16[256,1,1,256]{3,0,2,1:T(8,128)(2,1)} %param.8) | copy-start | bytes 393220
  0.7 3.9 %copy-start.5 = (bf16[1,1024]{1,0:T(2,128)(2,1)S(1)}, bf16[1,1024]{1,0:T(2,128)(2,1)}, u32[]{:S(2)}) copy-start(bf16[1,1024]{1,0:T(2,128)(2,1)} %refs_4_.4) | copy-start | bytes 6148
  0.7 3.9 %collective-permute-start.1 = (bf16[256,256]{1,0:T(8,128)(2,1)}, bf16[256,256]{1,0:T(8,128)(2,1)S(1)}, u32[]{:S(2)}, u32[]{:S(2)}) collective-permute-start(bf16[256,256]{1,0:T(8,128)(2,1)} %bitcast.25), channel_id=1, source_target_pairs={{0,32},{16,48},{32,0},{48,16},{64,80},{80,64},{96,112},{112,96},{1... | collective-permute-start | bytes 393224 | tf_op jit(solution)/shard_map/ppermute | solution.py:540
  0.8 4.0 %collective-permute-start = (bf16[256,256]{1,0:T(8,128)(2,1)}, bf16[256,256]{1,0:T(8,128)(2,1)S(1)}, u32[]{:S(2)}, u32[]{:S(2)}) collective-permute-start(bf16[256,256]{1,0:T(8,128)(2,1)} %bitcast.26), channel_id=1, source_target_pairs={{0,16},{16,0},{32,48},{48,32},{64,80},{80,64},{96,112},{112,96},{1... | collective-permute-start | bytes 393224 | tf_op jit(solution)/shard_map/ppermute | solution.py:540
  1.3 0.7 copy-start.6
  2.9 3.1 %copy-start.1 = (bf16[1,1024,2048]{2,1,0:T(8,128)(2,1)S(1)}, bf16[1,1024,2048]{2,1,0:T(8,128)(2,1)}, u32[]{:S(2)}) copy-start(bf16[1,1024,2048]{2,1,0:T(8,128)(2,1)} %param.10) | copy-start | bytes 12582916
  4.6 1.4 collective-permute-start.2
  6.3 44.1 %copy-start = (bf16[1,2048,1024]{2,1,0:T(8,128)(2,1)S(1)}, bf16[1,2048,1024]{2,1,0:T(8,128)(2,1)}, u32[]{:S(2)}) copy-start(bf16[1,2048,1024]{2,1,0:T(8,128)(2,1)} %param.12) | copy-start | bytes 12582916
  35.4 1.3 collective-permute-start.3
  72.6 1.6 collective-permute-start.4
  74.3 1.4 collective-permute-start.5
  75.7 11.1 %collective-permute-start.6 = (bf16[256,256]{1,0:T(8,128)(2,1)S(1)}, bf16[256,256]{1,0:T(8,128)(2,1)S(1)}, u32[]{:S(2)}, u32[]{:S(2)}) collective-permute-start(bf16[256,256]{1,0:T(8,128)(2,1)S(1)} %add_next.1), channel_id=1, source_target_pairs={{0,64},{16,80},{32,96},{48,112},{1,65},{17,81},{33,97},{49,113},{2... | collective-permute-start | bytes 393224 | tf_op jit(solution)/shard_map/ppermute | solution.py:545
  77.0 12.5 %collective-permute-start.8 = (bf16[256,256]{1,0:T(8,128)(2,1)S(1)}, bf16[256,256]{1,0:T(8,128)(2,1)S(1)}, u32[]{:S(2)}, u32[]{:S(2)}) collective-permute-start(bf16[256,256]{1,0:T(8,128)(2,1)S(1)} %add_next.1), channel_id=1, source_target_pairs={{0,96},{16,112},{32,64},{48,80},{1,97},{17,113},{33,65},{49,81},{2... | collective-permute-start | bytes 393224 | tf_op jit(solution)/shard_map/ppermute | solution.py:545
  86.9 2.7 %collective-permute-start.7 = (bf16[256,256]{1,0:T(8,128)(2,1)S(1)}, bf16[256,256]{1,0:T(8,128)(2,1)S(1)}, u32[]{:S(2)}, u32[]{:S(2)}) collective-permute-start(bf16[256,256]{1,0:T(8,128)(2,1)S(1)} %collective-permute-done.6.refs_0_.state), channel_id=1, source_target_pairs={{0,16},{16,0},{32,48},{48,32},{64,80},{80,64},{96,112},{112,96},{1... | collective-permute-start | bytes 393224 | tf_op jit(solution)/shard_map/ppermute | solution.py:540
  89.6 1.4 collective-permute-start.9
  116.8 1.3 collective-permute-start.10
  153.4 1.6 %collective-permute-start.11 = (bf16[2,272,256]{2,1,0:T(8,128)(2,1)S(1)}, bf16[2,272,256]{2,1,0:T(8,128)(2,1)S(1)}, u32[]{:S(2)}, u32[]{:S(2)}) collective-permute-start(bf16[2,272,256]{2,1,0:T(8,128)(2,1)S(1)} %project_out.7), channel_id=1, source_target_pairs={{0,16},{16,0},{32,48},{48,32},{64,80},{80,64},{96,112},{112,96},{1... | collective-permute-start | bytes 835592 | tf_op jit(solution)/shard_map/ppermute | solution.py:540
  155.1 5.8 %collective-permute-start.12 = (bf16[272,256]{1,0:T(8,128)(2,1)S(1)}, bf16[272,256]{1,0:T(8,128)(2,1)S(1)}, u32[]{:S(2)}, u32[]{:S(2)}) collective-permute-start(bf16[272,256]{1,0:T(8,128)(2,1)S(1)} %get-tuple-element.29), channel_id=1, source_target_pairs={{0,32},{16,48},{32,0},{48,16},{64,96},{80,112},{96,64},{112,80},{1... | collective-permute-start | bytes 417800 | tf_op jit(solution)/shard_map/ppermute | solution.py:540
